TPU v7x, 32 devices: a whole 2x2x4 slice. The times are simulated.
32 devices in a mesh: shot: 8 (over y, x, core), slab: 4 (over z).
Axes of the slice: x: 2, y: 2, z: 4, core: 2. Of those that a mesh axis runs over, the one named last changes fastest.
Arguments:
- velocity: float32 [32, 64, 128], P('slab'), may hold values from 0.2 to 0.4
- wave_state: float32 [2, 8, 2, 32, 64, 128], P(None, 'shot', None, 'slab'), may hold values from -6 to 6
- source_cells: int32 [8, 4], P('shot'), may hold values from 0 to 262143
- source_codes: int32 [8, 4], P('shot'), may hold values from 0 to 7
- wavelets: float32 [8, 2], replicated, may hold values from -48 to 48
- receiver_cells: int32 [8, 256], P('shot'), may hold values from 0 to 262143
- residuals: float32 [8, 2, 256], P('shot'), may hold values from -48 to 48
- momentum: float32 [32, 64, 128], P('slab', 'shot'), may hold values from -6 to 6
- diffusivity: float32 [3, 32, 64, 128], P(None, 'slab', 'shot'), may hold values from 0.02 to 0.15
Outputs:
- final_fields: float32 [8, 2, 32, 64, 128], P('shot', None, 'slab')
- new_momentum: float32 [32, 64, 128], P('slab', 'shot')
- new_velocity: float32 [32, 64, 128], P('slab', 'shot')
All inputs are finite; a program needn't handle non-finite values.
Results may differ from a plain program's by a relative error of at most 0.000076.
Values sent between devices are 32-bit elements; how exact they have to be, the bound alone decides.
No kernel may reach another device: no remote copies, remote signals or barrier semaphores. Data moves between devices by JAX's collectives and lax.ppermute only.
A program may use at most 64 MiB of HBM per device.

v0:
```python
import math

import jax
import jax.numpy as jnp
from jax import lax
from jax.sharding import PartitionSpec as P

STENCIL_TAPS = (-205.0 / 72.0, 8.0 / 5.0, -1.0 / 5.0, 8.0 / 315.0, -1.0 / 560.0)


def with_halo(cells, sides, width):
    for axis, dim in sides:
        count = lax.axis_size(axis)
        ends = count - 1
        head = lax.slice_in_dim(cells, 0, width, axis=dim)
        tail = lax.slice_in_dim(cells, cells.shape[dim] - width, cells.shape[dim], axis=dim)
        cells = jnp.concatenate(
            [
                lax.ppermute(tail, axis, [(i, (i + 1) % count) for i in range(ends)]),
                cells,
                lax.ppermute(head, axis, [((i + 1) % count, i) for i in range(ends)]),
            ],
            axis=dim,
        )
    return cells


def laplacian(padded):
    leading = padded.ndim - 2
    lateral = jnp.pad(padded, [(0, 0)] * leading + [(4, 4), (4, 4)])
    row_count = padded.shape[-3] - 8
    size_x = padded.shape[-2]
    size_y = padded.shape[-1]

    def shifted(off_z, off_x, off_y):
        return lateral[
            ...,
            4 + off_z : 4 + off_z + row_count,
            4 + off_x : 4 + off_x + size_x,
            4 + off_y : 4 + off_y + size_y,
        ]

    summed = 3.0 * STENCIL_TAPS[0] * shifted(0, 0, 0)
    for radius in range(1, 5):
        cycle_sum = (
            shifted(radius, 0, 0)
            + shifted(-radius, 0, 0)
            + shifted(0, radius, 0)
            + shifted(0, -radius, 0)
            + shifted(0, 0, radius)
            + shifted(0, 0, -radius)
        )
        summed = summed + STENCIL_TAPS[radius] * cycle_sum
    return summed


def smooth_step(extended, kappas):
    lateral = jnp.pad(extended, ((0, 0), (0, 0), (1, 1)))
    centre = extended[1:-1, 1:-1, :]
    along_z = extended[2:, 1:-1, :] - 2.0 * centre + extended[:-2, 1:-1, :]
    along_x = extended[1:-1, 2:, :] - 2.0 * centre + extended[1:-1, :-2, :]
    along_y = lateral[1:-1, 1:-1, 2:] - 2.0 * centre + lateral[1:-1, 1:-1, :-2]
    return centre + kappas[0] * along_z + kappas[1] * along_x + kappas[2] * along_y


def point_grid(cell_ids, amounts, first_row, row_count, size_x, size_y):
    groups_here = cell_ids.shape[0]
    plane_size = size_x * size_y
    volume = row_count * plane_size
    local_ids = cell_ids - first_row * plane_size
    inside = (local_ids >= 0) & (local_ids < volume)
    offsets = jnp.arange(groups_here, dtype=jnp.int32)[:, None] * volume
    flat_index = jnp.where(inside, local_ids + offsets, groups_here * volume)
    grid = (
        jnp.zeros((groups_here * volume,), jnp.float32)
        .at[flat_index.reshape(-1)]
        .add(amounts.reshape(-1), mode="drop")
    )
    return grid.reshape(groups_here, row_count, size_x, size_y)


def on_device(
    velocity,
    wave_state,
    source_cells,
    source_codes,
    wavelets,
    receiver_cells,
    residuals,
    momentum,
    diffusivity,
):
    depth_rows = velocity.shape[0]
    size_x = velocity.shape[1]
    size_y = velocity.shape[2]
    groups_here = wave_state.shape[1]
    step_count = wavelets.shape[1]
    code_count = wavelets.shape[0]
    first_row = lax.axis_index("slab") * depth_rows
    speed_sq = velocity * velocity
    selector = (
        source_codes[:, :, None] == jnp.arange(code_count, dtype=jnp.int32)[None, None, :]
    ).astype(jnp.float32)
    amplitude = jnp.einsum("gkc,ct->gkt", selector, wavelets, precision=lax.Precision.HIGHEST)
    previous = wave_state[0]
    current = wave_state[1]
    imaging = jnp.zeros((depth_rows, size_x, size_y), jnp.float32)
    for moment in range(step_count):
        padded = with_halo(current, (("slab", 2),), 4)
        source_grid = point_grid(
            source_cells, amplitude[:, :, moment], first_row, depth_rows, size_x, size_y
        )
        rec_grid = point_grid(
            receiver_cells, residuals[:, moment, :], first_row, depth_rows, size_x, size_y
        )
        driven = speed_sq * (laplacian(padded) + jnp.stack([source_grid, rec_grid], axis=1))
        imaging = imaging + jnp.sum(driven[:, 0] * current[:, 1], axis=0)
        previous, current = (current, 2.0 * current - previous + driven)
    summed = lax.psum_scatter(imaging, "shot", scatter_dimension=1, tiled=True)
    strip_rows = summed.shape[1]
    column = lax.axis_index("shot") * strip_rows
    speed_strip = lax.dynamic_slice_in_dim(velocity, column, strip_rows, 1)
    total_groups = groups_here * lax.axis_size("shot")
    gradient = -0.2 * summed / (speed_strip * math.sqrt(total_groups * step_count))
    stacked = jnp.concatenate([gradient[None], diffusivity], axis=0)
    extended = with_halo(stacked, (("shot", 2), ("slab", 1)), 2)
    partial_pass = smooth_step(extended[0], extended[1:, 1:-1, 1:-1, :])
    smoothed = smooth_step(partial_pass, diffusivity)
    new_momentum = 0.9 * momentum + smoothed
    new_velocity = speed_strip - 0.02 * new_momentum
    return (current, new_momentum, new_velocity)


def solution(mesh):
    return jax.shard_map(
        on_device,
        mesh=mesh,
        in_specs=(
            P("slab", None, None),
            P(None, "shot", None, "slab", None, None),
            P("shot", None),
            P("shot", None),
            P(),
            P("shot", None),
            P("shot", None, None),
            P("slab", "shot", None),
            P(None, "slab", "shot", None),
        ),
        out_specs=(
            P("shot", None, "slab", None, None),
            P("slab", "shot", None),
            P("slab", "shot", None),
        ),
        check_vma=False,
    )
```

profile of v0, /device:TPU:0, one launch (start us, length us, event | category | flops | bytes accessed | tf_op | source)
XLA Modules:
  0.0 110.1 jit_solution(10289829085301739534)
XLA Ops:
  7.2 1.1 %slice_bitcast_fusion = f32[1,2,8,64,128]{4,3,2,1,0:T(8,128)S(1)} fusion(f32[2,1,2,8,64,128]{5,4,3,2,1,0:T(8,128)} %param.10), kind=kLoop, calls=%fused_computation.119 | loop fusion | bytes 1048576 | tf_op jit(solution)/shard_map/squeeze | solution.py:106
  8.4 4.9 %collective-permute-start.1 = (f32[1,2,4,64,128]{4,3,2,1,0:T(8,128)S(1)}, f32[1,2,4,64,128]{4,3,2,1,0:T(8,128)S(1)}, u32[]{:S(2)}, u32[]{:S(2)}) collective-permute-start(f32[1,2,4,64,128]{4,3,2,1,0:T(8,128)S(1)} %get-tuple-element.11), channel_id=1, source_target_pairs={{0,1},{1,2},{2,3},{4,5},{5,6},{6,7},{8,9},{9,10},{10,11},{12,13},{... | collective-permute-start | bytes 786440 | tf_op jit(solution)/shard_map/ppermute | solution.py:19
  13.4 1.3 %collective-permute-start = (f32[1,2,4,64,128]{4,3,2,1,0:T(8,128)S(1)}, f32[1,2,4,64,128]{4,3,2,1,0:T(8,128)}, u32[]{:S(2)}, u32[]{:S(2)}) collective-permute-start(f32[1,2,4,64,128]{4,3,2,1,0:T(8,128)S(1)} %get-tuple-element.12), channel_id=1, source_target_pairs={{1,0},{2,1},{3,2},{5,4},{6,5},{7,6},{9,8},{10,9},{11,10},{13,12},{... | collective-permute-start | bytes 786440 | tf_op jit(solution)/shard_map/ppermute | solution.py:21
  18.4 2.6 %scatter_custom_fusion.1 = f32[65536]{0:T(1024)} fusion(s32[256]{0:T(256)S(1)} %bitcast.68, f32[256]{0:T(256)S(1)} %bitcast.71, f32[]{:T(128)} %constant.19.clone.1), kind=kCustom, calls=%fused_computation.133 | custom fusion | flops 256 | bytes 262148 | tf_op jit(solution)/shard_map/scatter-add | solution.py:77
  21.0 1.3 %scatter_custom_fusion = f32[65536]{0:T(1024)} fusion(s32[4]{0:T(128)S(1)} %fusion.98, f32[4]{0:T(128)S(1)} %get-tuple-element.20, f32[]{:T(128)} %constant.19.clone.1), kind=kCustom, calls=%fused_computation.135 | custom fusion | flops 4 | bytes 262148 | tf_op jit(solution)/shard_map/scatter-add | solution.py:77
  22.3 0.9 collective-permute-done
  23.1 1.6 %select_maximum_fusion.2 = f32[1,2,16,72,136]{4,3,2,1,0:T(8,128)S(1)} fusion(f32[1,2,4,64,128]{4,3,2,1,0:T(8,128)} %collective-permute-done, f32[1,2,8,64,128]{4,3,2,1,0:T(8,128)S(1)} %slice_bitcast_fusion, f32[1,2,4,64,128]{4,3,2,1,0:T(8,128)S(1)} %collective-permute-done.1), kind=kLoop, calls=%fused_computation.10 | loop fusion | flops 4700160 | bytes 2301952 | tf_op jit(solution)/shard_map/concatenate | solution.py:17
  24.8 4.5 %fusion.67 = (f32[1,2,8,64,128]{4,3,2,1,0:T(8,128)S(1)}, f32[1,2,8,64,128]{4,3,2,1,0:T(8,128)}) fusion(f32[2,1,2,8,64,128]{5,4,3,2,1,0:T(8,128)} %param.10, f32[1,1,8,64,128]{4,3,2,1,0:T(8,128)} %bitcast.65, f32[1,1,8,64,128]{4,3,2,1,0:T(8,128)} %bitcast.67, f32[1,2,16,72,136]{4,3,2,1,0:T(8,128)S(1)} %select_maximum_fusion.2, ...), kind=kLoop, calls=%fused_computation.117 | loop fusion | flops 5636096 | bytes 12320768 | tf_op jit(solution)/shard_map/add | solution.py:118
  29.3 3.8 %collective-permute-start.3 = (f32[1,2,4,64,128]{4,3,2,1,0:T(8,128)S(1)}, f32[1,2,4,64,128]{4,3,2,1,0:T(8,128)S(1)}, u32[]{:S(2)}, u32[]{:S(2)}) collective-permute-start(f32[1,2,4,64,128]{4,3,2,1,0:T(8,128)S(1)} %get-tuple-element.9), channel_id=1, source_target_pairs={{0,1},{1,2},{2,3},{4,5},{5,6},{6,7},{8,9},{9,10},{10,11},{12,13},{... | collective-permute-start | bytes 786440 | tf_op jit(solution)/shard_map/ppermute | solution.py:19
  33.1 1.3 %collective-permute-start.2 = (f32[1,2,4,64,128]{4,3,2,1,0:T(8,128)S(1)}, f32[1,2,4,64,128]{4,3,2,1,0:T(8,128)}, u32[]{:S(2)}, u32[]{:S(2)}) collective-permute-start(f32[1,2,4,64,128]{4,3,2,1,0:T(8,128)S(1)} %get-tuple-element.10), channel_id=1, source_target_pairs={{1,0},{2,1},{3,2},{5,4},{6,5},{7,6},{9,8},{10,9},{11,10},{13,12},{... | collective-permute-start | bytes 786440 | tf_op jit(solution)/shard_map/ppermute | solution.py:21
  34.4 2.6 %scatter_custom_fusion.3 = f32[65536]{0:T(1024)} fusion(s32[256]{0:T(256)S(1)} %bitcast.69, f32[256]{0:T(256)S(1)} %bitcast.70, f32[]{:T(128)} %constant.19.clone.1), kind=kCustom, calls=%fused_computation.129 | custom fusion | flops 256 | bytes 262148 | tf_op jit(solution)/shard_map/scatter-add | solution.py:77
  37.0 1.3 %scatter_custom_fusion.2 = f32[65536]{0:T(1024)} fusion(s32[4]{0:T(128)S(1)} %fusion.98, f32[4]{0:T(128)S(1)} %get-tuple-element.19, f32[]{:T(128)} %constant.19.clone.1), kind=kCustom, calls=%fused_computation.131 | custom fusion | flops 4 | bytes 262148 | tf_op jit(solution)/shard_map/scatter-add | solution.py:77
  39.0 3.3 %collective-permute-done.2 = f32[1,2,4,64,128]{4,3,2,1,0:T(8,128)} collective-permute-done((f32[1,2,4,64,128]{4,3,2,1,0:T(8,128)S(1)}, f32[1,2,4,64,128]{4,3,2,1,0:T(8,128)}, u32[]{:S(2)}, u32[]{:S(2)}) %collective-permute-start.2) | collective-permute-done | bytes 262176 | tf_op jit(solution)/shard_map/ppermute | solution.py:21
  42.3 1.7 %select_maximum_fusion = f32[1,2,16,72,136]{4,3,2,1,0:T(8,128)S(1)} fusion(f32[1,2,4,64,128]{4,3,2,1,0:T(8,128)} %collective-permute-done.2, f32[1,2,8,64,128]{4,3,2,1,0:T(8,128)S(1)} %get-tuple-element.7, f32[1,2,4,64,128]{4,3,2,1,0:T(8,128)} %copy-done.4), kind=kLoop, calls=%fused_computation.8 | loop fusion | flops 4700160 | bytes 2301952 | tf_op jit(solution)/shard_map/concatenate | solution.py:17
  44.0 4.5 %subtract_add_fusion = (f32[1,2,8,64,128]{4,3,2,1,0:T(8,128)}, f32[1,2,8,64,128]{4,3,2,1,0:T(8,128)}) fusion(f32[1,2,8,64,128]{4,3,2,1,0:T(8,128)S(1)} %get-tuple-element.7, f32[2,1,2,8,64,128]{5,4,3,2,1,0:T(8,128)} %param.10, f32[1,1,8,64,128]{4,3,2,1,0:T(8,128)} %bitcast.64, f32[1,1,8,64,128]{4,3,2,1,0:T(8,128)} %bitcast.66, ...), kind=kLoop, calls=%fused_computation.118 | loop fusion | flops 5636096 | bytes 11796480 | tf_op jit(solution)/shard_map/add | solution.py:118
  48.6 1.8 %fusion.69 = f32[8,64,128]{2,1,0:T(8,128)} fusion(f32[1,2,8,64,128]{4,3,2,1,0:T(8,128)S(1)} %get-tuple-element.7, f32[1,2,8,64,128]{4,3,2,1,0:T(8,128)} %get-tuple-element.6, f32[1,2,8,64,128]{4,3,2,1,0:T(8,128)S(1)} %slice_bitcast_fusion, f32[1,2,8,64,128]{4,3,2,1,0:T(8,128)} %get-tuple-element.8), kind=kLoop, calls=%fused_computation.123 | loop fusion | flops 196608 | bytes 1310720 | tf_op jit(solution)/shard_map/add | solution.py:117
  50.4 34.6 %reduce-scatter.2.cloned.1.call-done = f32[8,8,128]{2,1,0:T(8,128)} async-done(((f32[8,64,128]{2,1,0:T(8,128)}), f32[8,8,128]{2,1,0:T(8,128)}) %reduce-scatter.2.cloned.1.call-update) | async-done | bytes 32784 | tf_op jit(solution)/shard_map/reduce_scatter | solution.py:119
  85.9 1.3 %collective-permute-start.4 = (f32[4,8,2,128]{3,2,1,0:T(2,128)S(1)}, f32[4,8,2,128]{3,2,1,0:T(2,128)S(1)}, u32[]{:S(2)}, u32[]{:S(2)}) collective-permute-start(f32[4,8,2,128]{3,2,1,0:T(2,128)S(1)} %get-tuple-element.15), channel_id=1, source_target_pairs={{0,4},{4,8},{8,12},{12,16},{16,20},{20,24},{24,28},{1,5},{5,9},{9,... | collective-permute-start | bytes 98312 | tf_op jit(solution)/shard_map/ppermute | solution.py:19
  87.2 1.3 %collective-permute-start.5 = (f32[4,8,2,128]{3,2,1,0:T(2,128)S(1)}, f32[4,8,2,128]{3,2,1,0:T(2,128)S(1)}, u32[]{:S(2)}, u32[]{:S(2)}) collective-permute-start(f32[4,8,2,128]{3,2,1,0:T(2,128)S(1)} %get-tuple-element.16), channel_id=1, source_target_pairs={{4,0},{8,4},{12,8},{16,12},{20,16},{24,20},{28,24},{5,1},{9,5},{13... | collective-permute-start | bytes 98312 | tf_op jit(solution)/shard_map/ppermute | solution.py:21
  88.5 3.5 %collective-permute-done.5 = f32[4,8,2,128]{3,2,1,0:T(2,128)S(1)} collective-permute-done((f32[4,8,2,128]{3,2,1,0:T(2,128)S(1)}, f32[4,8,2,128]{3,2,1,0:T(2,128)S(1)}, u32[]{:S(2)}, u32[]{:S(2)}) %collective-permute-start.5) | collective-permute-done | bytes 32800 | tf_op jit(solution)/shard_map/ppermute | solution.py:21
  92.0 3.4 %collective-permute-start.6 = (f32[4,2,12,128]{3,2,1,0:T(8,128)S(1)}, f32[4,2,12,128]{3,2,1,0:T(8,128)S(1)}, u32[]{:S(2)}, u32[]{:S(2)}) collective-permute-start(f32[4,2,12,128]{3,2,1,0:T(8,128)S(1)} %get-tuple-element.13), channel_id=1, source_target_pairs={{0,1},{1,2},{2,3},{4,5},{5,6},{6,7},{8,9},{9,10},{10,11},{12,13},{... | collective-permute-start | bytes 147464 | tf_op jit(solution)/shard_map/ppermute | solution.py:19
  95.4 1.3 %collective-permute-start.7 = (f32[4,2,12,128]{3,2,1,0:T(8,128)S(1)}, f32[4,2,12,128]{3,2,1,0:T(8,128)S(1)}, u32[]{:S(2)}, u32[]{:S(2)}) collective-permute-start(f32[4,2,12,128]{3,2,1,0:T(8,128)S(1)} %get-tuple-element.14), channel_id=1, source_target_pairs={{1,0},{2,1},{3,2},{5,4},{6,5},{7,6},{9,8},{10,9},{11,10},{13,12},{... | collective-permute-start | bytes 147464 | tf_op jit(solution)/shard_map/ppermute | solution.py:21
  97.3 4.3 %collective-permute-done.7 = f32[4,2,12,128]{3,2,1,0:T(8,128)S(1)} collective-permute-done((f32[4,2,12,128]{3,2,1,0:T(8,128)S(1)}, f32[4,2,12,128]{3,2,1,0:T(8,128)S(1)}, u32[]{:S(2)}, u32[]{:S(2)}) %collective-permute-start.7) | collective-permute-done | bytes 49184 | tf_op jit(solution)/shard_map/ppermute | solution.py:21
  101.8 1.5 %multiply_subtract_fusion = (f32[8,8,128]{2,1,0:T(8,128)}, f32[8,8,128]{2,1,0:T(8,128)}) fusion(f32[8,64,128]{2,1,0:T(8,128)} %param.9, s32[]{:T(128)S(6)} %select_n.39, f32[10,10,128]{2,1,0:T(8,128)S(1)} %fusion.81, f32[3,8,8,128]{3,2,1,0:T(8,128)S(1)} %copy-done.1, f32[8,8,128]{2,1,0:T(8,128)S(1)} %copy-done.5), kind=kLoop, calls=%fused_computation.172 | loop fusion | flops 139264 | bytes 475140 | tf_op jit(solution)/shard_map/sub | solution.py:130
  (32 shorter events, 6.2 us)
Async XLA Ops:
  7.2 9.6 %copy-start = (f32[8,2]{0,1:T(2,128)S(1)}, f32[8,2]{0,1:T(2,128)}, u32[]{:S(2)}) copy-start(f32[8,2]{0,1:T(2,128)} %param.13) | copy-start | bytes 196
  7.2 10.4 %copy-start.2 = (f32[8,64,128]{2,1,0:T(8,128)S(1)}, f32[8,64,128]{2,1,0:T(8,128)}, u32[]{:S(2)}) copy-start(f32[8,64,128]{2,1,0:T(8,128)} %param.9) | copy-start | bytes 786436
  7.2 77.9 %reduce-scatter.2.cloned.1.call-start = ((), (), s32[]{:S(2)}) async-start(), calls=%async_computation.1 | async-start | bytes 294912 | tf_op jit(solution)/shard_map/reduce_scatter | solution.py:119
  8.4 13.9 %collective-permute-start.1 = (f32[1,2,4,64,128]{4,3,2,1,0:T(8,128)S(1)}, f32[1,2,4,64,128]{4,3,2,1,0:T(8,128)S(1)}, u32[]{:S(2)}, u32[]{:S(2)}) collective-permute-start(f32[1,2,4,64,128]{4,3,2,1,0:T(8,128)S(1)} %get-tuple-element.11), channel_id=1, source_target_pairs={{0,1},{1,2},{2,3},{4,5},{5,6},{6,7},{8,9},{9,10},{10,11},{12,13},{... | collective-permute-start | bytes 786440 | tf_op jit(solution)/shard_map/ppermute | solution.py:19
  13.4 9.8 %collective-permute-start = (f32[1,2,4,64,128]{4,3,2,1,0:T(8,128)S(1)}, f32[1,2,4,64,128]{4,3,2,1,0:T(8,128)}, u32[]{:S(2)}, u32[]{:S(2)}) collective-permute-start(f32[1,2,4,64,128]{4,3,2,1,0:T(8,128)S(1)} %get-tuple-element.12), channel_id=1, source_target_pairs={{1,0},{2,1},{3,2},{5,4},{6,5},{7,6},{9,8},{10,9},{11,10},{13,12},{... | collective-permute-start | bytes 786440 | tf_op jit(solution)/shard_map/ppermute | solution.py:21
  22.3 2.5 %copy-start.3 = (f32[1,2,4,64,128]{4,3,2,1,0:T(8,128)}, f32[1,2,4,64,128]{4,3,2,1,0:T(8,128)S(1)}, u32[]{:S(2)}) copy-start(f32[1,2,4,64,128]{4,3,2,1,0:T(8,128)S(1)} %collective-permute-done.1) | copy-start | bytes 786436
  29.3 9.0 %collective-permute-start.3 = (f32[1,2,4,64,128]{4,3,2,1,0:T(8,128)S(1)}, f32[1,2,4,64,128]{4,3,2,1,0:T(8,128)S(1)}, u32[]{:S(2)}, u32[]{:S(2)}) collective-permute-start(f32[1,2,4,64,128]{4,3,2,1,0:T(8,128)S(1)} %get-tuple-element.9), channel_id=1, source_target_pairs={{0,1},{1,2},{2,3},{4,5},{5,6},{6,7},{8,9},{9,10},{10,11},{12,13},{... | collective-permute-start | bytes 786440 | tf_op jit(solution)/shard_map/ppermute | solution.py:19
  33.1 9.2 %collective-permute-start.2 = (f32[1,2,4,64,128]{4,3,2,1,0:T(8,128)S(1)}, f32[1,2,4,64,128]{4,3,2,1,0:T(8,128)}, u32[]{:S(2)}, u32[]{:S(2)}) collective-permute-start(f32[1,2,4,64,128]{4,3,2,1,0:T(8,128)S(1)} %get-tuple-element.10), channel_id=1, source_target_pairs={{1,0},{2,1},{3,2},{5,4},{6,5},{7,6},{9,8},{10,9},{11,10},{13,12},{... | collective-permute-start | bytes 786440 | tf_op jit(solution)/shard_map/ppermute | solution.py:21
  38.3 0.7 copy-start.4
  44.0 41.8 %copy-start.1 = (f32[3,8,8,128]{3,2,1,0:T(8,128)S(1)}, f32[3,8,8,128]{3,2,1,0:T(8,128)}, u32[]{:S(2)}) copy-start(f32[3,8,8,128]{3,2,1,0:T(8,128)} %param.17) | copy-start | bytes 294916
  48.6 53.2 %copy-start.5 = (f32[8,8,128]{2,1,0:T(8,128)S(1)}, f32[8,8,128]{2,1,0:T(8,128)}, u32[]{:S(2)}) copy-start(f32[8,8,128]{2,1,0:T(8,128)} %param.16) | copy-start | bytes 98308
  85.9 2.6 %collective-permute-start.4 = (f32[4,8,2,128]{3,2,1,0:T(2,128)S(1)}, f32[4,8,2,128]{3,2,1,0:T(2,128)S(1)}, u32[]{:S(2)}, u32[]{:S(2)}) collective-permute-start(f32[4,8,2,128]{3,2,1,0:T(2,128)S(1)} %get-tuple-element.15), channel_id=1, source_target_pairs={{0,4},{4,8},{8,12},{12,16},{16,20},{20,24},{24,28},{1,5},{5,9},{9,... | collective-permute-start | bytes 98312 | tf_op jit(solution)/shard_map/ppermute | solution.py:19
  87.2 4.8 %collective-permute-start.5 = (f32[4,8,2,128]{3,2,1,0:T(2,128)S(1)}, f32[4,8,2,128]{3,2,1,0:T(2,128)S(1)}, u32[]{:S(2)}, u32[]{:S(2)}) collective-permute-start(f32[4,8,2,128]{3,2,1,0:T(2,128)S(1)} %get-tuple-element.16), channel_id=1, source_target_pairs={{4,0},{8,4},{12,8},{16,12},{20,16},{24,20},{28,24},{5,1},{9,5},{13... | collective-permute-start | bytes 98312 | tf_op jit(solution)/shard_map/ppermute | solution.py:21
  92.0 5.3 %collective-permute-start.6 = (f32[4,2,12,128]{3,2,1,0:T(8,128)S(1)}, f32[4,2,12,128]{3,2,1,0:T(8,128)S(1)}, u32[]{:S(2)}, u32[]{:S(2)}) collective-permute-start(f32[4,2,12,128]{3,2,1,0:T(8,128)S(1)} %get-tuple-element.13), channel_id=1, source_target_pairs={{0,1},{1,2},{2,3},{4,5},{5,6},{6,7},{8,9},{9,10},{10,11},{12,13},{... | collective-permute-start | bytes 147464 | tf_op jit(solution)/shard_map/ppermute | solution.py:19
  95.4 6.2 %collective-permute-start.7 = (f32[4,2,12,128]{3,2,1,0:T(8,128)S(1)}, f32[4,2,12,128]{3,2,1,0:T(8,128)S(1)}, u32[]{:S(2)}, u32[]{:S(2)}) collective-permute-start(f32[4,2,12,128]{3,2,1,0:T(8,128)S(1)} %get-tuple-element.14), channel_id=1, source_target_pairs={{1,0},{2,1},{3,2},{5,4},{6,5},{7,6},{9,8},{10,9},{11,10},{13,12},{... | collective-permute-start | bytes 147464 | tf_op jit(solution)/shard_map/ppermute | solution.py:21
Sparse Core Ops, SparseCore 0:
  50.6 34.4 reduce-scatter.1
where the time goes:
time: 112 us; the launch traced here: 110 us
  waiting for transfers between devices  47.1 us (42%)
  other arithmetic  26.6 us (24%)
  starting transfers between devices  18.7 us (17%)
  between operations  14.2 us (13%)
  local copies, waits for them, and re-layouts  2.7 us (2%)
    reduce_scatter x1, waiting for transfers between devices, on_device(): summed = lax.psum_scatter(imaging, 'shot', scatter_dimension=1, tiled=True)  34.6 us
    ppermute x4, starting transfers between devices, with_halo(): lax.ppermute(tail, axis, [(i, (i + 1) % count) for i in range(ends)])  13.5 us
    ppermute x4, waiting for transfers between devices, with_halo(): lax.ppermute(head, axis, [((i + 1) % count, i) for i in range(ends)])  11.9 us
    add x2, other arithmetic, on_device(): previous, current = (current, 2.0 * current - previous + driven)  9 us
    scatter-add x4, other arithmetic, point_grid(): grid = jnp.zeros((groups_here * volume,), jnp.float32).at[flat_index.resh...  7.79 us
    ppermute x4, starting transfers between devices, with_halo(): lax.ppermute(head, axis, [((i + 1) % count, i) for i in range(ends)])  5.17 us
    concatenate x3, other arithmetic, with_halo(): jnp.concatenate([lax.ppermute(tail, axis, [(i, (i + 1) % count) for i in...  3.39 us
  transfers between devices with their start and end apart: 9, of which 6 were waited for; matrix products, arithmetic and copies ran while one was open for 10% of the time, Pallas kernels for 0%

commit v1 on v0

v1 whole, which is shorter than its diff:
```python
import functools
import math

import jax
import jax.numpy as jnp
from jax import lax
from jax.experimental import pallas as pl
from jax.experimental.pallas import tpu as pltpu
from jax.sharding import PartitionSpec as P

STENCIL_TAPS = (-205.0 / 72.0, 8.0 / 5.0, -1.0 / 5.0, 8.0 / 315.0, -1.0 / 560.0)
RADIUS = 4
PAD = 8
STEPS = 2
F32 = jnp.float32


def even_pairs(count):
    return [(i, i ^ 1) for i in range(count) if (i ^ 1) < count]


def odd_pairs(count):
    low = [(i, i + 1) for i in range(1, count - 1, 2)]
    return low + [(b, a) for a, b in low]


def run_copies(pairs, sems):
    copies = [pltpu.make_async_copy(src, dst, sems.at[k]) for k, (src, dst) in enumerate(pairs)]
    for copy in copies:
        copy.start()
    return copies


def call(body, out_shapes, operands, in_specs=None, out_specs=None, scratch=(), aliases=None, flops=0):
    moved = sum(math.prod(o.shape) * 4 for o in operands) + sum(math.prod(o.shape) * 4 for o in out_shapes)
    whole = pl.BlockSpec(memory_space=pl.ANY)
    return pl.pallas_call(
        body,
        out_shape=list(out_shapes),
        in_specs=[whole if s == "any" else pl.BlockSpec(memory_space=pltpu.SMEM) if s == "smem" else pl.BlockSpec() for s in in_specs],
        out_specs=[whole if s == "any" else pl.BlockSpec() for s in out_specs],
        scratch_shapes=list(scratch),
        input_output_aliases=aliases or {},
        cost_estimate=pl.CostEstimate(flops=flops, bytes_accessed=moved, transcendentals=0),
    )(*operands)


def shape(*dims):
    return jax.ShapeDtypeStruct(dims, F32)


def y_sums(centre, lane, size_y):
    sums = []
    for r in range(1, RADIUS + 1):
        before = jnp.where(lane >= r, pltpu.roll(centre, r, 1), 0.0)
        after = jnp.where(lane < size_y - r, pltpu.roll(centre, size_y - r, 1), 0.0)
        sums.append(before + after)
    return sums


def laplacian_row(field, z, rows, size_x, size_y, lane):
    centre = field[z, PAD : PAD + size_x, :]
    along_y = y_sums(centre, lane, size_y)
    total = (3.0 * STENCIL_TAPS[0]) * centre
    for r in range(1, RADIUS + 1):
        ring = along_y[r - 1]
        ring = ring + (field[z, PAD + r : PAD + r + size_x, :] + field[z, PAD - r : PAD - r + size_x, :])
        if z + r < rows:
            ring = ring + field[z + r, PAD : PAD + size_x, :]
        if z - r >= 0:
            ring = ring + field[z - r, PAD : PAD + size_x, :]
        total = total + STENCIL_TAPS[r] * ring
    return total


def clear_sides(field, size_x):
    rows, _, size_y = field.shape
    edge = jnp.zeros((rows, PAD, size_y), F32)
    field[:, 0:PAD, :] = edge
    field[:, PAD + size_x : PAD + size_x + PAD, :] = edge


def pack_body(state, velocity, out_a, out_b, sems):
    depth = velocity.shape[0]
    even = lax.rem(lax.axis_index("slab"), 2) == 0
    at_a = jnp.where(even, depth - RADIUS, 0)
    at_b = jnp.where(even, 0, depth - RADIUS)
    pairs = []
    for out, at in ((out_a, at_a), (out_b, at_b)):
        pairs.append((state.at[1, 0, 0, pl.ds(at, RADIUS)], out.at[0:RADIUS]))
        pairs.append((state.at[1, 0, 1, pl.ds(at, RADIUS)], out.at[RADIUS : 2 * RADIUS]))
        pairs.append((velocity.at[pl.ds(at, RADIUS)], out.at[2 * RADIUS : 3 * RADIUS]))
    for copy in run_copies(pairs, sems):
        copy.wait()


def partial_u_body(state, velocity, kappa, partial, image, out_a, out_b, field, older, adjoint, speed, sems):
    depth, size_x, size_y = velocity.shape
    strip = kappa.shape[2]
    copies = run_copies(
        [
            (state.at[1, 0, 0], field.at[:, PAD : PAD + size_x]),
            (velocity, speed),
            (state.at[0, 0, 0], older),
            (state.at[1, 0, 1], adjoint),
        ],
        sems,
    )
    clear_sides(field, size_x)
    even = lax.rem(lax.axis_index("slab"), 2) == 0
    for j in range(3):
        tail = kappa[j, depth - 1]
        head = kappa[j, 0]
        at = RADIUS * size_x + j * strip
        out_a[at : at + strip, :] = jnp.where(even, tail, head)
        out_b[at : at + strip, :] = jnp.where(even, head, tail)
    lane = lax.broadcasted_iota(jnp.int32, (size_x, size_y), 1)
    for copy in copies:
        copy.wait()
    for z in range(depth):
        centre = field[z, PAD : PAD + size_x, :]
        v = speed[z]
        drive = (v * v) * laplacian_row(field, z, depth, size_x, size_y, lane)
        partial[z] = (2.0 * centre - older[z]) + drive
        image[z] = drive * adjoint[z]
    for k in range(RADIUS):
        tail = partial[depth - RADIUS + k]
        head = partial[k]
        out_a[k * size_x : (k + 1) * size_x, :] = jnp.where(even, tail, head)
        out_b[k * size_x : (k + 1) * size_x, :] = jnp.where(even, head, tail)


def partial_q_body(
    state, velocity, cells, residuals, kappa, partial, push, side_a, side_b, field, older, speed, grid_now, sems
):
    depth, size_x, size_y = velocity.shape
    strip = kappa.shape[2]
    copies = run_copies(
        [(state.at[1, 0, 1], field.at[:, PAD : PAD + size_x]), (velocity, speed), (state.at[0, 0, 1], older)], sems
    )
    clear_sides(field, size_x)
    even_strip = lax.rem(lax.axis_index("shot"), 2) == 0
    for j in range(3):
        tail = kappa[j, :, strip - 1, :]
        head = kappa[j, :, 0, :]
        side_a[j * depth : (j + 1) * depth, :] = jnp.where(even_strip, tail, head)
        side_b[j * depth : (j + 1) * depth, :] = jnp.where(even_strip, head, tail)
    volume = depth * size_x * size_y
    count = cells.shape[1]
    ids = cells[...] - lax.axis_index("slab") * volume
    inside = (ids >= 0) & (ids < volume)
    kept = jnp.where(inside, ids, 0)
    row = lax.div(kept, jnp.int32(size_y))
    column = kept - row * size_y
    rows = depth * size_x
    pick_row = (lax.broadcasted_iota(jnp.int32, (rows, count), 0) == row).astype(F32)
    pick_column = lax.broadcasted_iota(jnp.int32, (size_y, count), 0) == column
    for moment in range(STEPS):
        amounts = jnp.where(inside, residuals[0, moment : moment + 1, :], 0.0)
        grid_now[moment] = lax.dot_general(
            pick_row,
            jnp.where(pick_column, amounts, 0.0),
            (((1,), (1,)), ((), ())),
            precision=lax.Precision.HIGHEST,
            preferred_element_type=F32,
        )
    lane = lax.broadcasted_iota(jnp.int32, (size_x, size_y), 1)
    for copy in copies:
        copy.wait()
    for z in range(depth):
        centre = field[z, PAD : PAD + size_x, :]
        v = speed[z]
        vv = v * v
        at = slice(z * size_x, (z + 1) * size_x)
        drive = vv * (laplacian_row(field, z, depth, size_x, size_y, lane) + grid_now[0, at, :])
        partial[z] = (2.0 * centre - older[z]) + drive
        push[z] = vv * grid_now[1, at, :]


def image_body(
    state,
    velocity,
    partial_u,
    image0,
    partial_q,
    first_a,
    first_b,
    second_a,
    second_b,
    cells,
    codes,
    wavelets,
    fields,
    keep,
    send,
    q_next,
    edge_a,
    edge_b,
    speed,
    u_old,
    q_old,
    u_now,
    image,
    u_out,
    sems,
    out_sem,
    *,
    scale,
):
    depth, size_x, size_y = velocity.shape
    whole = depth + 2 * RADIUS
    own = slice(RADIUS, RADIUS + depth)
    here = lax.axis_index("slab")
    even = lax.rem(here, 2) == 0
    at_a = jnp.where(even, RADIUS + depth, 0)
    at_b = jnp.where(even, 0, RADIUS + depth)
    middle = slice(PAD, PAD + size_x)
    pairs = [
        (state.at[1, 0, 0], u_old.at[own]),
        (state.at[1, 0, 1], q_old.at[own]),
        (velocity, speed.at[own]),
        (partial_u, u_now.at[own, middle]),
        (image0, image.at[:, middle]),
        (partial_q, q_next),
    ]
    for got, at in ((first_a, at_a), (first_b, at_b)):
        pairs.append((got.at[0:RADIUS], u_old.at[pl.ds(at, RADIUS)]))
        pairs.append((got.at[RADIUS : 2 * RADIUS], q_old.at[pl.ds(at, RADIUS)]))
        pairs.append((got.at[2 * RADIUS : 3 * RADIUS], speed.at[pl.ds(at, RADIUS)]))
    for got, at in ((second_a, at_a), (second_b, at_b)):
        for k in range(RADIUS):
            pairs.append((got.at[k * size_x : (k + 1) * size_x], u_now.at[at + k, middle]))
    copies = run_copies(pairs, sems)
    clear_sides(u_now, size_x)
    clear_sides(image, size_x)
    lane = lax.broadcasted_iota(jnp.int32, (size_x, size_y), 1)
    row_lane = lax.broadcasted_iota(jnp.int32, (1, size_y), 1)
    for copy in copies:
        copy.wait()

    def across(field, z, inner):
        total = None
        for r in range(1, RADIUS + 1):
            for other in (z - r, z + r):
                if 0 <= other < whole and (RADIUS <= other < RADIUS + depth) != inner:
                    term = STENCIL_TAPS[r] * field[other]
                    total = term if total is None else total + term
        return total

    for z in range(whole):
        inner = RADIUS <= z < RADIUS + depth
        crossing = across(u_old, z, inner)
        v = speed[z]
        vv = v * v
        if crossing is not None:
            change = vv * crossing
            u_now[z, middle, :] = u_now[z, middle, :] + change
            if inner:
                image[z - RADIUS, middle, :] = image[z - RADIUS, middle, :] + change * q_old[z]
        if inner:
            crossing = across(q_old, z, True)
            if crossing is not None:
                q_next[z - RADIUS] = q_next[z - RADIUS] + vv * crossing

    plane = size_x * size_y
    first = here * depth - RADIUS

    def points(moment, act):
        for k in range(cells.shape[1]):
            cell = cells[0, k]
            amount = wavelets[codes[0, k], moment]
            z = lax.div(cell, plane) - first
            rest = lax.rem(cell, plane)
            x = lax.div(rest, size_y)
            y = lax.rem(rest, size_y)
            act(z, x, jnp.where(row_lane == y, amount, 0.0))

    def first_step(z, x, spot):
        @pl.when((z >= 0) & (z < whole))
        def _():
            v = speed[z, pl.ds(x, 1), :]
            change = (v * v) * spot
            u_now[z, pl.ds(PAD + x, 1), :] = u_now[z, pl.ds(PAD + x, 1), :] + change

            @pl.when((z >= RADIUS) & (z < RADIUS + depth))
            def _():
                at = (z - RADIUS, pl.ds(PAD + x, 1), slice(None))
                image[at] = image[at] + change * q_old[z, pl.ds(x, 1), :]

    points(0, first_step)

    for z in range(depth):
        v = speed[z + RADIUS]
        drive = (v * v) * laplacian_row(u_now, z + RADIUS, whole, size_x, size_y, lane)
        u_out[z] = (2.0 * u_now[z + RADIUS, middle, :] - u_old[z + RADIUS]) + drive
        image[z, middle, :] = image[z, middle, :] + drive * q_next[z]

    def second_step(z, x, spot):
        @pl.when((z >= RADIUS) & (z < RADIUS + depth))
        def _():
            v = speed[z, pl.ds(x, 1), :]
            change = (v * v) * spot
            to = z - RADIUS
            u_out[to, pl.ds(x, 1), :] = u_out[to, pl.ds(x, 1), :] + change
            at = (to, pl.ds(PAD + x, 1), slice(None))
            image[at] = image[at] + change * q_next[to, pl.ds(x, 1), :]

    points(1, second_step)
    copy_out = pltpu.make_async_copy(u_out, fields.at[0, 0], out_sem)
    copy_out.start()

    for z in range(depth):
        image[z, middle, :] = (-0.2 * image[z, middle, :]) / (speed[z + RADIUS] * scale)
    me = lax.axis_index("shot")
    core = lax.rem(me, 2)
    chip = lax.div(me, 2)
    chips = keep.shape[0]
    strip = size_x // (2 * chips)
    wide = strip + 4
    for m in range(chips):
        to = jnp.bitwise_xor(chip, m)
        for z in range(depth):
            at = PAD + 2 * m * strip - 2
            low = image[z, at : at + wide, :]
            high = image[z, at + strip : at + strip + wide, :]
            keep[to, z * wide : (z + 1) * wide, :] = jnp.where(core == 0, low, high)
            send[to, z * wide : (z + 1) * wide, :] = jnp.where(core == 0, high, low)
    for k in range(RADIUS):
        tail = q_next[depth - RADIUS + k]
        head = q_next[k]
        edge_a[k] = jnp.where(even, tail, head)
        edge_b[k] = jnp.where(even, head, tail)
    copy_out.wait()


def pair_sum_body(keep, got, *outs):
    for k, out in enumerate(outs):
        out[...] = keep[k] + got[k]


def strip_sum_body(*refs, count, wide):
    parts, (total, edge_a, edge_b) = refs[:count], refs[count:]
    added = parts[0][...]
    for part in parts[1:]:
        added = added + part[...]
    total[...] = added
    even = lax.rem(lax.axis_index("slab"), 2) == 0
    rows = total.shape[0]
    head = total[0 : 2 * wide, :]
    tail = total[rows - 2 * wide : rows, :]
    edge_a[...] = jnp.where(even, tail, head)
    edge_b[...] = jnp.where(even, head, tail)


def adjoint_body(fields_in, state, velocity, q_next, push, got_a, got_b, fields, field, q_out, sems, out_sem):
    depth, size_x, size_y = velocity.shape
    whole = depth + 2 * RADIUS
    even = lax.rem(lax.axis_index("slab"), 2) == 0
    at_a = jnp.where(even, RADIUS + depth, 0)
    at_b = jnp.where(even, 0, RADIUS + depth)
    middle = slice(PAD, PAD + size_x)
    copies = run_copies(
        [
            (q_next, field.at[RADIUS : RADIUS + depth, middle]),
            (got_a, field.at[pl.ds(at_a, RADIUS), middle]),
            (got_b, field.at[pl.ds(at_b, RADIUS), middle]),
            (state.at[1, 0, 1], q_out),
        ],
        sems,
    )
    clear_sides(field, size_x)
    lane = lax.broadcasted_iota(jnp.int32, (size_x, size_y), 1)
    for copy in copies:
        copy.wait()
    for z in range(depth):
        v = velocity[z]
        drive = (v * v) * laplacian_row(field, z + RADIUS, whole, size_x, size_y, lane) + push[z]
        q_out[z] = (2.0 * field[z + RADIUS, middle, :] - q_out[z]) + drive
    copy = pltpu.make_async_copy(q_out, fields.at[0, 1], out_sem)
    copy.start()
    copy.wait()


def smooth_body(
    total, got_a, got_b, kappa, second_a, second_b, side_a, side_b, speed, momentum, new_momentum, new_speed, grad, half, coef,
    *, size_x
):
    depth, strip, size_y = speed.shape
    wide = strip + 4
    even = lax.rem(lax.axis_index("slab"), 2) == 0
    even_strip = lax.rem(lax.axis_index("shot"), 2) == 0
    for k in range(2):
        at = slice(k * wide, (k + 1) * wide)
        grad[k, 0:wide, :] = jnp.where(even, got_b[at, :], got_a[at, :])
        grad[depth + 2 + k, 0:wide, :] = jnp.where(even, got_a[at, :], got_b[at, :])
    for z in range(depth):
        grad[z + 2, 0:wide, :] = total[z * wide : (z + 1) * wide, :]
    coef[...] = jnp.zeros(coef.shape, F32)
    for j in range(3):
        at = slice(RADIUS * size_x + j * strip, RADIUS * size_x + (j + 1) * strip)
        coef[j, 0, 1 : strip + 1, :] = jnp.where(even, second_b[at, :], second_a[at, :])
        coef[j, depth + 1, 1 : strip + 1, :] = jnp.where(even, second_a[at, :], second_b[at, :])
        left = jnp.where(even_strip, side_b[j * depth : (j + 1) * depth, :], side_a[j * depth : (j + 1) * depth, :])
        right = jnp.where(even_strip, side_a[j * depth : (j + 1) * depth, :], side_b[j * depth : (j + 1) * depth, :])
        for z in range(depth):
            coef[j, z + 1, 1 : strip + 1, :] = kappa[j, z]
            coef[j, z + 1, 0:1, :] = left[z : z + 1, :]
            coef[j, z + 1, strip + 1 : strip + 2, :] = right[z : z + 1, :]

    def step(source, z, rows, factors):
        centre = source[z, 1 : 1 + rows, :]
        lane = lax.broadcasted_iota(jnp.int32, centre.shape, 1)
        twice = 2.0 * centre
        along_z = source[z + 1, 1 : 1 + rows, :] - twice + source[z - 1, 1 : 1 + rows, :]
        along_x = source[z, 2 : 2 + rows, :] - twice + source[z, 0:rows, :]
        after = jnp.where(lane < size_y - 1, pltpu.roll(centre, size_y - 1, 1), 0.0)
        before = jnp.where(lane >= 1, pltpu.roll(centre, 1, 1), 0.0)
        along_y = after - twice + before
        return centre + factors[0] * along_z + factors[1] * along_x + factors[2] * along_y

    for z in range(depth + 2):
        half[z, 0 : strip + 2, :] = step(grad, z + 1, strip + 2, [coef[j, z, 0 : strip + 2, :] for j in range(3)])
    for z in range(depth):
        smoothed = step(half, z + 1, strip, [kappa[j, z] for j in range(3)])
        fresh = 0.9 * momentum[z] + smoothed
        new_momentum[z] = fresh
        new_speed[z] = speed[z] - 0.02 * fresh


def on_device(
    velocity,
    wave_state,
    source_cells,
    source_codes,
    wavelets,
    receiver_cells,
    residuals,
    momentum,
    diffusivity,
):
    depth, size_x, size_y = velocity.shape
    strip = momentum.shape[1]
    wide = strip + 4
    slabs = lax.axis_size("slab")
    shots = lax.axis_size("shot")
    chips = shots // 2
    z_even, z_odd = even_pairs(slabs), odd_pairs(slabs)
    cube = (depth, size_x, size_y)
    padded = (depth, size_x + 2 * PAD, size_y)
    whole = depth + 2 * RADIUS
    stencil = 45 * depth * size_x * size_y
    dma = pltpu.SemaphoreType.DMA

    block = shape(3 * RADIUS, size_x, size_y)
    out_a, out_b = call(
        pack_body, [block] * 2, (wave_state, velocity), ["any"] * 2, ["vmem"] * 2, [dma((6,))]
    )
    first_a = lax.ppermute(out_a, "slab", z_even)
    first_b = lax.ppermute(out_b, "slab", z_odd)

    flat = shape(RADIUS * size_x + 3 * strip, size_y)
    partial_u, image0, out_a, out_b = call(
        partial_u_body,
        [shape(*cube), shape(*cube), flat, flat],
        (wave_state, velocity, diffusivity),
        ["any", "any", "vmem"],
        ["vmem"] * 4,
        [pltpu.VMEM(padded, F32), pltpu.VMEM(cube, F32), pltpu.VMEM(cube, F32), pltpu.VMEM(cube, F32), dma((4,))],
        flops=stencil,
    )
    second_a = lax.ppermute(out_a, "slab", z_even)
    second_b = lax.ppermute(out_b, "slab", z_odd)

    side = shape(3 * depth, size_y)
    partial_q, push, out_a, out_b = call(
        partial_q_body,
        [shape(*cube), shape(*cube), side, side],
        (wave_state, velocity, receiver_cells, residuals, diffusivity),
        ["any", "any", "vmem", "vmem", "vmem"],
        ["vmem"] * 4,
        [
            pltpu.VMEM(padded, F32),
            pltpu.VMEM(cube, F32),
            pltpu.VMEM(cube, F32),
            pltpu.VMEM((STEPS, depth * size_x, size_y), F32),
            dma((3,)),
        ],
        flops=2 * stencil,
    )
    side_a = lax.ppermute(out_a, "shot", even_pairs(shots))
    side_b = lax.ppermute(out_b, "shot", odd_pairs(shots))
    speed_strip = lax.dynamic_slice_in_dim(velocity, lax.axis_index("shot") * strip, strip, 1)

    part = shape(chips, depth * wide, size_y)
    edge = shape(RADIUS, size_x, size_y)
    extended = (whole, size_x, size_y)
    fields, keep, send, q_next, out_a, out_b = call(
        functools.partial(image_body, scale=math.sqrt(shots * STEPS)),
        [shape(1, 2, *cube), part, part, shape(*cube), edge, edge],
        (
            wave_state,
            velocity,
            partial_u,
            image0,
            partial_q,
            first_a,
            first_b,
            second_a,
            second_b,
            source_cells,
            source_codes,
            wavelets,
        ),
        ["any"] * 9 + ["smem"] * 3,
        ["any"] + ["vmem"] * 5,
        [
            pltpu.VMEM(extended, F32),
            pltpu.VMEM(extended, F32),
            pltpu.VMEM(extended, F32),
            pltpu.VMEM((whole, size_x + 2 * PAD, size_y), F32),
            pltpu.VMEM(padded, F32),
            pltpu.VMEM(cube, F32),
            dma((12 + 2 * RADIUS,)),
            dma,
        ],
        flops=2 * stencil,
    )
    got = lax.ppermute(send, "shot", even_pairs(shots))
    row_block = shape(depth * wide, size_y)
    parts = call(pair_sum_body, [row_block] * chips, (keep, got), ["vmem"] * 2, ["vmem"] * chips)
    arrived = [
        parts[0] if k == 0 else lax.ppermute(parts[k], "shot", [(i, i ^ (2 * k)) for i in range(shots)])
        for k in range(chips)
    ]
    edge_a = lax.ppermute(out_a, "slab", z_even)
    edge_b = lax.ppermute(out_b, "slab", z_odd)
    two = shape(2 * wide, size_y)
    total, out_a, out_b = call(
        functools.partial(strip_sum_body, count=chips, wide=wide),
        [row_block, two, two],
        arrived,
        ["vmem"] * chips,
        ["vmem"] * 3,
    )
    grad_a = lax.ppermute(out_a, "slab", z_even)
    grad_b = lax.ppermute(out_b, "slab", z_odd)
    (fields,) = call(
        adjoint_body,
        [shape(1, 2, *cube)],
        (fields, wave_state, velocity, q_next, push, edge_a, edge_b),
        ["any", "any", "vmem", "any", "vmem", "any", "any"],
        ["any"],
        [
            pltpu.VMEM((whole, size_x + 2 * PAD, size_y), F32),
            pltpu.VMEM(cube, F32),
            dma((4,)),
            dma,
        ],
        aliases={0: 0},
        flops=stencil,
    )
    tall = 8 * ((wide + 7) // 8)
    new_momentum, new_velocity = call(
        functools.partial(smooth_body, size_x=size_x),
        [shape(*momentum.shape)] * 2,
        (total, grad_a, grad_b, diffusivity, second_a, second_b, side_a, side_b, speed_strip, momentum),
        ["vmem"] * 10,
        ["vmem"] * 2,
        [
            pltpu.VMEM((depth + 4, tall, size_y), F32),
            pltpu.VMEM((depth + 2, tall, size_y), F32),
            pltpu.VMEM((3, depth + 2, tall, size_y), F32),
        ],
    )
    return (fields, new_momentum, new_velocity)


def solution(mesh):
    return jax.shard_map(
        on_device,
        mesh=mesh,
        in_specs=(
            P("slab", None, None),
            P(None, "shot", None, "slab", None, None),
            P("shot", None),
            P("shot", None),
            P(),
            P("shot", None),
            P("shot", None, None),
            P("slab", "shot", None),
            P(None, "slab", "shot", None),
        ),
        out_specs=(
            P("shot", None, "slab", None, None),
            P("slab", "shot", None),
            P("slab", "shot", None),
        ),
        check_vma=False,
    )
```

time: 112 us -> 54.9 us (0.49)
  the two profiles are of different devices: /device:TPU:0 before, /device:TPU:1 now
where the time goes in v1:
time: 54.9 us; the launch traced here: 54.3 us
  starting transfers between devices  24.8 us (45%)
  Pallas kernels  23 us (42%)
  local copies, waits for them, and re-layouts  5.5 us (10%)
  between operations  0.93 us (2%)
    pallas_call x8, Pallas kernels, call(): pl.pallas_call(body, out_shape=list(out_shapes), in_specs=[whole if s ==...  23 us
    unnamed x37, local copies, waits for them, and re-layouts  4.14 us
    ppermute x1, starting transfers between devices, on_device(): second_a = lax.ppermute(out_a, 'slab', z_even)  3.88 us
    ppermute x1, starting transfers between devices, on_device(): grad_a = lax.ppermute(out_a, 'slab', z_even)  3.74 us
    ppermute x1, starting transfers between devices, on_device(): side_b = lax.ppermute(out_b, 'shot', odd_pairs(shots))  3.52 us
    ppermute x1, starting transfers between devices, on_device(): edge_a = lax.ppermute(out_a, 'slab', z_even)  3.28 us
    ppermute x3, starting transfers between devices, on_device(): lax.ppermute(parts[k], 'shot', [(i, i ^ 2 * k) for i in range(shots)])  2.69 us
    ppermute x1, starting transfers between devices, on_device(): first_a = lax.ppermute(out_a, 'slab', z_even)  2.19 us
  transfers between devices with their start and end apart: 14, of which 0 were waited for; matrix products, arithmetic and copies ran while one was open for 4% of the time, Pallas kernels for 25%

profile of v1, /device:TPU:1, one launch (start us, length us, event | category | flops | bytes accessed | tf_op | source)
XLA Modules:
  0.0 54.3 jit_solution(8415841647439824326)
XLA Ops:
  0.6 2.2 %shard_map.114 = (f32[12,64,128]{2,1,0:T(8,128)}, f32[12,64,128]{2,1,0:T(8,128)}) custom-call(f32[2,1,2,8,64,128]{5,4,3,2,1,0:T(8,128)} %state.9, f32[8,64,128]{2,1,0:T(8,128)} %velocity.9), custom_call_target="tpu_custom_call" | custom-call | bytes 2097152 | tf_op jit(solution)/shard_map/pallas_call | solution.py:37
  2.8 2.2 %collective-permute-start = (f32[12,64,128]{2,1,0:T(8,128)}, f32[12,64,128]{2,1,0:T(8,128)S(1)}, u32[]{:S(2)}, u32[]{:S(2)}) collective-permute-start(f32[12,64,128]{2,1,0:T(8,128)} %get-tuple-element.31), channel_id=1, source_target_pairs={{0,1},{1,0},{2,3},{3,2},{4,5},{5,4},{6,7},{7,6},{8,9},{9,8},{10,11... | collective-permute-start | bytes 1179656 | tf_op jit(solution)/shard_map/ppermute | solution.py:458
  5.0 0.7 %collective-permute-start.1 = (f32[12,64,128]{2,1,0:T(8,128)}, f32[12,64,128]{2,1,0:T(8,128)S(1)}, u32[]{:S(2)}, u32[]{:S(2)}) collective-permute-start(f32[12,64,128]{2,1,0:T(8,128)} %get-tuple-element.32), channel_id=1, source_target_pairs={{1,2},{2,1},{5,6},{6,5},{9,10},{10,9},{13,14},{14,13},{17,18},{18,... | collective-permute-start | bytes 1179656 | tf_op jit(solution)/shard_map/ppermute | solution.py:459
  5.7 3.6 %shard_map.112 = (f32[8,64,128]{2,1,0:T(8,128)}, f32[8,64,128]{2,1,0:T(8,128)}, f32[280,128]{1,0:T(8,128)}, f32[280,128]{1,0:T(8,128)}) custom-call(f32[2,1,2,8,64,128]{5,4,3,2,1,0:T(8,128)} %state.9, f32[8,64,128]{2,1,0:T(8,128)} %velocity.9, f32[3,8,8,128]{3,2,1,0:T(8,128)} %kappa.5), custom_call_target="tpu_custom_call" | custom-call | flops 2949120 | bytes 2220032 | tf_op jit(solution)/shard_map/pallas_call | solution.py:37
  9.3 3.9 %collective-permute-start.2 = (f32[280,128]{1,0:T(8,128)}, f32[280,128]{1,0:T(8,128)S(1)}, u32[]{:S(2)}, u32[]{:S(2)}) collective-permute-start(f32[280,128]{1,0:T(8,128)} %get-tuple-element.33), channel_id=1, source_target_pairs={{0,1},{1,0},{2,3},{3,2},{4,5},{5,4},{6,7},{7,6},{8,9},{9,8},{10,11... | collective-permute-start | bytes 430088 | tf_op jit(solution)/shard_map/ppermute | solution.py:471
  13.2 0.7 %collective-permute-start.3 = (f32[280,128]{1,0:T(8,128)}, f32[280,128]{1,0:T(8,128)S(1)}, u32[]{:S(2)}, u32[]{:S(2)}) collective-permute-start(f32[280,128]{1,0:T(8,128)} %get-tuple-element.34), channel_id=1, source_target_pairs={{1,2},{2,1},{5,6},{6,5},{9,10},{10,9},{13,14},{14,13},{17,18},{18,... | collective-permute-start | bytes 430088 | tf_op jit(solution)/shard_map/ppermute | solution.py:472
  13.9 0.7 %copy.13.wavelets = f32[8,2]{1,0:T(8,128)} copy(f32[8,2]{0,1:T(2,128)S(1)} %copy-done.14) | data formatting | bytes 128 | tf_op args[4]
  14.5 3.4 %shard_map.113 = (f32[8,64,128]{2,1,0:T(8,128)}, f32[8,64,128]{2,1,0:T(8,128)}, f32[24,128]{1,0:T(8,128)}, f32[24,128]{1,0:T(8,128)}) custom-call(f32[2,1,2,8,64,128]{5,4,3,2,1,0:T(8,128)} %state.9, f32[8,64,128]{2,1,0:T(8,128)} %velocity.9, s32[1,256]{1,0:T(1,128)} %cells.2, f32[1,2,256]{2,1,0:T(2,128)} %residuals.1, f32[3,8,8,128]{3,2,1,0:T(8,128)} %kappa.5), custom_call_target="tpu_custom_call" | custom-call | flops 5898240 | bytes 1960960 | tf_op jit(solution)/shard_map/pallas_call | solution.py:37
  19.0 5.0 %shard_map.115 = (f32[1,2,8,64,128]{4,3,2,1,0:T(8,128)}, f32[4,96,128]{2,1,0:T(8,128)}, f32[4,96,128]{2,1,0:T(8,128)}, f32[8,64,128]{2,1,0:T(8,128)}, f32[4,64,128]{2,1,0:T(8,128)}, /*index=5*/f32[4,64,128]{2,1,0:T(8,128)}) custom-call(f32[2,1,2,8,64,128]{5,4,3,2,1,0:T(8,128)} %state.9, f32[8,64,128]{2,1,0:T(8,128)} %velocity.9, ...), custom_call_target="tpu_custom_call" | custom-call | flops 5898240 | bytes 4612192 | tf_op jit(solution)/shard_map/pallas_call | solution.py:37
  24.1 1.6 %collective-permute-start.6 = (f32[4,96,128]{2,1,0:T(8,128)}, f32[4,96,128]{2,1,0:T(8,128)S(1)}, u32[]{:S(2)}, u32[]{:S(2)}) collective-permute-start(f32[4,96,128]{2,1,0:T(8,128)} %get-tuple-element.41), channel_id=1, source_target_pairs={{0,4},{4,0},{8,12},{12,8},{16,20},{20,16},{24,28},{28,24},{1,5},{5... | collective-permute-start | bytes 589832 | tf_op jit(solution)/shard_map/ppermute | solution.py:528
  25.6 3.3 %collective-permute-start.4 = (f32[4,64,128]{2,1,0:T(8,128)}, f32[4,64,128]{2,1,0:T(8,128)S(1)}, u32[]{:S(2)}, u32[]{:S(2)}) collective-permute-start(f32[4,64,128]{2,1,0:T(8,128)} %get-tuple-element.38), channel_id=1, source_target_pairs={{0,1},{1,0},{2,3},{3,2},{4,5},{5,4},{6,7},{7,6},{8,9},{9,8},{10,11... | collective-permute-start | bytes 393224 | tf_op jit(solution)/shard_map/ppermute | solution.py:535
  28.9 0.7 %copy-done.4 = f32[4,96,128]{2,1,0:T(8,128)} copy-done((f32[4,96,128]{2,1,0:T(8,128)}, f32[4,96,128]{2,1,0:T(8,128)S(1)}, u32[]{:S(2)}) %copy-start.4) | copy-done | bytes 196632
  29.6 1.7 %shard_map.117 = (f32[96,128]{1,0:T(8,128)}, f32[96,128]{1,0:T(8,128)}, f32[96,128]{1,0:T(8,128)}, f32[96,128]{1,0:T(8,128)}) custom-call(f32[4,96,128]{2,1,0:T(8,128)} %get-tuple-element.40.keep, f32[4,96,128]{2,1,0:T(8,128)} %copy-done.4), custom_call_target="tpu_custom_call" | custom-call | bytes 589824 | tf_op jit(solution)/shard_map/pallas_call | solution.py:37
  31.4 1.3 %collective-permute-start.7 = (f32[96,128]{1,0:T(8,128)}, f32[96,128]{1,0:T(8,128)S(1)}, u32[]{:S(2)}, u32[]{:S(2)}) collective-permute-start(f32[96,128]{1,0:T(8,128)} %get-tuple-element.43), channel_id=1, source_target_pairs={{0,8},{4,12},{8,0},{12,4},{16,24},{20,28},{24,16},{28,20},{1,9},{5... | collective-permute-start | bytes 147464 | tf_op jit(solution)/shard_map/ppermute | solution.py:532
  32.6 1.2 %collective-permute-start.8 = (f32[96,128]{1,0:T(8,128)}, f32[96,128]{1,0:T(8,128)S(1)}, u32[]{:S(2)}, u32[]{:S(2)}) collective-permute-start(f32[96,128]{1,0:T(8,128)} %get-tuple-element.44), channel_id=1, source_target_pairs={{0,16},{4,20},{8,24},{12,28},{16,0},{20,4},{24,8},{28,12},{1,17},{... | collective-permute-start | bytes 147464 | tf_op jit(solution)/shard_map/ppermute | solution.py:532
  34.0 0.7 %collective-permute-start.5 = (f32[4,64,128]{2,1,0:T(8,128)S(1)}, f32[4,64,128]{2,1,0:T(8,128)S(1)}, u32[]{:S(2)}, u32[]{:S(2)}) collective-permute-start(f32[4,64,128]{2,1,0:T(8,128)S(1)} %copy-done.15), channel_id=1, source_target_pairs={{1,2},{2,1},{5,6},{6,5},{9,10},{10,9},{13,14},{14,13},{17,18},{18,... | collective-permute-start | bytes 393224 | tf_op jit(solution)/shard_map/ppermute | solution.py:536
  34.7 1.3 %collective-permute-start.12 = (f32[24,128]{1,0:T(8,128)S(1)}, f32[24,128]{1,0:T(8,128)S(1)}, u32[]{:S(2)}, u32[]{:S(2)}) collective-permute-start(f32[24,128]{1,0:T(8,128)S(1)} %copy-done.17), channel_id=1, source_target_pairs={{0,4},{4,0},{8,12},{12,8},{16,20},{20,16},{24,28},{28,24},{1,5},{5... | collective-permute-start | bytes 36872 | tf_op jit(solution)/shard_map/ppermute | solution.py:490
  36.1 3.5 %collective-permute-start.13 = (f32[24,128]{1,0:T(8,128)S(1)}, f32[24,128]{1,0:T(8,128)S(1)}, u32[]{:S(2)}, u32[]{:S(2)}) collective-permute-start(f32[24,128]{1,0:T(8,128)S(1)} %copy-done.16), channel_id=1, source_target_pairs={{4,8},{12,16},{20,24},{8,4},{16,12},{24,20},{5,9},{13,17},{21,25},... | collective-permute-start | bytes 36872 | tf_op jit(solution)/shard_map/ppermute | solution.py:491
  40.2 1.5 %shard_map.118 = (f32[96,128]{1,0:T(8,128)}, f32[24,128]{1,0:T(8,128)}, f32[24,128]{1,0:T(8,128)}) custom-call(f32[96,128]{1,0:T(8,128)} %get-tuple-element.42.refs_0_, f32[96,128]{1,0:T(8,128)} %copy-done.7, f32[96,128]{1,0:T(8,128)} %copy-done.8, f32[96,128]{1,0:T(8,128)} %copy-done.9), custom_call_target="tpu_custom_call" | custom-call | bytes 270336 | tf_op jit(solution)/shard_map/pallas_call | solution.py:37
  41.7 3.7 %collective-permute-start.10 = (f32[24,128]{1,0:T(8,128)}, f32[24,128]{1,0:T(8,128)S(1)}, u32[]{:S(2)}, u32[]{:S(2)}) collective-permute-start(f32[24,128]{1,0:T(8,128)} %get-tuple-element.47), channel_id=1, source_target_pairs={{0,1},{1,0},{2,3},{3,2},{4,5},{5,4},{6,7},{7,6},{8,9},{9,8},{10,11... | collective-permute-start | bytes 36872 | tf_op jit(solution)/shard_map/ppermute | solution.py:545
  45.4 0.7 %collective-permute-start.11 = (f32[24,128]{1,0:T(8,128)}, f32[24,128]{1,0:T(8,128)S(1)}, u32[]{:S(2)}, u32[]{:S(2)}) collective-permute-start(f32[24,128]{1,0:T(8,128)} %get-tuple-element.48), channel_id=1, source_target_pairs={{1,2},{2,1},{5,6},{6,5},{9,10},{10,9},{13,14},{14,13},{17,18},{18,... | collective-permute-start | bytes 36872 | tf_op jit(solution)/shard_map/ppermute | solution.py:546
  46.1 1.4 %constant_dynamic-slice_fusion.speed = f32[8,8,128]{2,1,0:T(8,128)} fusion(f32[8,64,128]{2,1,0:T(8,128)} %velocity.9, s32[]{:T(128)S(6)} %select_n.3), kind=kLoop, calls=%fused_computation | loop fusion | bytes 65540 | tf_op jit(solution)/shard_map/dynamic_slice | solution.py:492
  48.1 3.5 %shard_map.116 = f32[1,2,8,64,128]{4,3,2,1,0:T(8,128)} custom-call(f32[1,2,8,64,128]{4,3,2,1,0:T(8,128)} %get-tuple-element.35.fields_in, f32[2,1,2,8,64,128]{5,4,3,2,1,0:T(8,128)} %state.9, f32[8,64,128]{2,1,0:T(8,128)} %velocity.9, f32[8,64,128]{2,1,0:T(8,128)} %get-tuple-element.36.q_next, ...), custom_call_target="tpu_custom_call", output_to_operand_aliasing={{}: (0, {})} | custom-call | flops 2949120 | bytes 3145728 | tf_op jit(solution)/shard_map/pallas_call | solution.py:37
  52.3 2.0 %shard_map.119 = (f32[8,8,128]{2,1,0:T(8,128)}, f32[8,8,128]{2,1,0:T(8,128)}) custom-call(f32[96,128]{1,0:T(8,128)} %get-tuple-element.46.total, f32[24,128]{1,0:T(8,128)} %copy-done.12, f32[24,128]{1,0:T(8,128)} %copy-done.13, f32[3,8,8,128]{3,2,1,0:T(8,128)} %kappa.5, f32[280,128]{1,0:T(8,128)} %copy-done, f32[280,128]{1,0:T(8,128)} %copy-done.1, ...), custom_call_target="tpu_custom_call" | custom-call | bytes 614400 | tf_op jit(solution)/shard_map/pallas_call | solution.py:37
  (50 shorter events, 3.0 us)
Async XLA Ops:
  2.8 15.2 %collective-permute-start = (f32[12,64,128]{2,1,0:T(8,128)}, f32[12,64,128]{2,1,0:T(8,128)S(1)}, u32[]{:S(2)}, u32[]{:S(2)}) collective-permute-start(f32[12,64,128]{2,1,0:T(8,128)} %get-tuple-element.31), channel_id=1, source_target_pairs={{0,1},{1,0},{2,3},{3,2},{4,5},{5,4},{6,7},{7,6},{8,9},{9,8},{10,11... | collective-permute-start | bytes 1179656 | tf_op jit(solution)/shard_map/ppermute | solution.py:458
  5.0 13.1 %collective-permute-start.1 = (f32[12,64,128]{2,1,0:T(8,128)}, f32[12,64,128]{2,1,0:T(8,128)S(1)}, u32[]{:S(2)}, u32[]{:S(2)}) collective-permute-start(f32[12,64,128]{2,1,0:T(8,128)} %get-tuple-element.32), channel_id=1, source_target_pairs={{1,2},{2,1},{5,6},{6,5},{9,10},{10,9},{13,14},{14,13},{17,18},{18,... | collective-permute-start | bytes 1179656 | tf_op jit(solution)/shard_map/ppermute | solution.py:459
  9.3 4.6 %copy-start.14 = (f32[8,2]{0,1:T(2,128)S(1)}, f32[8,2]{0,1:T(2,128)}, u32[]{:S(2)}) copy-start(f32[8,2]{0,1:T(2,128)} %param.13) | copy-start | bytes 196
  9.3 8.7 %collective-permute-start.2 = (f32[280,128]{1,0:T(8,128)}, f32[280,128]{1,0:T(8,128)S(1)}, u32[]{:S(2)}, u32[]{:S(2)}) collective-permute-start(f32[280,128]{1,0:T(8,128)} %get-tuple-element.33), channel_id=1, source_target_pairs={{0,1},{1,0},{2,3},{3,2},{4,5},{5,4},{6,7},{7,6},{8,9},{9,8},{10,11... | collective-permute-start | bytes 430088 | tf_op jit(solution)/shard_map/ppermute | solution.py:471
  13.2 4.8 %collective-permute-start.3 = (f32[280,128]{1,0:T(8,128)}, f32[280,128]{1,0:T(8,128)S(1)}, u32[]{:S(2)}, u32[]{:S(2)}) collective-permute-start(f32[280,128]{1,0:T(8,128)} %get-tuple-element.34), channel_id=1, source_target_pairs={{1,2},{2,1},{5,6},{6,5},{9,10},{10,9},{13,14},{14,13},{17,18},{18,... | collective-permute-start | bytes 430088 | tf_op jit(solution)/shard_map/ppermute | solution.py:472
  18.0 0.7 %copy-start.1 = (f32[280,128]{1,0:T(8,128)}, f32[280,128]{1,0:T(8,128)S(1)}, u32[]{:S(2)}) copy-start(f32[280,128]{1,0:T(8,128)S(1)} %collective-permute-done.3.second_b) | copy-start | bytes 430084
  18.0 0.8 %copy-start.2 = (f32[12,64,128]{2,1,0:T(8,128)}, f32[12,64,128]{2,1,0:T(8,128)S(1)}, u32[]{:S(2)}) copy-start(f32[12,64,128]{2,1,0:T(8,128)S(1)} %collective-permute-done.first_a) | copy-start | bytes 1179652
  18.1 0.9 %copy-start.3 = (f32[12,64,128]{2,1,0:T(8,128)}, f32[12,64,128]{2,1,0:T(8,128)S(1)}, u32[]{:S(2)}) copy-start(f32[12,64,128]{2,1,0:T(8,128)S(1)} %collective-permute-done.1.first_b) | copy-start | bytes 1179652
  24.1 4.9 %collective-permute-start.6 = (f32[4,96,128]{2,1,0:T(8,128)}, f32[4,96,128]{2,1,0:T(8,128)S(1)}, u32[]{:S(2)}, u32[]{:S(2)}) collective-permute-start(f32[4,96,128]{2,1,0:T(8,128)} %get-tuple-element.41), channel_id=1, source_target_pairs={{0,4},{4,0},{8,12},{12,8},{16,20},{20,16},{24,28},{28,24},{1,5},{5... | collective-permute-start | bytes 589832 | tf_op jit(solution)/shard_map/ppermute | solution.py:528
  25.6 19.8 %collective-permute-start.4 = (f32[4,64,128]{2,1,0:T(8,128)}, f32[4,64,128]{2,1,0:T(8,128)S(1)}, u32[]{:S(2)}, u32[]{:S(2)}) collective-permute-start(f32[4,64,128]{2,1,0:T(8,128)} %get-tuple-element.38), channel_id=1, source_target_pairs={{0,1},{1,0},{2,3},{3,2},{4,5},{5,4},{6,7},{7,6},{8,9},{9,8},{10,11... | collective-permute-start | bytes 393224 | tf_op jit(solution)/shard_map/ppermute | solution.py:535
  29.6 4.4 %copy-start.15 = (f32[4,64,128]{2,1,0:T(8,128)S(1)}, f32[4,64,128]{2,1,0:T(8,128)}, u32[]{:S(2)}) copy-start(f32[4,64,128]{2,1,0:T(8,128)} %get-tuple-element.39) | copy-start | bytes 393220
  31.3 3.4 %copy-start.17 = (f32[24,128]{1,0:T(8,128)S(1)}, f32[24,128]{1,0:T(8,128)}, u32[]{:S(2)}) copy-start(f32[24,128]{1,0:T(8,128)} %get-tuple-element.49) | copy-start | bytes 36868
  31.3 4.7 %copy-start.16 = (f32[24,128]{1,0:T(8,128)S(1)}, f32[24,128]{1,0:T(8,128)}, u32[]{:S(2)}) copy-start(f32[24,128]{1,0:T(8,128)} %get-tuple-element.50) | copy-start | bytes 36868
  31.4 3.4 %collective-permute-start.7 = (f32[96,128]{1,0:T(8,128)}, f32[96,128]{1,0:T(8,128)S(1)}, u32[]{:S(2)}, u32[]{:S(2)}) collective-permute-start(f32[96,128]{1,0:T(8,128)} %get-tuple-element.43), channel_id=1, source_target_pairs={{0,8},{4,12},{8,0},{12,4},{16,24},{20,28},{24,16},{28,20},{1,9},{5... | collective-permute-start | bytes 147464 | tf_op jit(solution)/shard_map/ppermute | solution.py:532
  32.6 3.4 %collective-permute-start.8 = (f32[96,128]{1,0:T(8,128)}, f32[96,128]{1,0:T(8,128)S(1)}, u32[]{:S(2)}, u32[]{:S(2)}) collective-permute-start(f32[96,128]{1,0:T(8,128)} %get-tuple-element.44), channel_id=1, source_target_pairs={{0,16},{4,20},{8,24},{12,28},{16,0},{20,4},{24,8},{28,12},{1,17},{... | collective-permute-start | bytes 147464 | tf_op jit(solution)/shard_map/ppermute | solution.py:532
  33.8 5.7 %collective-permute-start.9 = (f32[96,128]{1,0:T(8,128)}, f32[96,128]{1,0:T(8,128)S(1)}, u32[]{:S(2)}, u32[]{:S(2)}) collective-permute-start(f32[96,128]{1,0:T(8,128)} %get-tuple-element.45), channel_id=1, source_target_pairs={{0,24},{4,28},{8,16},{12,20},{16,8},{20,12},{24,0},{28,4},{1,25},{... | collective-permute-start | bytes 147464 | tf_op jit(solution)/shard_map/ppermute | solution.py:532
  34.0 13.4 %collective-permute-start.5 = (f32[4,64,128]{2,1,0:T(8,128)S(1)}, f32[4,64,128]{2,1,0:T(8,128)S(1)}, u32[]{:S(2)}, u32[]{:S(2)}) collective-permute-start(f32[4,64,128]{2,1,0:T(8,128)S(1)} %copy-done.15), channel_id=1, source_target_pairs={{1,2},{2,1},{5,6},{6,5},{9,10},{10,9},{13,14},{14,13},{17,18},{18,... | collective-permute-start | bytes 393224 | tf_op jit(solution)/shard_map/ppermute | solution.py:536
  34.7 4.9 %copy-start.7 = (f32[96,128]{1,0:T(8,128)}, f32[96,128]{1,0:T(8,128)S(1)}, u32[]{:S(2)}) copy-start(f32[96,128]{1,0:T(8,128)S(1)} %collective-permute-done.7.refs_1_) | copy-start | bytes 147460
  34.7 16.9 %collective-permute-start.12 = (f32[24,128]{1,0:T(8,128)S(1)}, f32[24,128]{1,0:T(8,128)S(1)}, u32[]{:S(2)}, u32[]{:S(2)}) collective-permute-start(f32[24,128]{1,0:T(8,128)S(1)} %copy-done.17), channel_id=1, source_target_pairs={{0,4},{4,0},{8,12},{12,8},{16,20},{20,16},{24,28},{28,24},{1,5},{5... | collective-permute-start | bytes 36872 | tf_op jit(solution)/shard_map/ppermute | solution.py:490
  36.0 3.6 %copy-start.8 = (f32[96,128]{1,0:T(8,128)}, f32[96,128]{1,0:T(8,128)S(1)}, u32[]{:S(2)}) copy-start(f32[96,128]{1,0:T(8,128)S(1)} %collective-permute-done.8.refs_2_) | copy-start | bytes 147460
  36.1 15.7 %collective-permute-start.13 = (f32[24,128]{1,0:T(8,128)S(1)}, f32[24,128]{1,0:T(8,128)S(1)}, u32[]{:S(2)}, u32[]{:S(2)}) collective-permute-start(f32[24,128]{1,0:T(8,128)S(1)} %copy-done.16), channel_id=1, source_target_pairs={{4,8},{12,16},{20,24},{8,4},{16,12},{24,20},{5,9},{13,17},{21,25},... | collective-permute-start | bytes 36872 | tf_op jit(solution)/shard_map/ppermute | solution.py:491
  41.7 10.0 %collective-permute-start.10 = (f32[24,128]{1,0:T(8,128)}, f32[24,128]{1,0:T(8,128)S(1)}, u32[]{:S(2)}, u32[]{:S(2)}) collective-permute-start(f32[24,128]{1,0:T(8,128)} %get-tuple-element.47), channel_id=1, source_target_pairs={{0,1},{1,0},{2,3},{3,2},{4,5},{5,4},{6,7},{7,6},{8,9},{9,8},{10,11... | collective-permute-start | bytes 36872 | tf_op jit(solution)/shard_map/ppermute | solution.py:545
  45.4 2.0 %copy-start.5 = (f32[4,64,128]{2,1,0:T(8,128)}, f32[4,64,128]{2,1,0:T(8,128)S(1)}, u32[]{:S(2)}) copy-start(f32[4,64,128]{2,1,0:T(8,128)S(1)} %collective-permute-done.4.got_a) | copy-start | bytes 393220
  45.4 6.3 %collective-permute-start.11 = (f32[24,128]{1,0:T(8,128)}, f32[24,128]{1,0:T(8,128)S(1)}, u32[]{:S(2)}, u32[]{:S(2)}) collective-permute-start(f32[24,128]{1,0:T(8,128)} %get-tuple-element.48), channel_id=1, source_target_pairs={{1,2},{2,1},{5,6},{6,5},{9,10},{10,9},{13,14},{14,13},{17,18},{18,... | collective-permute-start | bytes 36872 | tf_op jit(solution)/shard_map/ppermute | solution.py:546
  (8 other events, 5.0 us)

commit v2 on v1

v2 whole, which is shorter than its diff:
```python
import functools
import math

import jax
import jax.numpy as jnp
from jax import lax
from jax.experimental import pallas as pl
from jax.experimental.pallas import tpu as pltpu
from jax.sharding import PartitionSpec as P

STENCIL_TAPS = (-205.0 / 72.0, 8.0 / 5.0, -1.0 / 5.0, 8.0 / 315.0, -1.0 / 560.0)
RADIUS = 4
PAD = 8
STEPS = 2
F32 = jnp.float32
BYTES_PER_US = 3.69e6


def even_pairs(count):
    return [(i, i ^ 1) for i in range(count) if (i ^ 1) < count]


def odd_pairs(count):
    low = [(i, i + 1) for i in range(1, count - 1, 2)]
    return low + [(b, a) for a, b in low]


def run_copies(pairs, sems):
    copies = [pltpu.make_async_copy(src, dst, sems.at[k]) for k, (src, dst) in enumerate(pairs)]
    for copy in copies:
        copy.start()
    return copies


SPECS = {
    "any": pl.BlockSpec(memory_space=pl.ANY),
    "hbm": pl.BlockSpec(memory_space=pltpu.HBM),
    "vmem": pl.BlockSpec(memory_space=pltpu.VMEM),
    "block": pl.BlockSpec(),
}


def call(body, out_shapes, operands, in_specs=None, out_specs=None, scratch=(), aliases=None, us=0.1):
    return pl.pallas_call(
        body,
        out_shape=list(out_shapes),
        in_specs=[SPECS[s] for s in in_specs],
        out_specs=[SPECS[s] for s in out_specs],
        scratch_shapes=list(scratch),
        input_output_aliases=aliases or {},
        cost_estimate=pl.CostEstimate(flops=0, bytes_accessed=int(us * BYTES_PER_US), transcendentals=0),
        compiler_params=pltpu.CompilerParams(vmem_limit_bytes=16 * 1024 * 1024),
    )(*operands)


def shape(*dims):
    return jax.ShapeDtypeStruct(dims, F32)


def y_sums(centre, lane, size_y):
    sums = []
    for r in range(1, RADIUS + 1):
        before = jnp.where(lane >= r, pltpu.roll(centre, r, 1), 0.0)
        after = jnp.where(lane < size_y - r, pltpu.roll(centre, size_y - r, 1), 0.0)
        sums.append(before + after)
    return sums


def laplacian_row(field, z, rows, size_x, size_y, lane):
    centre = field[z, PAD : PAD + size_x, :]
    along_y = y_sums(centre, lane, size_y)
    total = (3.0 * STENCIL_TAPS[0]) * centre
    for r in range(1, RADIUS + 1):
        ring = along_y[r - 1]
        ring = ring + (field[z, PAD + r : PAD + r + size_x, :] + field[z, PAD - r : PAD - r + size_x, :])
        if z + r < rows:
            ring = ring + field[z + r, PAD : PAD + size_x, :]
        if z - r >= 0:
            ring = ring + field[z - r, PAD : PAD + size_x, :]
        total = total + STENCIL_TAPS[r] * ring
    return total


def clear_sides(field, size_x):
    rows, _, size_y = field.shape
    edge = jnp.zeros((rows, PAD, size_y), F32)
    field[:, 0:PAD, :] = edge
    field[:, PAD + size_x : PAD + size_x + PAD, :] = edge


def pack_body(state, velocity, out_a, out_b, sems):
    depth = velocity.shape[0]
    half = RADIUS // 2
    even = lax.rem(lax.axis_index("slab"), 2) == 0
    share = lax.rem(lax.axis_index("shot"), 2) * half
    at_a = jnp.where(even, depth - RADIUS, 0)
    at_b = jnp.where(even, 0, depth - RADIUS)
    pairs = []
    for out, at in ((out_a, at_a), (out_b, at_b)):
        for k in range(RADIUS):
            pairs.append((state.at[1, 0, 0, at + k], out.at[k]))
            pairs.append((state.at[1, 0, 1, at + k], out.at[RADIUS + k]))
        for k in range(half):
            pairs.append((velocity.at[at + share + k], out.at[2 * RADIUS + k]))
    for copy in run_copies(pairs, sems):
        copy.wait()


def point_cells(cells, codes, wavelets, moment, first, size_x, size_y, act):
    plane = size_x * size_y
    row_lane = lax.broadcasted_iota(jnp.int32, (1, size_y), 1)
    for k in range(cells.shape[1]):
        cell = cells[0, k]
        amount = wavelets[moment, codes[0, k]]
        z = lax.div(cell, plane) - first
        rest = lax.rem(cell, plane)
        x = lax.div(rest, size_y)
        y = lax.rem(rest, size_y)
        act(z, x, jnp.where(row_lane == y, amount, 0.0))


def weighted(terms):
    total = None
    for r, value in terms:
        term = STENCIL_TAPS[r] * value
        total = term if total is None else total + term
    return total


def partial_body(
    state, velocity, cells, residuals, kappa,
    partial_u, image, partial_q, push, out_a, out_b, side_a, side_b, field_u, field_q, grid_now,
):
    depth, size_x, size_y = velocity.shape
    strip = kappa.shape[2]
    even = lax.rem(lax.axis_index("slab"), 2) == 0
    even_strip = lax.rem(lax.axis_index("shot"), 2) == 0
    for j in range(3):
        tail = kappa[j, :, strip - 1, :]
        head = kappa[j, :, 0, :]
        side_a[j * depth : (j + 1) * depth, :] = jnp.where(even_strip, tail, head)
        side_b[j * depth : (j + 1) * depth, :] = jnp.where(even_strip, head, tail)
        tail = kappa[j, depth - 1]
        head = kappa[j, 0]
        at = 2 * RADIUS * size_x + j * strip
        out_a[at : at + strip, :] = jnp.where(even, tail, head)
        out_b[at : at + strip, :] = jnp.where(even, head, tail)
    for which, field in ((0, field_u), (1, field_q)):
        clear_sides(field, size_x)
        for z in range(depth):
            field[z, PAD : PAD + size_x, :] = state[1, 0, which, z]

    volume = depth * size_x * size_y
    count = cells.shape[1]
    ids = cells[...] - lax.axis_index("slab") * volume
    inside = (ids >= 0) & (ids < volume)
    kept = jnp.where(inside, ids, 0)
    row = lax.div(kept, jnp.int32(size_y))
    column = kept - row * size_y
    rows = depth * size_x
    pick_row = (lax.broadcasted_iota(jnp.int32, (rows, count), 0) == row).astype(F32)
    pick_column = lax.broadcasted_iota(jnp.int32, (size_y, count), 0) == column
    for moment in range(STEPS):
        amounts = jnp.where(inside, residuals[0, moment : moment + 1, :], 0.0)
        grid_now[moment] = lax.dot_general(
            pick_row,
            jnp.where(pick_column, amounts, 0.0),
            (((1,), (1,)), ((), ())),
            precision=lax.Precision.HIGHEST,
            preferred_element_type=F32,
        )

    lane = lax.broadcasted_iota(jnp.int32, (size_x, size_y), 1)
    for z in range(depth):
        at = slice(z * size_x, (z + 1) * size_x)
        v = velocity[z]
        vv = v * v
        drive = vv * laplacian_row(field_u, z, depth, size_x, size_y, lane)
        partial_u[z] = (2.0 * state[1, 0, 0, z] - state[0, 0, 0, z]) + drive
        image[z] = drive * state[1, 0, 1, z]
        drive = vv * (laplacian_row(field_q, z, depth, size_x, size_y, lane) + grid_now[0, at, :])
        partial_q[z] = (2.0 * state[1, 0, 1, z] - state[0, 0, 1, z]) + drive
        push[z] = vv * grid_now[1, at, :]
    for k in range(2 * RADIUS):
        source = partial_u if k < RADIUS else partial_q
        tail = source[depth - RADIUS + k % RADIUS]
        head = source[k % RADIUS]
        out_a[k * size_x : (k + 1) * size_x, :] = jnp.where(even, tail, head)
        out_b[k * size_x : (k + 1) * size_x, :] = jnp.where(even, head, tail)


def share_body(first_a, first_b, share):
    half = RADIUS // 2
    for k in range(half):
        share[k] = first_a[2 * RADIUS + k]
        share[half + k] = first_b[2 * RADIUS + k]


def halo_speed(k, share_own, share_got):
    half = RADIUS // 2
    row = k % RADIUS
    even = lax.rem(lax.axis_index("slab"), 2) == 0
    own = lax.rem(lax.axis_index("shot"), 2) == row // half
    at_a = jnp.where(own, share_own[row % half], share_got[row % half])
    at_b = jnp.where(own, share_own[half + row % half], share_got[half + row % half])
    return jnp.where(even, at_b, at_a) if k < RADIUS else jnp.where(even, at_a, at_b)


def halo_near(k, depth):
    if k < RADIUS:
        return [(r, k - RADIUS + r) for r in range(1, RADIUS + 1) if k - RADIUS + r >= 0]
    row = k - RADIUS
    return [(r, depth + row - r) for r in range(1, RADIUS + 1) if depth + row - r < depth]


def border_body(
    state, velocity, partial_u, image0, partial_q, first_a, first_b, u_own, image, q_next, u_edge, q_edge
):
    depth = velocity.shape[0]
    even = lax.rem(lax.axis_index("slab"), 2) == 0
    for k in range(2 * RADIUS):
        row = k % RADIUS
        one, other = (first_b, first_a) if k < RADIUS else (first_a, first_b)
        u_edge[k] = jnp.where(even, one[row], other[row])
        q_edge[k] = jnp.where(even, one[RADIUS + row], other[RADIUS + row])
    for z in range(depth):
        near = [(r, RADIUS + z - r) for r in range(1, RADIUS + 1) if z - r < 0]
        near += [(r, RADIUS + z + r - depth) for r in range(1, RADIUS + 1) if z + r >= depth]
        if not near:
            u_own[z] = partial_u[z]
            q_next[z] = partial_q[z]
            image[z] = image0[z]
            continue
        v = velocity[z]
        vv = v * v
        change = vv * weighted([(r, u_edge[k]) for r, k in near])
        u_own[z] = partial_u[z] + change
        image[z] = image0[z] + change * state[1, 0, 1, z]
        q_next[z] = partial_q[z] + vv * weighted([(r, q_edge[k]) for r, k in near])

def image_body(
    state, velocity, u_own, image0, q_next, share_own, share_got, second_a, second_b, cells, codes, wavelets,
    fields, keep, send, speed, u_now, image, u_out, cells_here, codes_here, wavelets_here, sems, out_sem, *, scale,
):
    small = run_copies([(cells, cells_here), (codes, codes_here), (wavelets, wavelets_here)], sems)
    depth, size_x, size_y = velocity.shape
    whole = depth + 2 * RADIUS
    half = RADIUS // 2
    here = lax.axis_index("slab")
    even = lax.rem(here, 2) == 0
    core = lax.rem(lax.axis_index("shot"), 2)
    middle = slice(PAD, PAD + size_x)
    clear_sides(u_now, size_x)
    clear_sides(image, size_x)
    lane = lax.broadcasted_iota(jnp.int32, (size_x, size_y), 1)
    for z in range(depth):
        u_now[RADIUS + z, middle, :] = u_own[z]
    for k in range(2 * RADIUS):
        row = k % RADIUS
        one, other = (second_b, second_a) if k < RADIUS else (second_a, second_b)
        rows = slice(row * size_x, (row + 1) * size_x)
        before = jnp.where(even, one[rows, :], other[rows, :])
        v = halo_speed(k, share_own, share_got)
        speed[k] = v
        near = halo_near(k, depth)
        z = k if k < RADIUS else k + depth
        u_now[z, middle, :] = before + (v * v) * weighted([(r, state[1, 0, 0, own]) for r, own in near])

    def first_step(z, x, spot):
        at = (z, pl.ds(PAD + x, 1), slice(None))

        @pl.when((z >= 0) & (z < whole) & ((z < RADIUS) | (z >= RADIUS + depth)))
        def _():
            v = speed[jnp.where(z < RADIUS, z, z - depth), pl.ds(x, 1), :]
            u_now[at] = u_now[at] + (v * v) * spot

        @pl.when((z >= RADIUS) & (z < RADIUS + depth))
        def _():
            v = velocity[z - RADIUS, pl.ds(x, 1), :]
            u_now[at] = u_now[at] + (v * v) * spot

    for copy in small:
        copy.wait()
    sources = (cells_here, codes_here, wavelets_here)
    point_cells(*sources, 0, here * depth - RADIUS, size_x, size_y, first_step)

    for z in range(depth):
        v = velocity[z]
        drive = (v * v) * laplacian_row(u_now, z + RADIUS, whole, size_x, size_y, lane)
        u_out[z] = (2.0 * u_now[RADIUS + z, middle, :] - state[1, 0, 0, z]) + drive
        image[z, middle, :] = (-0.2 * (image0[z] + drive * q_next[z])) / (v * scale)

    def image_spot(z, x, change, adjoint):
        v = velocity[z, pl.ds(x, 1), :]
        to = (z, pl.ds(PAD + x, 1), slice(None))
        image[to] = image[to] + (-0.2 * ((v * v) * change * adjoint)) / (v * scale)

    def first_image(z, x, spot):
        @pl.when((z >= 0) & (z < depth))
        def _():
            image_spot(z, x, spot, state[1, 0, 1, z, pl.ds(x, 1), :])

    def second_step(z, x, spot):
        @pl.when((z >= 0) & (z < depth))
        def _():
            at = (z, pl.ds(x, 1), slice(None))
            v = velocity[at]
            u_out[at] = u_out[at] + (v * v) * spot
            image_spot(z, x, spot, q_next[at])

    point_cells(*sources, 0, here * depth, size_x, size_y, first_image)
    point_cells(*sources, 1, here * depth, size_x, size_y, second_step)
    copy_out = pltpu.make_async_copy(u_out, fields.at[0, 0], out_sem)
    copy_out.start()
    chip = lax.div(lax.axis_index("shot"), 2)
    chips = keep.shape[0]
    strip = size_x // (2 * chips)
    wide = strip + 4
    for m in range(chips):
        to = jnp.bitwise_xor(chip, m)
        for z in range(depth):
            at = PAD + 2 * m * strip - 2
            low = image[z, at : at + wide, :]
            high = image[z, at + strip : at + strip + wide, :]
            keep[to, z * wide : (z + 1) * wide, :] = jnp.where(core == 0, low, high)
            send[to, z * wide : (z + 1) * wide, :] = jnp.where(core == 0, high, low)
    copy_out.wait()


def pair_sum_body(keep, got, *outs):
    for k, out in enumerate(outs):
        out[...] = keep[k] + got[k]


def strip_sum_body(*refs, count, wide):
    parts, (total, edge_a, edge_b) = refs[:count], refs[count:]
    added = parts[0][...]
    for part in parts[1:]:
        added = added + part[...]
    total[...] = added
    even = lax.rem(lax.axis_index("slab"), 2) == 0
    rows = total.shape[0]
    head = total[0 : 2 * wide, :]
    tail = total[rows - 2 * wide : rows, :]
    edge_a[...] = jnp.where(even, tail, head)
    edge_b[...] = jnp.where(even, head, tail)


def adjoint_body(
    fields_in, state, velocity, q_next, push, second_a, second_b, share_own, share_got, fields, field, q_out, out_sem
):
    depth, size_x, size_y = velocity.shape
    whole = depth + 2 * RADIUS
    even = lax.rem(lax.axis_index("slab"), 2) == 0
    middle = slice(PAD, PAD + size_x)
    clear_sides(field, size_x)
    for z in range(depth):
        field[RADIUS + z, middle, :] = q_next[z]
    for k in range(2 * RADIUS):
        row = k % RADIUS
        one, other = (second_b, second_a) if k < RADIUS else (second_a, second_b)
        rows = slice((RADIUS + row) * size_x, (RADIUS + row + 1) * size_x)
        before = jnp.where(even, one[rows, :], other[rows, :])
        v = halo_speed(k, share_own, share_got)
        z = k if k < RADIUS else k + depth
        near = halo_near(k, depth)
        field[z, middle, :] = before + (v * v) * weighted([(r, state[1, 0, 1, own]) for r, own in near])
    lane = lax.broadcasted_iota(jnp.int32, (size_x, size_y), 1)
    for z in range(depth):
        v = velocity[z]
        drive = (v * v) * laplacian_row(field, z + RADIUS, whole, size_x, size_y, lane) + push[z]
        q_out[z] = (2.0 * q_next[z] - state[1, 0, 1, z]) + drive
    copy = pltpu.make_async_copy(q_out, fields.at[0, 1], out_sem)
    copy.start()
    copy.wait()


def smooth_body(
    total, got_a, got_b, kappa, second_a, second_b, side_a, side_b, velocity, momentum, new_momentum, new_speed, grad, half, coef,
    *, size_x
):
    depth, strip, size_y = momentum.shape
    column = lax.axis_index("shot") * strip
    wide = strip + 4
    even = lax.rem(lax.axis_index("slab"), 2) == 0
    even_strip = lax.rem(lax.axis_index("shot"), 2) == 0
    for k in range(2):
        at = slice(k * wide, (k + 1) * wide)
        grad[k, 0:wide, :] = jnp.where(even, got_b[at, :], got_a[at, :])
        grad[depth + 2 + k, 0:wide, :] = jnp.where(even, got_a[at, :], got_b[at, :])
    for z in range(depth):
        grad[z + 2, 0:wide, :] = total[z * wide : (z + 1) * wide, :]
    coef[...] = jnp.zeros(coef.shape, F32)
    for j in range(3):
        at = slice(2 * RADIUS * size_x + j * strip, 2 * RADIUS * size_x + (j + 1) * strip)
        coef[j, 0, 1 : strip + 1, :] = jnp.where(even, second_b[at, :], second_a[at, :])
        coef[j, depth + 1, 1 : strip + 1, :] = jnp.where(even, second_a[at, :], second_b[at, :])
        left = jnp.where(even_strip, side_b[j * depth : (j + 1) * depth, :], side_a[j * depth : (j + 1) * depth, :])
        right = jnp.where(even_strip, side_a[j * depth : (j + 1) * depth, :], side_b[j * depth : (j + 1) * depth, :])
        for z in range(depth):
            coef[j, z + 1, 1 : strip + 1, :] = kappa[j, z]
            coef[j, z + 1, 0:1, :] = left[z : z + 1, :]
            coef[j, z + 1, strip + 1 : strip + 2, :] = right[z : z + 1, :]

    def step(source, z, rows, factors):
        centre = source[z, 1 : 1 + rows, :]
        lane = lax.broadcasted_iota(jnp.int32, centre.shape, 1)
        twice = 2.0 * centre
        along_z = source[z + 1, 1 : 1 + rows, :] - twice + source[z - 1, 1 : 1 + rows, :]
        along_x = source[z, 2 : 2 + rows, :] - twice + source[z, 0:rows, :]
        after = jnp.where(lane < size_y - 1, pltpu.roll(centre, size_y - 1, 1), 0.0)
        before = jnp.where(lane >= 1, pltpu.roll(centre, 1, 1), 0.0)
        along_y = after - twice + before
        return centre + factors[0] * along_z + factors[1] * along_x + factors[2] * along_y

    for z in range(depth + 2):
        half[z, 0 : strip + 2, :] = step(grad, z + 1, strip + 2, [coef[j, z, 0 : strip + 2, :] for j in range(3)])
    for z in range(depth):
        smoothed = step(half, z + 1, strip, [kappa[j, z] for j in range(3)])
        fresh = 0.9 * momentum[z] + smoothed
        new_momentum[z] = fresh
        new_speed[z] = velocity[z, pl.ds(column, strip), :] - 0.02 * fresh


def on_device(
    velocity,
    wave_state,
    source_cells,
    source_codes,
    wavelets,
    receiver_cells,
    residuals,
    momentum,
    diffusivity,
):
    depth, size_x, size_y = velocity.shape
    strip = momentum.shape[1]
    wide = strip + 4
    slabs = lax.axis_size("slab")
    shots = lax.axis_size("shot")
    chips = shots // 2
    z_even, z_odd = even_pairs(slabs), odd_pairs(slabs)
    cube = (depth, size_x, size_y)
    padded = (depth, size_x + 2 * PAD, size_y)
    whole = depth + 2 * RADIUS
    dma = pltpu.SemaphoreType.DMA

    half = RADIUS // 2
    block = shape(2 * RADIUS + half, size_x, size_y)
    out_a, out_b = call(
        pack_body, [block] * 2, tuple(pltpu.with_memory_space_constraint(x, pltpu.HBM) for x in (wave_state, velocity)), ["hbm"] * 2, ["vmem"] * 2, [dma((2 * (2 * RADIUS + half),))], us=1.3
    )
    first_a = lax.ppermute(out_a, "slab", z_even)
    first_b = lax.ppermute(out_b, "slab", z_odd)

    flat = shape(2 * RADIUS * size_x + 3 * strip, size_y)
    side = shape(3 * depth, size_y)
    edge = shape(RADIUS, size_x, size_y)
    partial_u, image0, partial_q, push, out_a, out_b, side_a, side_b = call(
        partial_body,
        [shape(*cube)] * 4 + [flat, flat, side, side],
        (wave_state, velocity, receiver_cells, residuals, diffusivity),
        ["vmem"] * 5,
        ["vmem"] * 8,
        [pltpu.VMEM(padded, F32)] * 2 + [pltpu.VMEM((STEPS, depth * size_x, size_y), F32)],
        us=1.7,
    )
    second_a = lax.ppermute(out_a, "slab", z_even)
    second_b = lax.ppermute(out_b, "slab", z_odd)
    side_a = lax.ppermute(side_a, "shot", even_pairs(shots))
    side_b = lax.ppermute(side_b, "shot", odd_pairs(shots))

    first_a, first_b, side_a, side_b = lax.optimization_barrier((first_a, first_b, side_a, side_b))
    (share_own,) = call(share_body, [edge], (first_a, first_b), ["vmem"] * 2, ["vmem"])
    share_got = lax.ppermute(share_own, "shot", even_pairs(shots))
    u_own, image0, q_next = call(
        border_body,
        [shape(*cube)] * 3,
        (wave_state, velocity, partial_u, image0, partial_q, first_a, first_b),
        ["vmem"] * 7,
        ["vmem"] * 3,
        [pltpu.VMEM((2 * RADIUS, size_x, size_y), F32)] * 2,
        us=0.3,
    )

    small = (source_cells, source_codes, wavelets.T)
    part = shape(chips, depth * wide, size_y)
    fields, keep, send = call(
        functools.partial(image_body, scale=math.sqrt(shots * STEPS)),
        [shape(1, 2, *cube), part, part],
        (wave_state, velocity, u_own, image0, q_next, share_own, share_got, second_a, second_b)
        + tuple(pltpu.with_memory_space_constraint(x, pltpu.HBM) for x in small),
        ["vmem"] * 9 + ["hbm"] * 3,
        ["any"] + ["vmem"] * 2,
        [
            pltpu.VMEM((2 * RADIUS, size_x, size_y), F32),
            pltpu.VMEM((whole, size_x + 2 * PAD, size_y), F32),
            pltpu.VMEM(padded, F32),
            pltpu.VMEM(cube, F32),
        ]
        + [pltpu.SMEM(x.shape, x.dtype) for x in small]
        + [dma((3,)), dma],
        us=2.3,
    )
    got = lax.ppermute(send, "shot", even_pairs(shots))
    (fields,) = call(
        adjoint_body,
        [shape(1, 2, *cube)],
        (fields, wave_state, velocity, q_next, push, second_a, second_b, share_own, share_got),
        ["any"] + ["vmem"] * 8,
        ["any"],
        [pltpu.VMEM((whole, size_x + 2 * PAD, size_y), F32), pltpu.VMEM(cube, F32), dma],
        aliases={0: 0},
        us=1.4,
    )
    got, fields = lax.optimization_barrier((got, fields))
    row_block = shape(depth * wide, size_y)
    parts = call(pair_sum_body, [row_block] * chips, (keep, got), ["vmem"] * 2, ["vmem"] * chips)
    arrived = [
        parts[0] if k == 0 else lax.ppermute(parts[k], "shot", [(i, i ^ (2 * k)) for i in range(shots)])
        for k in range(chips)
    ]
    two = shape(2 * wide, size_y)
    total, out_a, out_b = call(
        functools.partial(strip_sum_body, count=chips, wide=wide),
        [row_block, two, two],
        arrived,
        ["vmem"] * chips,
        ["vmem"] * 3,
    )
    grad_a = lax.ppermute(out_a, "slab", z_even)
    grad_b = lax.ppermute(out_b, "slab", z_odd)
    tall = 8 * ((wide + 7) // 8)
    new_momentum, new_velocity = call(
        functools.partial(smooth_body, size_x=size_x),
        [shape(*momentum.shape)] * 2,
        (total, grad_a, grad_b, diffusivity, second_a, second_b, side_a, side_b, velocity, momentum),
        ["vmem"] * 10,
        ["block"] * 2,
        [
            pltpu.VMEM((depth + 4, tall, size_y), F32),
            pltpu.VMEM((depth + 2, tall, size_y), F32),
            pltpu.VMEM((3, depth + 2, tall, size_y), F32),
        ],
        us=0.9,
    )
    return (fields, new_momentum, new_velocity)


def solution(mesh):
    return jax.shard_map(
        on_device,
        mesh=mesh,
        in_specs=(
            P("slab", None, None),
            P(None, "shot", None, "slab", None, None),
            P("shot", None),
            P("shot", None),
            P(),
            P("shot", None),
            P("shot", None, None),
            P("slab", "shot", None),
            P(None, "slab", "shot", None),
        ),
        out_specs=(
            P("shot", None, "slab", None, None),
            P("slab", "shot", None),
            P("slab", "shot", None),
        ),
        check_vma=False,
    )
```

time: 54.9 us -> 39.3 us (0.72)
  the two profiles are of different devices: /device:TPU:1 before, /device:TPU:16 now
where the time goes in v2:
time: 39.3 us; the launch traced here: 39 us
  starting transfers between devices  16.8 us (43%)
  waiting for transfers between devices  12.9 us (33%)
  Pallas kernels  7.58 us (19%)
  local copies, waits for them, and re-layouts  0.92 us (2%)
  between operations  0.84 us (2%)
    pallas_call x9, Pallas kernels, call(): pl.pallas_call(body, out_shape=list(out_shapes), in_specs=[SPECS[s] for s...  7.58 us
    ppermute x3, waiting for transfers between devices, on_device(): lax.ppermute(parts[k], 'shot', [(i, i ^ 2 * k) for i in range(shots)])  4.51 us
    ppermute x1, starting transfers between devices, on_device(): second_b = lax.ppermute(out_b, 'slab', z_odd)  3.92 us
    ppermute x3, starting transfers between devices, on_device(): lax.ppermute(parts[k], 'shot', [(i, i ^ 2 * k) for i in range(shots)])  3.55 us
    ppermute x1, starting transfers between devices, on_device(): share_got = lax.ppermute(share_own, 'shot', even_pairs(shots))  2.64 us
    ppermute x1, starting transfers between devices, on_device(): grad_b = lax.ppermute(out_b, 'slab', z_odd)  2.22 us
    ppermute x1, waiting for transfers between devices, on_device(): first_b = lax.ppermute(out_b, 'slab', z_odd)  2.22 us
    ppermute x1, starting transfers between devices, on_device(): first_b = lax.ppermute(out_b, 'slab', z_odd)  1.91 us
  transfers between devices with their start and end apart: 13, of which 9 were waited for; matrix products, arithmetic and copies ran while one was open for 0% of the time, Pallas kernels for 8%

profile of v2, /device:TPU:16, one launch (start us, length us, event | category | flops | bytes accessed | tf_op | source)
XLA Modules:
  0.0 39.0 jit_solution(16917405211793179657)
XLA Ops:
  0.6 1.3 %shard_map.113 = (f32[10,64,128]{2,1,0:T(8,128)S(1)}, f32[10,64,128]{2,1,0:T(8,128)S(1)}) custom-call(f32[2,1,2,8,64,128]{5,4,3,2,1,0:T(8,128)} %state.9, f32[8,64,128]{2,1,0:T(8,128)} %velocity.11), custom_call_target="tpu_custom_call" | custom-call | bytes 4797000 | tf_op jit(solution)/shard_map/pallas_call | solution.py:44
  2.0 1.6 %collective-permute-start = (f32[10,64,128]{2,1,0:T(8,128)S(1)}, f32[10,64,128]{2,1,0:T(8,128)S(1)}, u32[]{:S(2)}, u32[]{:S(2)}) collective-permute-start(f32[10,64,128]{2,1,0:T(8,128)S(1)} %get-tuple-element.37), channel_id=1, source_target_pairs={{0,1},{1,0},{2,3},{3,2},{4,5},{5,4},{6,7},{7,6},{8,9},{9,8},{10,11... | collective-permute-start | bytes 983048 | tf_op jit(solution)/shard_map/ppermute | solution.py:453
  3.6 1.9 %collective-permute-start.1 = (f32[10,64,128]{2,1,0:T(8,128)S(1)}, f32[10,64,128]{2,1,0:T(8,128)S(1)}, u32[]{:S(2)}, u32[]{:S(2)}) collective-permute-start(f32[10,64,128]{2,1,0:T(8,128)S(1)} %get-tuple-element.38), channel_id=1, source_target_pairs={{1,2},{2,1},{5,6},{6,5},{9,10},{10,9},{13,14},{14,13},{17,18},{18,... | collective-permute-start | bytes 983048 | tf_op jit(solution)/shard_map/ppermute | solution.py:454
  5.6 0.9 %copy-done.2 = f32[3,8,8,128]{3,2,1,0:T(8,128)S(1)} copy-done((f32[3,8,8,128]{3,2,1,0:T(8,128)S(1)}, f32[3,8,8,128]{3,2,1,0:T(8,128)}, u32[]{:S(2)}) %copy-start.2) | copy-done | bytes 98328
  6.5 1.5 %shard_map.112 = (f32[8,64,128]{2,1,0:T(8,128)S(1)}, f32[8,64,128]{2,1,0:T(8,128)S(1)}, f32[8,64,128]{2,1,0:T(8,128)S(1)}, f32[8,64,128]{2,1,0:T(8,128)S(1)}, f3...) custom-call(f32[2,1,2,8,64,128]{5,4,3,2,1,0:T(8,128)S(1)} %copy-done, ...), custom_call_target="tpu_custom_call" | custom-call | bytes 6273000 | tf_op jit(solution)/shard_map/pallas_call | solution.py:44
  8.1 3.9 %collective-permute-start.6 = (f32[536,128]{1,0:T(8,128)S(1)}, f32[536,128]{1,0:T(8,128)S(1)}, u32[]{:S(2)}, u32[]{:S(2)}) collective-permute-start(f32[536,128]{1,0:T(8,128)S(1)} %get-tuple-element.47), channel_id=1, source_target_pairs={{1,2},{2,1},{5,6},{6,5},{9,10},{10,9},{13,14},{14,13},{17,18},{18,... | collective-permute-start | bytes 823304 | tf_op jit(solution)/shard_map/ppermute | solution.py:469
  12.1 1.2 %collective-permute-done.2.side_a = f32[24,128]{1,0:T(8,128)S(1)} collective-permute-done((f32[24,128]{1,0:T(8,128)S(1)}, f32[24,128]{1,0:T(8,128)S(1)}, u32[]{:S(2)}, u32[]{:S(2)}) %collective-permute-start.2) | collective-permute-done | bytes 12320 | tf_op jit(solution)/shard_map/ppermute | solution.py:470
  13.3 0.7 %collective-permute-start.3 = (f32[24,128]{1,0:T(8,128)S(1)}, f32[24,128]{1,0:T(8,128)S(1)}, u32[]{:S(2)}, u32[]{:S(2)}) collective-permute-start(f32[24,128]{1,0:T(8,128)S(1)} %get-tuple-element.40), channel_id=1, source_target_pairs={{4,8},{12,16},{20,24},{8,4},{16,12},{24,20},{5,9},{13,17},{21,25},... | collective-permute-start | bytes 36872 | tf_op jit(solution)/shard_map/ppermute | solution.py:471
  13.9 2.2 %collective-permute-done.1.first_b = f32[10,64,128]{2,1,0:T(8,128)S(1)} collective-permute-done((f32[10,64,128]{2,1,0:T(8,128)S(1)}, f32[10,64,128]{2,1,0:T(8,128)S(1)}, u32[]{:S(2)}, u32[]{:S(2)}) %collective-permute-start.1) | collective-permute-done | bytes 327712 | tf_op jit(solution)/shard_map/ppermute | solution.py:454
  16.2 2.6 %collective-permute-start.4 = (f32[4,64,128]{2,1,0:T(8,128)S(1)}, f32[4,64,128]{2,1,0:T(8,128)S(1)}, u32[]{:S(2)}, u32[]{:S(2)}) collective-permute-start(f32[4,64,128]{2,1,0:T(8,128)S(1)} %shard_map.115.share_own), channel_id=1, source_target_pairs={{0,4},{4,0},{8,12},{12,8},{16,20},{20,16},{24,28},{28,24},{1,5},{5... | collective-permute-start | bytes 393224 | tf_op jit(solution)/shard_map/ppermute | solution.py:475
  18.8 0.2 shard_map.114
  19.0 1.5 %collective-permute-done.6.second_b = f32[536,128]{1,0:T(8,128)S(1)} collective-permute-done((f32[536,128]{1,0:T(8,128)S(1)}, f32[536,128]{1,0:T(8,128)S(1)}, u32[]{:S(2)}, u32[]{:S(2)}) %collective-permute-start.6) | collective-permute-done | bytes 274464 | tf_op jit(solution)/shard_map/ppermute | solution.py:469
  20.6 2.3 %shard_map.116 = (f32[1,2,8,64,128]{4,3,2,1,0:T(8,128)}, f32[4,96,128]{2,1,0:T(8,128)S(1)}, f32[4,96,128]{2,1,0:T(8,128)S(1)}) custom-call(f32[2,1,2,8,64,128]{5,4,3,2,1,0:T(8,128)S(1)} %copy-done, f32[8,64,128]{2,1,0:T(8,128)S(1)} %copy-done.1, f32[8,64,128]{2,1,0:T(8,128)S(1)} %get-tuple-element.43.u_own, f32[8,64,128]{2,1,0:T(8,128)S(1)} %get-tuple-element.44.image0, ...), custom_call_target="tpu_custom_call" | custom-call | bytes 8487000 | tf_op jit(solution)/shard_map/pallas_call | solution.py:44
  23.0 1.4 %shard_map.117 = f32[1,2,8,64,128]{4,3,2,1,0:T(8,128)} custom-call(f32[1,2,8,64,128]{4,3,2,1,0:T(8,128)} %get-tuple-element.49.fields_in, f32[2,1,2,8,64,128]{5,4,3,2,1,0:T(8,128)S(1)} %copy-done, f32[8,64,128]{2,1,0:T(8,128)S(1)} %copy-done.1, f32[8,64,128]{2,1,0:T(8,128)S(1)} %get-tuple-element.45.q_next, ...), custom_call_target="tpu_custom_call", output_to_operand_aliasing={{}: (0, {})} | custom-call | bytes 5166000 | tf_op jit(solution)/shard_map/pallas_call | solution.py:44
  24.4 1.7 %collective-permute-start.8 = (f32[96,128]{1,0:T(8,128)S(1)}, f32[96,128]{1,0:T(8,128)S(1)}, u32[]{:S(2)}, u32[]{:S(2)}) collective-permute-start(f32[96,128]{1,0:T(8,128)S(1)} %get-tuple-element.55), channel_id=1, source_target_pairs={{0,8},{4,12},{8,0},{12,4},{16,24},{20,28},{24,16},{28,20},{1,9},{5... | collective-permute-start | bytes 147464 | tf_op jit(solution)/shard_map/ppermute | solution.py:520
  26.1 1.4 %collective-permute-start.9 = (f32[96,128]{1,0:T(8,128)S(1)}, f32[96,128]{1,0:T(8,128)S(1)}, u32[]{:S(2)}, u32[]{:S(2)}) collective-permute-start(f32[96,128]{1,0:T(8,128)S(1)} %get-tuple-element.56), channel_id=1, source_target_pairs={{0,16},{4,20},{8,24},{12,28},{16,0},{20,4},{24,8},{28,12},{1,17},{... | collective-permute-start | bytes 147464 | tf_op jit(solution)/shard_map/ppermute | solution.py:520
  27.5 0.5 %collective-permute-start.10 = (f32[96,128]{1,0:T(8,128)S(1)}, f32[96,128]{1,0:T(8,128)S(1)}, u32[]{:S(2)}, u32[]{:S(2)}) collective-permute-start(f32[96,128]{1,0:T(8,128)S(1)} %get-tuple-element.57), channel_id=1, source_target_pairs={{0,24},{4,28},{8,16},{12,20},{16,8},{20,12},{24,0},{28,4},{1,25},{... | collective-permute-start | bytes 147464 | tf_op jit(solution)/shard_map/ppermute | solution.py:520
  28.0 0.6 %collective-permute-done.8.refs_1_ = f32[96,128]{1,0:T(8,128)S(1)} collective-permute-done((f32[96,128]{1,0:T(8,128)S(1)}, f32[96,128]{1,0:T(8,128)S(1)}, u32[]{:S(2)}, u32[]{:S(2)}) %collective-permute-start.8) | collective-permute-done | bytes 49184 | tf_op jit(solution)/shard_map/ppermute | solution.py:520
  28.6 1.6 %collective-permute-done.9.refs_2_ = f32[96,128]{1,0:T(8,128)S(1)} collective-permute-done((f32[96,128]{1,0:T(8,128)S(1)}, f32[96,128]{1,0:T(8,128)S(1)}, u32[]{:S(2)}, u32[]{:S(2)}) %collective-permute-start.9) | collective-permute-done | bytes 49184 | tf_op jit(solution)/shard_map/ppermute | solution.py:520
  30.2 2.3 %collective-permute-done.10.refs_3_ = f32[96,128]{1,0:T(8,128)S(1)} collective-permute-done((f32[96,128]{1,0:T(8,128)S(1)}, f32[96,128]{1,0:T(8,128)S(1)}, u32[]{:S(2)}, u32[]{:S(2)}) %collective-permute-start.10) | collective-permute-done | bytes 49184 | tf_op jit(solution)/shard_map/ppermute | solution.py:520
  32.6 2.2 %collective-permute-start.12 = (f32[24,128]{1,0:T(8,128)S(1)}, f32[24,128]{1,0:T(8,128)S(1)}, u32[]{:S(2)}, u32[]{:S(2)}) collective-permute-start(f32[24,128]{1,0:T(8,128)S(1)} %get-tuple-element.60), channel_id=1, source_target_pairs={{1,2},{2,1},{5,6},{6,5},{9,10},{10,9},{13,14},{14,13},{17,18},{18,... | collective-permute-start | bytes 36872 | tf_op jit(solution)/shard_map/ppermute | solution.py:532
  34.8 1.4 %collective-permute-done.11.got_a = f32[24,128]{1,0:T(8,128)S(1)} collective-permute-done((f32[24,128]{1,0:T(8,128)S(1)}, f32[24,128]{1,0:T(8,128)S(1)}, u32[]{:S(2)}, u32[]{:S(2)}) %collective-permute-start.11) | collective-permute-done | bytes 12320 | tf_op jit(solution)/shard_map/ppermute | solution.py:531
  36.3 1.9 %collective-permute-done.12.got_b = f32[24,128]{1,0:T(8,128)S(1)} collective-permute-done((f32[24,128]{1,0:T(8,128)S(1)}, f32[24,128]{1,0:T(8,128)S(1)}, u32[]{:S(2)}, u32[]{:S(2)}) %collective-permute-start.12) | collective-permute-done | bytes 12320 | tf_op jit(solution)/shard_map/ppermute | solution.py:532
  38.2 0.9 %shard_map.120 = (f32[8,8,128]{2,1,0:T(8,128)}, f32[8,8,128]{2,1,0:T(8,128)}) custom-call(f32[96,128]{1,0:T(8,128)S(1)} %get-tuple-element.58.total, f32[24,128]{1,0:T(8,128)S(1)} %collective-permute-done.11.got_a, f32[24,128]{1,0:T(8,128)S(1)} %collective-permute-done.12.got_b, f32[3,8,8,128]{3,2,1,0:T(8,128)S(1)} %copy-done.3, ...), custom_call_target="tpu_custom_call" | custom-call | bytes 3321000 | tf_op jit(solution)/shard_map/pallas_call | solution.py:44
  (25 shorter events, 0.4 us)
Async XLA Ops:
  0.6 4.9 %copy-start.1 = (f32[8,64,128]{2,1,0:T(8,128)S(1)}, f32[8,64,128]{2,1,0:T(8,128)}, u32[]{:S(2)}) copy-start(f32[8,64,128]{2,1,0:T(8,128)} %velocity.11) | copy-start | bytes 786436
  0.6 4.9 %copy-start = (f32[2,1,2,8,64,128]{5,4,3,2,1,0:T(8,128)S(1)}, f32[2,1,2,8,64,128]{5,4,3,2,1,0:T(8,128)}, u32[]{:S(2)}) copy-start(f32[2,1,2,8,64,128]{5,4,3,2,1,0:T(8,128)} %state.9) | copy-start | bytes 3145732
  2.0 3.6 %copy-start.5 = (f32[1,2,256]{2,1,0:T(2,128)S(1)}, f32[1,2,256]{2,1,0:T(2,128)}, u32[]{:S(2)}) copy-start(f32[1,2,256]{2,1,0:T(2,128)} %residuals.1) | copy-start | bytes 6148
  2.0 3.6 %copy-start.6 = (s32[1,256]{1,0:T(1,128)S(1)}, s32[1,256]{1,0:T(1,128)}, u32[]{:S(2)}) copy-start(s32[1,256]{1,0:T(1,128)} %cells.2) | copy-start | bytes 3076
  2.0 11.9 %collective-permute-start = (f32[10,64,128]{2,1,0:T(8,128)S(1)}, f32[10,64,128]{2,1,0:T(8,128)S(1)}, u32[]{:S(2)}, u32[]{:S(2)}) collective-permute-start(f32[10,64,128]{2,1,0:T(8,128)S(1)} %get-tuple-element.37), channel_id=1, source_target_pairs={{0,1},{1,0},{2,3},{3,2},{4,5},{5,4},{6,7},{7,6},{8,9},{9,8},{10,11... | collective-permute-start | bytes 983048 | tf_op jit(solution)/shard_map/ppermute | solution.py:453
  3.6 12.5 %collective-permute-start.1 = (f32[10,64,128]{2,1,0:T(8,128)S(1)}, f32[10,64,128]{2,1,0:T(8,128)S(1)}, u32[]{:S(2)}, u32[]{:S(2)}) collective-permute-start(f32[10,64,128]{2,1,0:T(8,128)S(1)} %get-tuple-element.38), channel_id=1, source_target_pairs={{1,2},{2,1},{5,6},{6,5},{9,10},{10,9},{13,14},{14,13},{17,18},{18,... | collective-permute-start | bytes 983048 | tf_op jit(solution)/shard_map/ppermute | solution.py:454
  5.6 0.9 %copy-start.2 = (f32[3,8,8,128]{3,2,1,0:T(8,128)S(1)}, f32[3,8,8,128]{3,2,1,0:T(8,128)}, u32[]{:S(2)}) copy-start(f32[3,8,8,128]{3,2,1,0:T(8,128)} %kappa.3) | copy-start | bytes 294916
  8.0 11.0 %collective-permute-start.5 = (f32[536,128]{1,0:T(8,128)S(1)}, f32[536,128]{1,0:T(8,128)S(1)}, u32[]{:S(2)}, u32[]{:S(2)}) collective-permute-start(f32[536,128]{1,0:T(8,128)S(1)} %get-tuple-element.46), channel_id=1, source_target_pairs={{0,1},{1,0},{2,3},{3,2},{4,5},{5,4},{6,7},{7,6},{8,9},{9,8},{10,11... | collective-permute-start | bytes 823304 | tf_op jit(solution)/shard_map/ppermute | solution.py:468
  8.1 12.5 %collective-permute-start.6 = (f32[536,128]{1,0:T(8,128)S(1)}, f32[536,128]{1,0:T(8,128)S(1)}, u32[]{:S(2)}, u32[]{:S(2)}) collective-permute-start(f32[536,128]{1,0:T(8,128)S(1)} %get-tuple-element.47), channel_id=1, source_target_pairs={{1,2},{2,1},{5,6},{6,5},{9,10},{10,9},{13,14},{14,13},{17,18},{18,... | collective-permute-start | bytes 823304 | tf_op jit(solution)/shard_map/ppermute | solution.py:469
  12.0 1.2 %collective-permute-start.2 = (f32[24,128]{1,0:T(8,128)S(1)}, f32[24,128]{1,0:T(8,128)S(1)}, u32[]{:S(2)}, u32[]{:S(2)}) collective-permute-start(f32[24,128]{1,0:T(8,128)S(1)} %get-tuple-element.39), channel_id=1, source_target_pairs={{0,4},{4,0},{8,12},{12,8},{16,20},{20,16},{24,28},{28,24},{1,5},{5... | collective-permute-start | bytes 36872 | tf_op jit(solution)/shard_map/ppermute | solution.py:470
  13.3 0.7 %collective-permute-start.3 = (f32[24,128]{1,0:T(8,128)S(1)}, f32[24,128]{1,0:T(8,128)S(1)}, u32[]{:S(2)}, u32[]{:S(2)}) collective-permute-start(f32[24,128]{1,0:T(8,128)S(1)} %get-tuple-element.40), channel_id=1, source_target_pairs={{4,8},{12,16},{20,24},{8,4},{16,12},{24,20},{5,9},{13,17},{21,25},... | collective-permute-start | bytes 36872 | tf_op jit(solution)/shard_map/ppermute | solution.py:471
  16.2 4.4 %collective-permute-start.4 = (f32[4,64,128]{2,1,0:T(8,128)S(1)}, f32[4,64,128]{2,1,0:T(8,128)S(1)}, u32[]{:S(2)}, u32[]{:S(2)}) collective-permute-start(f32[4,64,128]{2,1,0:T(8,128)S(1)} %shard_map.115.share_own), channel_id=1, source_target_pairs={{0,4},{4,0},{8,12},{12,8},{16,20},{20,16},{24,28},{28,24},{1,5},{5... | collective-permute-start | bytes 393224 | tf_op jit(solution)/shard_map/ppermute | solution.py:475
  22.9 1.5 %collective-permute-start.7 = (f32[4,96,128]{2,1,0:T(8,128)S(1)}, f32[4,96,128]{2,1,0:T(8,128)S(1)}, u32[]{:S(2)}, u32[]{:S(2)}) collective-permute-start(f32[4,96,128]{2,1,0:T(8,128)S(1)} %get-tuple-element.48), channel_id=1, source_target_pairs={{0,4},{4,0},{8,12},{12,8},{16,20},{20,16},{24,28},{28,24},{1,5},{5... | collective-permute-start | bytes 589832 | tf_op jit(solution)/shard_map/ppermute | solution.py:505
  24.4 4.2 %collective-permute-start.8 = (f32[96,128]{1,0:T(8,128)S(1)}, f32[96,128]{1,0:T(8,128)S(1)}, u32[]{:S(2)}, u32[]{:S(2)}) collective-permute-start(f32[96,128]{1,0:T(8,128)S(1)} %get-tuple-element.55), channel_id=1, source_target_pairs={{0,8},{4,12},{8,0},{12,4},{16,24},{20,28},{24,16},{28,20},{1,9},{5... | collective-permute-start | bytes 147464 | tf_op jit(solution)/shard_map/ppermute | solution.py:520
  26.1 4.1 %collective-permute-start.9 = (f32[96,128]{1,0:T(8,128)S(1)}, f32[96,128]{1,0:T(8,128)S(1)}, u32[]{:S(2)}, u32[]{:S(2)}) collective-permute-start(f32[96,128]{1,0:T(8,128)S(1)} %get-tuple-element.56), channel_id=1, source_target_pairs={{0,16},{4,20},{8,24},{12,28},{16,0},{20,4},{24,8},{28,12},{1,17},{... | collective-permute-start | bytes 147464 | tf_op jit(solution)/shard_map/ppermute | solution.py:520
  27.5 5.0 %collective-permute-start.10 = (f32[96,128]{1,0:T(8,128)S(1)}, f32[96,128]{1,0:T(8,128)S(1)}, u32[]{:S(2)}, u32[]{:S(2)}) collective-permute-start(f32[96,128]{1,0:T(8,128)S(1)} %get-tuple-element.57), channel_id=1, source_target_pairs={{0,24},{4,28},{8,16},{12,20},{16,8},{20,12},{24,0},{28,4},{1,25},{... | collective-permute-start | bytes 147464 | tf_op jit(solution)/shard_map/ppermute | solution.py:520
  32.5 5.7 %copy-start.3 = (f32[3,8,8,128]{3,2,1,0:T(8,128)S(1)}, f32[3,8,8,128]{3,2,1,0:T(8,128)}, u32[]{:S(2)}) copy-start(f32[3,8,8,128]{3,2,1,0:T(8,128)} %kappa.3) | copy-start | bytes 294916
  32.5 5.7 %copy-start.4 = (f32[8,8,128]{2,1,0:T(8,128)S(1)}, f32[8,8,128]{2,1,0:T(8,128)}, u32[]{:S(2)}) copy-start(f32[8,8,128]{2,1,0:T(8,128)} %momentum.1) | copy-start | bytes 98308
  32.5 3.8 %collective-permute-start.11 = (f32[24,128]{1,0:T(8,128)S(1)}, f32[24,128]{1,0:T(8,128)S(1)}, u32[]{:S(2)}, u32[]{:S(2)}) collective-permute-start(f32[24,128]{1,0:T(8,128)S(1)} %get-tuple-element.59), channel_id=1, source_target_pairs={{0,1},{1,0},{2,3},{3,2},{4,5},{5,4},{6,7},{7,6},{8,9},{9,8},{10,11... | collective-permute-start | bytes 36872 | tf_op jit(solution)/shard_map/ppermute | solution.py:531
  32.6 5.6 %collective-permute-start.12 = (f32[24,128]{1,0:T(8,128)S(1)}, f32[24,128]{1,0:T(8,128)S(1)}, u32[]{:S(2)}, u32[]{:S(2)}) collective-permute-start(f32[24,128]{1,0:T(8,128)S(1)} %get-tuple-element.60), channel_id=1, source_target_pairs={{1,2},{2,1},{5,6},{6,5},{9,10},{10,9},{13,14},{14,13},{17,18},{18,... | collective-permute-start | bytes 36872 | tf_op jit(solution)/shard_map/ppermute | solution.py:532

commit v3 on v2

--- a/solution.py
+++ b/solution.py
@@ -17,12 +17,37 @@
 
 
 def even_pairs(count):
-    return [(i, i ^ 1) for i in range(count) if (i ^ 1) < count]
+    return [(i, i ^ 1) for i in range(count)]
 
 
 def odd_pairs(count):
-    low = [(i, i + 1) for i in range(1, count - 1, 2)]
+    low = [(i, (i + 1) % count) for i in range(1, count, 2)]
     return low + [(b, a) for a, b in low]
+
+
+def odd_slabs(shots, slabs):
+    pairs = []
+    for shot in range(shots):
+        for slab in range(slabs):
+            if slab == 0 or slab == slabs - 1:
+                other = (shot ^ 1) * slabs + slab
+            else:
+                other = shot * slabs + (slab + 1 if slab % 2 else slab - 1)
+            pairs.append((shot * slabs + slab, other))
+    return pairs
+
+
+def at_border():
+    slab = lax.axis_index("slab")
+    return (slab == 0) | (slab == lax.axis_size("slab") - 1)
+
+
+def ahead(even, border, from_a, from_b):
+    return jnp.where(even, jnp.where(border, 0.0, from_b), from_a)
+
+
+def after(even, border, from_a, from_b):
+    return jnp.where(even, from_a, jnp.where(border, 0.0, from_b))
 
 
 def run_copies(pairs, sems):
@@ -88,7 +113,7 @@
     field[:, PAD + size_x : PAD + size_x + PAD, :] = edge
 
 
-def pack_body(state, velocity, out_a, out_b, sems):
+def pack_body(state, velocity, out_b, out_a, sems):
     depth = velocity.shape[0]
     half = RADIUS // 2
     even = lax.rem(lax.axis_index("slab"), 2) == 0
@@ -129,7 +154,7 @@
 
 def partial_body(
     state, velocity, cells, residuals, kappa,
-    partial_u, image, partial_q, push, out_a, out_b, side_a, side_b, field_u, field_q, grid_now,
+    partial_u, image, partial_q, push, out_b, out_a, side_a, side_b, field_u, field_q, grid_now,
 ):
     depth, size_x, size_y = velocity.shape
     strip = kappa.shape[2]
@@ -200,10 +225,11 @@
     half = RADIUS // 2
     row = k % RADIUS
     even = lax.rem(lax.axis_index("slab"), 2) == 0
+    border = at_border()
     own = lax.rem(lax.axis_index("shot"), 2) == row // half
     at_a = jnp.where(own, share_own[row % half], share_got[row % half])
     at_b = jnp.where(own, share_own[half + row % half], share_got[half + row % half])
-    return jnp.where(even, at_b, at_a) if k < RADIUS else jnp.where(even, at_a, at_b)
+    return (ahead if k < RADIUS else after)(even, border, at_a, at_b)
 
 
 def halo_near(k, depth):
@@ -213,103 +239,121 @@
     return [(r, depth + row - r) for r in range(1, RADIUS + 1) if depth + row - r < depth]
 
 
-def border_body(
-    state, velocity, partial_u, image0, partial_q, first_a, first_b, u_own, image, q_next, u_edge, q_edge
+def own_near(z, depth):
+    near = [(r, RADIUS + z - r) for r in range(1, RADIUS + 1) if z - r < 0]
+    return near + [(r, RADIUS + z + r - depth) for r in range(1, RADIUS + 1) if z + r >= depth]
+
+
+def near_body(
+    state, velocity, partial_u, image0, partial_q, push, first_b, first_a, cells, codes, wavelets,
+    u_part, q_part, image, gain, tap_u, tap_q,
+    u_edge, q_edge, u_now, q_now, cells_here, codes_here, wavelets_here, sems, *, scale,
 ):
-    depth = velocity.shape[0]
-    even = lax.rem(lax.axis_index("slab"), 2) == 0
+    small = run_copies([(cells, cells_here), (codes, codes_here), (wavelets, wavelets_here)], sems)
+    depth, size_x, size_y = velocity.shape
+    here = lax.axis_index("slab")
+    even = lax.rem(here, 2) == 0
+    border = at_border()
+    middle = slice(PAD, PAD + size_x)
+    clear_sides(u_now, size_x)
+    clear_sides(q_now, size_x)
     for k in range(2 * RADIUS):
         row = k % RADIUS
-        one, other = (first_b, first_a) if k < RADIUS else (first_a, first_b)
-        u_edge[k] = jnp.where(even, one[row], other[row])
-        q_edge[k] = jnp.where(even, one[RADIUS + row], other[RADIUS + row])
+        pick = ahead if k < RADIUS else after
+        u_edge[k] = pick(even, border, first_a[row], first_b[row])
+        q_edge[k] = pick(even, border, first_a[RADIUS + row], first_b[RADIUS + row])
+        near = halo_near(k, depth)
+        tap_u[k] = weighted([(r, state[1, 0, 0, own]) for r, own in near])
+        tap_q[k] = weighted([(r, state[1, 0, 1, own]) for r, own in near])
     for z in range(depth):
-        near = [(r, RADIUS + z - r) for r in range(1, RADIUS + 1) if z - r < 0]
-        near += [(r, RADIUS + z + r - depth) for r in range(1, RADIUS + 1) if z + r >= depth]
+        near = own_near(z, depth)
         if not near:
-            u_own[z] = partial_u[z]
-            q_next[z] = partial_q[z]
+            u_now[z, middle, :] = partial_u[z]
+            q_now[z, middle, :] = partial_q[z]
             image[z] = image0[z]
             continue
         v = velocity[z]
         vv = v * v
         change = vv * weighted([(r, u_edge[k]) for r, k in near])
-        u_own[z] = partial_u[z] + change
+        u_now[z, middle, :] = partial_u[z] + change
         image[z] = image0[z] + change * state[1, 0, 1, z]
-        q_next[z] = partial_q[z] + vv * weighted([(r, q_edge[k]) for r, k in near])
-
-def image_body(
-    state, velocity, u_own, image0, q_next, share_own, share_got, second_a, second_b, cells, codes, wavelets,
-    fields, keep, send, speed, u_now, image, u_out, cells_here, codes_here, wavelets_here, sems, out_sem, *, scale,
-):
-    small = run_copies([(cells, cells_here), (codes, codes_here), (wavelets, wavelets_here)], sems)
-    depth, size_x, size_y = velocity.shape
-    whole = depth + 2 * RADIUS
-    half = RADIUS // 2
-    here = lax.axis_index("slab")
-    even = lax.rem(here, 2) == 0
-    core = lax.rem(lax.axis_index("shot"), 2)
-    middle = slice(PAD, PAD + size_x)
-    clear_sides(u_now, size_x)
-    clear_sides(image, size_x)
-    lane = lax.broadcasted_iota(jnp.int32, (size_x, size_y), 1)
-    for z in range(depth):
-        u_now[RADIUS + z, middle, :] = u_own[z]
-    for k in range(2 * RADIUS):
-        row = k % RADIUS
-        one, other = (second_b, second_a) if k < RADIUS else (second_a, second_b)
-        rows = slice(row * size_x, (row + 1) * size_x)
-        before = jnp.where(even, one[rows, :], other[rows, :])
-        v = halo_speed(k, share_own, share_got)
-        speed[k] = v
-        near = halo_near(k, depth)
-        z = k if k < RADIUS else k + depth
-        u_now[z, middle, :] = before + (v * v) * weighted([(r, state[1, 0, 0, own]) for r, own in near])
+        q_now[z, middle, :] = partial_q[z] + vv * weighted([(r, q_edge[k]) for r, k in near])
 
     def first_step(z, x, spot):
-        at = (z, pl.ds(PAD + x, 1), slice(None))
-
-        @pl.when((z >= 0) & (z < whole) & ((z < RADIUS) | (z >= RADIUS + depth)))
-        def _():
-            v = speed[jnp.where(z < RADIUS, z, z - depth), pl.ds(x, 1), :]
-            u_now[at] = u_now[at] + (v * v) * spot
-
-        @pl.when((z >= RADIUS) & (z < RADIUS + depth))
-        def _():
-            v = velocity[z - RADIUS, pl.ds(x, 1), :]
-            u_now[at] = u_now[at] + (v * v) * spot
-
-    for copy in small:
-        copy.wait()
-    sources = (cells_here, codes_here, wavelets_here)
-    point_cells(*sources, 0, here * depth - RADIUS, size_x, size_y, first_step)
-
-    for z in range(depth):
-        v = velocity[z]
-        drive = (v * v) * laplacian_row(u_now, z + RADIUS, whole, size_x, size_y, lane)
-        u_out[z] = (2.0 * u_now[RADIUS + z, middle, :] - state[1, 0, 0, z]) + drive
-        image[z, middle, :] = (-0.2 * (image0[z] + drive * q_next[z])) / (v * scale)
-
-    def image_spot(z, x, change, adjoint):
-        v = velocity[z, pl.ds(x, 1), :]
-        to = (z, pl.ds(PAD + x, 1), slice(None))
-        image[to] = image[to] + (-0.2 * ((v * v) * change * adjoint)) / (v * scale)
-
-    def first_image(z, x, spot):
         @pl.when((z >= 0) & (z < depth))
         def _():
-            image_spot(z, x, spot, state[1, 0, 1, z, pl.ds(x, 1), :])
+            v = velocity[z, pl.ds(x, 1), :]
+            change = (v * v) * spot
+            at = (z, pl.ds(PAD + x, 1), slice(None))
+            u_now[at] = u_now[at] + change
+            at = (z, pl.ds(x, 1), slice(None))
+            image[at] = image[at] + change * state[1, 0, 1, z, pl.ds(x, 1), :]
+
+        before = (z >= -RADIUS) & (z < 0)
+
+        @pl.when(before | ((z >= depth) & (z < depth + RADIUS)))
+        def _():
+            at = (jnp.where(before, z + RADIUS, z + RADIUS - depth), pl.ds(x, 1), slice(None))
+            tap_u[at] = tap_u[at] + spot
 
     def second_step(z, x, spot):
         @pl.when((z >= 0) & (z < depth))
         def _():
             at = (z, pl.ds(x, 1), slice(None))
             v = velocity[at]
-            u_out[at] = u_out[at] + (v * v) * spot
-            image_spot(z, x, spot, q_next[at])
-
-    point_cells(*sources, 0, here * depth, size_x, size_y, first_image)
+            change = (v * v) * spot
+            u_part[at] = u_part[at] + change
+            image[at] = image[at] + (-0.2 * (change * q_now[z, pl.ds(PAD + x, 1), :])) / (v * scale)
+
+    for copy in small:
+        copy.wait()
+    sources = (cells_here, codes_here, wavelets_here)
+    point_cells(*sources, 0, here * depth, size_x, size_y, first_step)
+    lane = lax.broadcasted_iota(jnp.int32, (size_x, size_y), 1)
+    for z in range(depth):
+        v = velocity[z]
+        vv = v * v
+        adjoint = q_now[z, middle, :]
+        drive = vv * laplacian_row(u_now, z, depth, size_x, size_y, lane)
+        u_part[z] = (2.0 * u_now[z, middle, :] - state[1, 0, 0, z]) + drive
+        image[z] = (-0.2 * (image[z] + drive * adjoint)) / (v * scale)
+        gain[z] = (-0.2 / scale) * (v * adjoint)
+        drive = vv * laplacian_row(q_now, z, depth, size_x, size_y, lane) + push[z]
+        q_part[z] = (2.0 * adjoint - state[1, 0, 1, z]) + drive
     point_cells(*sources, 1, here * depth, size_x, size_y, second_step)
+
+
+def halo_field(halo, second_b, second_a, tap, share_own, share_got, which):
+    size_x = halo.shape[1]
+    even = lax.rem(lax.axis_index("slab"), 2) == 0
+    border = at_border()
+    for k in range(2 * RADIUS):
+        row = which * RADIUS + k % RADIUS
+        rows = slice(row * size_x, (row + 1) * size_x)
+        pick = ahead if k < RADIUS else after
+        v = halo_speed(k, share_own, share_got)
+        halo[k] = pick(even, border, second_a[rows, :], second_b[rows, :]) + (v * v) * tap[k]
+
+
+def image_body(
+    velocity, u_part, image_own, gain, tap_u, share_own, share_got, second_b, second_a,
+    fields, keep, send, halo, image, u_out, out_sem,
+):
+    depth, size_x, size_y = velocity.shape
+    core = lax.rem(lax.axis_index("shot"), 2)
+    middle = slice(PAD, PAD + size_x)
+    clear_sides(image, size_x)
+    halo_field(halo, second_b, second_a, tap_u, share_own, share_got, 0)
+    for z in range(depth):
+        near = own_near(z, depth)
+        if not near:
+            u_out[z] = u_part[z]
+            image[z, middle, :] = image_own[z]
+            continue
+        v = velocity[z]
+        crossing = weighted([(r, halo[k]) for r, k in near])
+        u_out[z] = u_part[z] + (v * v) * crossing
+        image[z, middle, :] = image_own[z] + gain[z] * crossing
     copy_out = pltpu.make_async_copy(u_out, fields.at[0, 0], out_sem)
     copy_out.start()
     chip = lax.div(lax.axis_index("shot"), 2)
@@ -333,7 +377,7 @@
 
 
 def strip_sum_body(*refs, count, wide):
-    parts, (total, edge_a, edge_b) = refs[:count], refs[count:]
+    parts, (total, edge_b, edge_a) = refs[:count], refs[count:]
     added = parts[0][...]
     for part in parts[1:]:
         added = added + part[...]
@@ -347,60 +391,52 @@
 
 
 def adjoint_body(
-    fields_in, state, velocity, q_next, push, second_a, second_b, share_own, share_got, fields, field, q_out, out_sem
+    fields_in, velocity, q_part, tap_q, share_own, share_got, second_b, second_a, fields, halo, q_out, out_sem
 ):
-    depth, size_x, size_y = velocity.shape
-    whole = depth + 2 * RADIUS
-    even = lax.rem(lax.axis_index("slab"), 2) == 0
-    middle = slice(PAD, PAD + size_x)
-    clear_sides(field, size_x)
+    depth = velocity.shape[0]
+    halo_field(halo, second_b, second_a, tap_q, share_own, share_got, 1)
     for z in range(depth):
-        field[RADIUS + z, middle, :] = q_next[z]
-    for k in range(2 * RADIUS):
-        row = k % RADIUS
-        one, other = (second_b, second_a) if k < RADIUS else (second_a, second_b)
-        rows = slice((RADIUS + row) * size_x, (RADIUS + row + 1) * size_x)
-        before = jnp.where(even, one[rows, :], other[rows, :])
-        v = halo_speed(k, share_own, share_got)
-        z = k if k < RADIUS else k + depth
-        near = halo_near(k, depth)
-        field[z, middle, :] = before + (v * v) * weighted([(r, state[1, 0, 1, own]) for r, own in near])
-    lane = lax.broadcasted_iota(jnp.int32, (size_x, size_y), 1)
-    for z in range(depth):
+        near = own_near(z, depth)
         v = velocity[z]
-        drive = (v * v) * laplacian_row(field, z + RADIUS, whole, size_x, size_y, lane) + push[z]
-        q_out[z] = (2.0 * q_next[z] - state[1, 0, 1, z]) + drive
+        q_out[z] = q_part[z] + (v * v) * weighted([(r, halo[k]) for r, k in near]) if near else q_part[z]
     copy = pltpu.make_async_copy(q_out, fields.at[0, 1], out_sem)
     copy.start()
     copy.wait()
 
 
-def smooth_body(
-    total, got_a, got_b, kappa, second_a, second_b, side_a, side_b, velocity, momentum, new_momentum, new_speed, grad, half, coef,
-    *, size_x
-):
+def coefficient_body(kappa, second_b, second_a, side_a, side_b, coef, *, size_x):
+    _, depth, strip, _ = kappa.shape
+    even = lax.rem(lax.axis_index("slab"), 2) == 0
+    border = at_border()
+    shot = lax.axis_index("shot")
+    even_strip = lax.rem(shot, 2) == 0
+    end_strip = (shot == 0) | (shot == lax.axis_size("shot") - 1)
+    coef[...] = jnp.zeros(coef.shape, F32)
+    for j in range(3):
+        at = slice(2 * RADIUS * size_x + j * strip, 2 * RADIUS * size_x + (j + 1) * strip)
+        coef[j, 0, 1 : strip + 1, :] = ahead(even, border, second_a[at, :], second_b[at, :])
+        coef[j, depth + 1, 1 : strip + 1, :] = after(even, border, second_a[at, :], second_b[at, :])
+        of = slice(j * depth, (j + 1) * depth)
+        left = ahead(even_strip, end_strip, side_a[of, :], side_b[of, :])
+        right = after(even_strip, end_strip, side_a[of, :], side_b[of, :])
+        for z in range(depth):
+            coef[j, z + 1, 1 : strip + 1, :] = kappa[j, z]
+            coef[j, z + 1, 0:1, :] = left[z : z + 1, :]
+            coef[j, z + 1, strip + 1 : strip + 2, :] = right[z : z + 1, :]
+
+
+def smooth_body(total, got_a, got_b, kappa, coef, velocity, momentum, new_momentum, new_speed, grad, half):
     depth, strip, size_y = momentum.shape
     column = lax.axis_index("shot") * strip
     wide = strip + 4
     even = lax.rem(lax.axis_index("slab"), 2) == 0
-    even_strip = lax.rem(lax.axis_index("shot"), 2) == 0
+    border = at_border()
     for k in range(2):
         at = slice(k * wide, (k + 1) * wide)
-        grad[k, 0:wide, :] = jnp.where(even, got_b[at, :], got_a[at, :])
-        grad[depth + 2 + k, 0:wide, :] = jnp.where(even, got_a[at, :], got_b[at, :])
+        grad[k, 0:wide, :] = ahead(even, border, got_a[at, :], got_b[at, :])
+        grad[depth + 2 + k, 0:wide, :] = after(even, border, got_a[at, :], got_b[at, :])
     for z in range(depth):
         grad[z + 2, 0:wide, :] = total[z * wide : (z + 1) * wide, :]
-    coef[...] = jnp.zeros(coef.shape, F32)
-    for j in range(3):
-        at = slice(2 * RADIUS * size_x + j * strip, 2 * RADIUS * size_x + (j + 1) * strip)
-        coef[j, 0, 1 : strip + 1, :] = jnp.where(even, second_b[at, :], second_a[at, :])
-        coef[j, depth + 1, 1 : strip + 1, :] = jnp.where(even, second_a[at, :], second_b[at, :])
-        left = jnp.where(even_strip, side_b[j * depth : (j + 1) * depth, :], side_a[j * depth : (j + 1) * depth, :])
-        right = jnp.where(even_strip, side_a[j * depth : (j + 1) * depth, :], side_b[j * depth : (j + 1) * depth, :])
-        for z in range(depth):
-            coef[j, z + 1, 1 : strip + 1, :] = kappa[j, z]
-            coef[j, z + 1, 0:1, :] = left[z : z + 1, :]
-            coef[j, z + 1, strip + 1 : strip + 2, :] = right[z : z + 1, :]
 
     def step(source, z, rows, factors):
         centre = source[z, 1 : 1 + rows, :]
@@ -439,24 +475,24 @@
     slabs = lax.axis_size("slab")
     shots = lax.axis_size("shot")
     chips = shots // 2
-    z_even, z_odd = even_pairs(slabs), odd_pairs(slabs)
+    z_even, z_odd = even_pairs(slabs), odd_slabs(shots, slabs)
+    both = ("shot", "slab")
     cube = (depth, size_x, size_y)
     padded = (depth, size_x + 2 * PAD, size_y)
-    whole = depth + 2 * RADIUS
     dma = pltpu.SemaphoreType.DMA
 
     half = RADIUS // 2
     block = shape(2 * RADIUS + half, size_x, size_y)
-    out_a, out_b = call(
+    out_b, out_a = call(
         pack_body, [block] * 2, tuple(pltpu.with_memory_space_constraint(x, pltpu.HBM) for x in (wave_state, velocity)), ["hbm"] * 2, ["vmem"] * 2, [dma((2 * (2 * RADIUS + half),))], us=1.3
     )
+    first_b = lax.ppermute(out_b, both, z_odd)
     first_a = lax.ppermute(out_a, "slab", z_even)
-    first_b = lax.ppermute(out_b, "slab", z_odd)
 
     flat = shape(2 * RADIUS * size_x + 3 * strip, size_y)
     side = shape(3 * depth, size_y)
     edge = shape(RADIUS, size_x, size_y)
-    partial_u, image0, partial_q, push, out_a, out_b, side_a, side_b = call(
+    partial_u, image0, partial_q, push, out_b, out_a, side_a, side_b = call(
         partial_body,
         [shape(*cube)] * 4 + [flat, flat, side, side],
         (wave_state, velocity, receiver_cells, residuals, diffusivity),
@@ -465,84 +501,85 @@
         [pltpu.VMEM(padded, F32)] * 2 + [pltpu.VMEM((STEPS, depth * size_x, size_y), F32)],
         us=1.7,
     )
+    second_b = lax.ppermute(out_b, both, z_odd)
     second_a = lax.ppermute(out_a, "slab", z_even)
-    second_b = lax.ppermute(out_b, "slab", z_odd)
     side_a = lax.ppermute(side_a, "shot", even_pairs(shots))
     side_b = lax.ppermute(side_b, "shot", odd_pairs(shots))
 
     first_a, first_b, side_a, side_b = lax.optimization_barrier((first_a, first_b, side_a, side_b))
     (share_own,) = call(share_body, [edge], (first_a, first_b), ["vmem"] * 2, ["vmem"])
     share_got = lax.ppermute(share_own, "shot", even_pairs(shots))
-    u_own, image0, q_next = call(
-        border_body,
-        [shape(*cube)] * 3,
-        (wave_state, velocity, partial_u, image0, partial_q, first_a, first_b),
-        ["vmem"] * 7,
-        ["vmem"] * 3,
-        [pltpu.VMEM((2 * RADIUS, size_x, size_y), F32)] * 2,
-        us=0.3,
-    )
-
+    ring = shape(2 * RADIUS, size_x, size_y)
+    ring_scratch = pltpu.VMEM(ring.shape, F32)
     small = (source_cells, source_codes, wavelets.T)
+    u_part, q_part, image_own, gain, tap_u, tap_q = call(
+        functools.partial(near_body, scale=math.sqrt(shots * STEPS)),
+        [shape(*cube)] * 4 + [ring, ring],
+        (wave_state, velocity, partial_u, image0, partial_q, push, first_b, first_a)
+        + tuple(pltpu.with_memory_space_constraint(x, pltpu.HBM) for x in small),
+        ["vmem"] * 8 + ["hbm"] * 3,
+        ["vmem"] * 6,
+        [ring_scratch] * 2
+        + [pltpu.VMEM(padded, F32)] * 2
+        + [pltpu.SMEM(x.shape, x.dtype) for x in small]
+        + [dma((3,))],
+        us=2.3,
+    )
+
     part = shape(chips, depth * wide, size_y)
     fields, keep, send = call(
-        functools.partial(image_body, scale=math.sqrt(shots * STEPS)),
+        image_body,
         [shape(1, 2, *cube), part, part],
-        (wave_state, velocity, u_own, image0, q_next, share_own, share_got, second_a, second_b)
-        + tuple(pltpu.with_memory_space_constraint(x, pltpu.HBM) for x in small),
-        ["vmem"] * 9 + ["hbm"] * 3,
+        (velocity, u_part, image_own, gain, tap_u, share_own, share_got, second_b, second_a),
+        ["vmem"] * 9,
         ["any"] + ["vmem"] * 2,
-        [
-            pltpu.VMEM((2 * RADIUS, size_x, size_y), F32),
-            pltpu.VMEM((whole, size_x + 2 * PAD, size_y), F32),
-            pltpu.VMEM(padded, F32),
-            pltpu.VMEM(cube, F32),
-        ]
-        + [pltpu.SMEM(x.shape, x.dtype) for x in small]
-        + [dma((3,)), dma],
-        us=2.3,
+        [ring_scratch, pltpu.VMEM(padded, F32), pltpu.VMEM(cube, F32), dma],
+        us=1.0,
     )
     got = lax.ppermute(send, "shot", even_pairs(shots))
     (fields,) = call(
         adjoint_body,
         [shape(1, 2, *cube)],
-        (fields, wave_state, velocity, q_next, push, second_a, second_b, share_own, share_got),
-        ["any"] + ["vmem"] * 8,
+        (fields, velocity, q_part, tap_q, share_own, share_got, second_b, second_a),
+        ["any"] + ["vmem"] * 7,
         ["any"],
-        [pltpu.VMEM((whole, size_x + 2 * PAD, size_y), F32), pltpu.VMEM(cube, F32), dma],
+        [ring_scratch, pltpu.VMEM(cube, F32), dma],
         aliases={0: 0},
-        us=1.4,
-    )
-    got, fields = lax.optimization_barrier((got, fields))
+        us=0.7,
+    )
+    tall = 8 * ((wide + 7) // 8)
+    (coef,) = call(
+        functools.partial(coefficient_body, size_x=size_x),
+        [shape(3, depth + 2, tall, size_y)],
+        (diffusivity, second_b, second_a, side_a, side_b),
+        ["vmem"] * 5,
+        ["vmem"],
+        us=0.3,
+    )
+    got, fields, coef = lax.optimization_barrier((got, fields, coef))
     row_block = shape(depth * wide, size_y)
     parts = call(pair_sum_body, [row_block] * chips, (keep, got), ["vmem"] * 2, ["vmem"] * chips)
     arrived = [
-        parts[0] if k == 0 else lax.ppermute(parts[k], "shot", [(i, i ^ (2 * k)) for i in range(shots)])
-        for k in range(chips)
-    ]
+        lax.ppermute(parts[k], "shot", [(i, i ^ (2 * k)) for i in range(shots)]) for k in reversed(range(1, chips))
+    ] + [parts[0]]
     two = shape(2 * wide, size_y)
-    total, out_a, out_b = call(
+    total, out_b, out_a = call(
         functools.partial(strip_sum_body, count=chips, wide=wide),
         [row_block, two, two],
         arrived,
         ["vmem"] * chips,
         ["vmem"] * 3,
     )
+    grad_b = lax.ppermute(out_b, both, z_odd)
     grad_a = lax.ppermute(out_a, "slab", z_even)
-    grad_b = lax.ppermute(out_b, "slab", z_odd)
-    tall = 8 * ((wide + 7) // 8)
     new_momentum, new_velocity = call(
-        functools.partial(smooth_body, size_x=size_x),
+        smooth_body,
         [shape(*momentum.shape)] * 2,
-        (total, grad_a, grad_b, diffusivity, second_a, second_b, side_a, side_b, velocity, momentum),
-        ["vmem"] * 10,
+        (total, grad_a, grad_b, diffusivity, coef, velocity, momentum),
+        ["vmem"] * 7,
         ["block"] * 2,
-        [
-            pltpu.VMEM((depth + 4, tall, size_y), F32),
-            pltpu.VMEM((depth + 2, tall, size_y), F32),
-            pltpu.VMEM((3, depth + 2, tall, size_y), F32),
-        ],
-        us=0.9,
+        [pltpu.VMEM((depth + 4, tall, size_y), F32), pltpu.VMEM((depth + 2, tall, size_y), F32)],
+        us=0.7,
     )
     return (fields, new_momentum, new_velocity)
 

time: 39.3 us -> 34 us (0.87)
  the two profiles are of different devices: /device:TPU:16 before, /device:TPU:0 now
where the time goes in v3:
time: 34 us; the launch traced here: 33.8 us
  starting transfers between devices  15.1 us (44%)
  waiting for transfers between devices  9.43 us (28%)
  Pallas kernels  7.58 us (22%)
  local copies, waits for them, and re-layouts  0.92 us (3%)
  between operations  0.79 us (2%)
    pallas_call x10, Pallas kernels, call(): pl.pallas_call(body, out_shape=list(out_shapes), in_specs=[SPECS[s] for s...  7.58 us
    ppermute x3, waiting for transfers between devices, on_device(): lax.ppermute(parts[k], 'shot', [(i, i ^ 2 * k) for i in range(shots)])  3.78 us
    ppermute x3, starting transfers between devices, on_device(): lax.ppermute(parts[k], 'shot', [(i, i ^ 2 * k) for i in range(shots)])  3.55 us
    ppermute x1, starting transfers between devices, on_device(): first_a = lax.ppermute(out_a, 'slab', z_even)  3.09 us
    ppermute x1, starting transfers between devices, on_device(): grad_a = lax.ppermute(out_a, 'slab', z_even)  2.78 us
    ppermute x1, starting transfers between devices, on_device(): second_a = lax.ppermute(out_a, 'slab', z_even)  2.72 us
    ppermute x1, starting transfers between devices, on_device(): side_b = lax.ppermute(side_b, 'shot', odd_pairs(shots))  2.22 us
    ppermute x1, waiting for transfers between devices, on_device(): side_b = lax.ppermute(side_b, 'shot', odd_pairs(shots))  1.8 us
  transfers between devices with their start and end apart: 13, of which 8 were waited for; matrix products, arithmetic and copies ran while one was open for 0% of the time, Pallas kernels for 13%

profile of v3, /device:TPU:0, one launch (start us, length us, event | category | flops | bytes accessed | tf_op | source)
XLA Modules:
  0.0 33.8 jit_solution(2007613463128427211)
XLA Ops:
  0.6 1.3 %shard_map.113 = (f32[10,64,128]{2,1,0:T(8,128)S(1)}, f32[10,64,128]{2,1,0:T(8,128)S(1)}) custom-call(f32[2,1,2,8,64,128]{5,4,3,2,1,0:T(8,128)} %state.5, f32[8,64,128]{2,1,0:T(8,128)} %velocity.11), custom_call_target="tpu_custom_call" | custom-call | bytes 4797000 | tf_op jit(solution)/shard_map/pallas_call | solution.py:69
  2.0 3.1 %collective-permute-start = (f32[10,64,128]{2,1,0:T(8,128)S(1)}, f32[10,64,128]{2,1,0:T(8,128)S(1)}, u32[]{:S(2)}, u32[]{:S(2)}) collective-permute-start(f32[10,64,128]{2,1,0:T(8,128)S(1)} %get-tuple-element.42), channel_id=1, source_target_pairs={{0,1},{1,0},{2,3},{3,2},{4,5},{5,4},{6,7},{7,6},{8,9},{9,8},{10,11... | collective-permute-start | bytes 983048 | tf_op jit(solution)/shard_map/ppermute | solution.py:490
  5.1 0.9 %copy-done.2 = f32[3,8,8,128]{3,2,1,0:T(8,128)S(1)} copy-done((f32[3,8,8,128]{3,2,1,0:T(8,128)S(1)}, f32[3,8,8,128]{3,2,1,0:T(8,128)}, u32[]{:S(2)}) %copy-start.2) | copy-done | bytes 98328
  6.0 1.5 %shard_map.112 = (f32[8,64,128]{2,1,0:T(8,128)S(1)}, f32[8,64,128]{2,1,0:T(8,128)S(1)}, f32[8,64,128]{2,1,0:T(8,128)S(1)}, f32[8,64,128]{2,1,0:T(8,128)S(1)}, f3...) custom-call(f32[2,1,2,8,64,128]{5,4,3,2,1,0:T(8,128)S(1)} %copy-done, ...), custom_call_target="tpu_custom_call" | custom-call | bytes 6273000 | tf_op jit(solution)/shard_map/pallas_call | solution.py:69
  7.5 0.6 %collective-permute-start.5 = (f32[536,128]{1,0:T(8,128)S(1)}, f32[536,128]{1,0:T(8,128)S(1)}, u32[]{:S(2)}, u32[]{:S(2)}) collective-permute-start(f32[536,128]{1,0:T(8,128)S(1)} %get-tuple-element.52), channel_id=1, source_target_pairs={{0,4},{1,2},{2,1},{3,7},{4,0},{5,6},{6,5},{7,3},{8,12},{9,10},{10,... | collective-permute-start | bytes 823304 | tf_op jit(solution)/shard_map/ppermute | solution.py:504
  8.1 2.7 %collective-permute-start.6 = (f32[536,128]{1,0:T(8,128)S(1)}, f32[536,128]{1,0:T(8,128)S(1)}, u32[]{:S(2)}, u32[]{:S(2)}) collective-permute-start(f32[536,128]{1,0:T(8,128)S(1)} %get-tuple-element.53), channel_id=1, source_target_pairs={{0,1},{1,0},{2,3},{3,2},{4,5},{5,4},{6,7},{7,6},{8,9},{9,8},{10,11... | collective-permute-start | bytes 823304 | tf_op jit(solution)/shard_map/ppermute | solution.py:505
  10.8 1.2 %collective-permute-done.2.side_a = f32[24,128]{1,0:T(8,128)S(1)} collective-permute-done((f32[24,128]{1,0:T(8,128)S(1)}, f32[24,128]{1,0:T(8,128)S(1)}, u32[]{:S(2)}, u32[]{:S(2)}) %collective-permute-start.2) | collective-permute-done | bytes 12320 | tf_op jit(solution)/shard_map/ppermute | solution.py:506
  12.0 2.2 %collective-permute-start.3 = (f32[24,128]{1,0:T(8,128)S(1)}, f32[24,128]{1,0:T(8,128)S(1)}, u32[]{:S(2)}, u32[]{:S(2)}) collective-permute-start(f32[24,128]{1,0:T(8,128)S(1)} %get-tuple-element.45), channel_id=1, source_target_pairs={{4,8},{12,16},{20,24},{28,0},{8,4},{16,12},{24,20},{0,28},{5,9},{1... | collective-permute-start | bytes 36872 | tf_op jit(solution)/shard_map/ppermute | solution.py:507
  14.2 1.8 %collective-permute-done.3.side_b = f32[24,128]{1,0:T(8,128)S(1)} collective-permute-done((f32[24,128]{1,0:T(8,128)S(1)}, f32[24,128]{1,0:T(8,128)S(1)}, u32[]{:S(2)}, u32[]{:S(2)}) %collective-permute-start.3) | collective-permute-done | bytes 12320 | tf_op jit(solution)/shard_map/ppermute | solution.py:507
  16.1 2.1 %shard_map.114 = (f32[8,64,128]{2,1,0:T(8,128)S(1)}, f32[8,64,128]{2,1,0:T(8,128)S(1)}, f32[8,64,128]{2,1,0:T(8,128)S(1)}, f32[8,64,128]{2,1,0:T(8,128)S(1)}, f3...) custom-call(f32[2,1,2,8,64,128]{5,4,3,2,1,0:T(8,128)S(1)} %copy-done, f32[8,64,128]{2,1,0:T(8,128)S(1)} %copy-done.1, ...), custom_call_target="tpu_custom_call" | custom-call | bytes 8487000 | tf_op jit(solution)/shard_map/pallas_call | solution.py:69
  18.2 0.5 %collective-permute-done.6.second_a = f32[536,128]{1,0:T(8,128)S(1)} collective-permute-done((f32[536,128]{1,0:T(8,128)S(1)}, f32[536,128]{1,0:T(8,128)S(1)}, u32[]{:S(2)}, u32[]{:S(2)}) %collective-permute-start.6) | collective-permute-done | bytes 274464 | tf_op jit(solution)/shard_map/ppermute | solution.py:505
  18.7 0.9 %shard_map.116 = (f32[1,2,8,64,128]{4,3,2,1,0:T(8,128)}, f32[4,96,128]{2,1,0:T(8,128)S(1)}, f32[4,96,128]{2,1,0:T(8,128)S(1)}) custom-call(f32[8,64,128]{2,1,0:T(8,128)S(1)} %copy-done.1, f32[8,64,128]{2,1,0:T(8,128)S(1)} %get-tuple-element.48.u_part, f32[8,64,128]{2,1,0:T(8,128)S(1)} %get-tuple-element.49.image_own, ...), custom_call_target="tpu_custom_call" | custom-call | bytes 3690000 | tf_op jit(solution)/shard_map/pallas_call | solution.py:69
  19.6 0.1 collective-permute-start.7
  19.7 0.9 %shard_map.117 = f32[1,2,8,64,128]{4,3,2,1,0:T(8,128)} custom-call(f32[1,2,8,64,128]{4,3,2,1,0:T(8,128)} %get-tuple-element.55.fields_in, f32[8,64,128]{2,1,0:T(8,128)S(1)} %copy-done.1, f32[8,64,128]{2,1,0:T(8,128)S(1)} %get-tuple-element.56.q_part, f32[8,64,128]{2,1,0:T(8,128)S(1)} %get-tuple-element.57.tap_q, ...), custom_call_target="tpu_custom_call", output_to_operand_aliasing={{}: (0, {})} | custom-call | bytes 2583000 | tf_op jit(solution)/shard_map/pallas_call | solution.py:69
  20.6 0.5 %collective-permute-done.7.got = f32[4,96,128]{2,1,0:T(8,128)S(1)} collective-permute-done((f32[4,96,128]{2,1,0:T(8,128)S(1)}, f32[4,96,128]{2,1,0:T(8,128)S(1)}, u32[]{:S(2)}, u32[]{:S(2)}) %collective-permute-start.7) | collective-permute-done | bytes 196640 | tf_op jit(solution)/shard_map/ppermute | solution.py:539
  21.1 1.7 %collective-permute-start.10 = (f32[96,128]{1,0:T(8,128)S(1)}, f32[96,128]{1,0:T(8,128)S(1)}, u32[]{:S(2)}, u32[]{:S(2)}) collective-permute-start(f32[96,128]{1,0:T(8,128)S(1)} %get-tuple-element.65), channel_id=1, source_target_pairs={{0,8},{4,12},{8,0},{12,4},{16,24},{20,28},{24,16},{28,20},{1,9},{5... | collective-permute-start | bytes 147464 | tf_op jit(solution)/shard_map/ppermute | solution.py:563
  22.9 1.5 %collective-permute-start.8 = (f32[96,128]{1,0:T(8,128)S(1)}, f32[96,128]{1,0:T(8,128)S(1)}, u32[]{:S(2)}, u32[]{:S(2)}) collective-permute-start(f32[96,128]{1,0:T(8,128)S(1)} %get-tuple-element.63), channel_id=1, source_target_pairs={{0,24},{4,28},{8,16},{12,20},{16,8},{20,12},{24,0},{28,4},{1,25},{... | collective-permute-start | bytes 147464 | tf_op jit(solution)/shard_map/ppermute | solution.py:563
  24.3 0.3 %collective-permute-start.9 = (f32[96,128]{1,0:T(8,128)S(1)}, f32[96,128]{1,0:T(8,128)S(1)}, u32[]{:S(2)}, u32[]{:S(2)}) collective-permute-start(f32[96,128]{1,0:T(8,128)S(1)} %get-tuple-element.64), channel_id=1, source_target_pairs={{0,16},{4,20},{8,24},{12,28},{16,0},{20,4},{24,8},{28,12},{1,17},{... | collective-permute-start | bytes 147464 | tf_op jit(solution)/shard_map/ppermute | solution.py:563
  24.7 0.6 %collective-permute-done.10.refs_2_ = f32[96,128]{1,0:T(8,128)S(1)} collective-permute-done((f32[96,128]{1,0:T(8,128)S(1)}, f32[96,128]{1,0:T(8,128)S(1)}, u32[]{:S(2)}, u32[]{:S(2)}) %collective-permute-start.10) | collective-permute-done | bytes 49184 | tf_op jit(solution)/shard_map/ppermute | solution.py:563
  25.3 2.6 %collective-permute-done.8.refs_0_ = f32[96,128]{1,0:T(8,128)S(1)} collective-permute-done((f32[96,128]{1,0:T(8,128)S(1)}, f32[96,128]{1,0:T(8,128)S(1)}, u32[]{:S(2)}, u32[]{:S(2)}) %collective-permute-start.8) | collective-permute-done | bytes 49184 | tf_op jit(solution)/shard_map/ppermute | solution.py:563
  27.9 0.6 %collective-permute-done.9.refs_1_ = f32[96,128]{1,0:T(8,128)S(1)} collective-permute-done((f32[96,128]{1,0:T(8,128)S(1)}, f32[96,128]{1,0:T(8,128)S(1)}, u32[]{:S(2)}, u32[]{:S(2)}) %collective-permute-start.9) | collective-permute-done | bytes 49184 | tf_op jit(solution)/shard_map/ppermute | solution.py:563
  28.5 2.8 %collective-permute-start.11 = (f32[24,128]{1,0:T(8,128)S(1)}, f32[24,128]{1,0:T(8,128)S(1)}, u32[]{:S(2)}, u32[]{:S(2)}) collective-permute-start(f32[24,128]{1,0:T(8,128)S(1)} %get-tuple-element.68), channel_id=1, source_target_pairs={{0,1},{1,0},{2,3},{3,2},{4,5},{5,4},{6,7},{7,6},{8,9},{9,8},{10,11... | collective-permute-start | bytes 36872 | tf_op jit(solution)/shard_map/ppermute | solution.py:574
  31.3 1.7 %collective-permute-done.11.got_a = f32[24,128]{1,0:T(8,128)S(1)} collective-permute-done((f32[24,128]{1,0:T(8,128)S(1)}, f32[24,128]{1,0:T(8,128)S(1)}, u32[]{:S(2)}, u32[]{:S(2)}) %collective-permute-start.11) | collective-permute-done | bytes 12320 | tf_op jit(solution)/shard_map/ppermute | solution.py:574
  33.0 0.8 %shard_map.121 = (f32[8,8,128]{2,1,0:T(8,128)}, f32[8,8,128]{2,1,0:T(8,128)}) custom-call(f32[96,128]{1,0:T(8,128)S(1)} %get-tuple-element.67.total, f32[24,128]{1,0:T(8,128)S(1)} %collective-permute-done.11.got_a, f32[24,128]{1,0:T(8,128)S(1)} %collective-permute-done.12.got_b, f32[3,8,8,128]{3,2,1,0:T(8,128)S(1)} %copy-done.3, ...), custom_call_target="tpu_custom_call" | custom-call | bytes 2583000 | tf_op jit(solution)/shard_map/pallas_call | solution.py:69
  (26 shorter events, 0.2 us)
Async XLA Ops:
  0.6 4.5 %copy-start = (f32[2,1,2,8,64,128]{5,4,3,2,1,0:T(8,128)S(1)}, f32[2,1,2,8,64,128]{5,4,3,2,1,0:T(8,128)}, u32[]{:S(2)}) copy-start(f32[2,1,2,8,64,128]{5,4,3,2,1,0:T(8,128)} %state.5) | copy-start | bytes 3145732
  0.6 4.5 %copy-start.1 = (f32[8,64,128]{2,1,0:T(8,128)S(1)}, f32[8,64,128]{2,1,0:T(8,128)}, u32[]{:S(2)}) copy-start(f32[8,64,128]{2,1,0:T(8,128)} %velocity.11) | copy-start | bytes 786436
  2.0 3.1 %copy-start.5 = (f32[1,2,256]{2,1,0:T(2,128)S(1)}, f32[1,2,256]{2,1,0:T(2,128)}, u32[]{:S(2)}) copy-start(f32[1,2,256]{2,1,0:T(2,128)} %residuals.1) | copy-start | bytes 6148
  2.0 3.1 %copy-start.6 = (s32[1,256]{1,0:T(1,128)S(1)}, s32[1,256]{1,0:T(1,128)}, u32[]{:S(2)}) copy-start(s32[1,256]{1,0:T(1,128)} %cells.2) | copy-start | bytes 3076
  2.0 14.0 %collective-permute-start = (f32[10,64,128]{2,1,0:T(8,128)S(1)}, f32[10,64,128]{2,1,0:T(8,128)S(1)}, u32[]{:S(2)}, u32[]{:S(2)}) collective-permute-start(f32[10,64,128]{2,1,0:T(8,128)S(1)} %get-tuple-element.42), channel_id=1, source_target_pairs={{0,1},{1,0},{2,3},{3,2},{4,5},{5,4},{6,7},{7,6},{8,9},{9,8},{10,11... | collective-permute-start | bytes 983048 | tf_op jit(solution)/shard_map/ppermute | solution.py:490
  5.1 10.9 %collective-permute-start.1 = (f32[10,64,128]{2,1,0:T(8,128)S(1)}, f32[10,64,128]{2,1,0:T(8,128)S(1)}, u32[]{:S(2)}, u32[]{:S(2)}) collective-permute-start(f32[10,64,128]{2,1,0:T(8,128)S(1)} %get-tuple-element.43), channel_id=1, source_target_pairs={{0,4},{1,2},{2,1},{3,7},{4,0},{5,6},{6,5},{7,3},{8,12},{9,10},{10,... | collective-permute-start | bytes 983048 | tf_op jit(solution)/shard_map/ppermute | solution.py:489
  5.1 0.9 %copy-start.2 = (f32[3,8,8,128]{3,2,1,0:T(8,128)S(1)}, f32[3,8,8,128]{3,2,1,0:T(8,128)}, u32[]{:S(2)}) copy-start(f32[3,8,8,128]{3,2,1,0:T(8,128)} %kappa.5) | copy-start | bytes 294916
  7.5 10.6 %collective-permute-start.5 = (f32[536,128]{1,0:T(8,128)S(1)}, f32[536,128]{1,0:T(8,128)S(1)}, u32[]{:S(2)}, u32[]{:S(2)}) collective-permute-start(f32[536,128]{1,0:T(8,128)S(1)} %get-tuple-element.52), channel_id=1, source_target_pairs={{0,4},{1,2},{2,1},{3,7},{4,0},{5,6},{6,5},{7,3},{8,12},{9,10},{10,... | collective-permute-start | bytes 823304 | tf_op jit(solution)/shard_map/ppermute | solution.py:504
  8.1 10.6 %collective-permute-start.6 = (f32[536,128]{1,0:T(8,128)S(1)}, f32[536,128]{1,0:T(8,128)S(1)}, u32[]{:S(2)}, u32[]{:S(2)}) collective-permute-start(f32[536,128]{1,0:T(8,128)S(1)} %get-tuple-element.53), channel_id=1, source_target_pairs={{0,1},{1,0},{2,3},{3,2},{4,5},{5,4},{6,7},{7,6},{8,9},{9,8},{10,11... | collective-permute-start | bytes 823304 | tf_op jit(solution)/shard_map/ppermute | solution.py:505
  10.8 1.2 %collective-permute-start.2 = (f32[24,128]{1,0:T(8,128)S(1)}, f32[24,128]{1,0:T(8,128)S(1)}, u32[]{:S(2)}, u32[]{:S(2)}) collective-permute-start(f32[24,128]{1,0:T(8,128)S(1)} %get-tuple-element.44), channel_id=1, source_target_pairs={{0,4},{4,0},{8,12},{12,8},{16,20},{20,16},{24,28},{28,24},{1,5},{5... | collective-permute-start | bytes 36872 | tf_op jit(solution)/shard_map/ppermute | solution.py:506
  12.0 4.0 %collective-permute-start.3 = (f32[24,128]{1,0:T(8,128)S(1)}, f32[24,128]{1,0:T(8,128)S(1)}, u32[]{:S(2)}, u32[]{:S(2)}) collective-permute-start(f32[24,128]{1,0:T(8,128)S(1)} %get-tuple-element.45), channel_id=1, source_target_pairs={{4,8},{12,16},{20,24},{28,0},{8,4},{16,12},{24,20},{0,28},{5,9},{1... | collective-permute-start | bytes 36872 | tf_op jit(solution)/shard_map/ppermute | solution.py:507
  16.0 2.7 %collective-permute-start.4 = (f32[4,64,128]{2,1,0:T(8,128)S(1)}, f32[4,64,128]{2,1,0:T(8,128)S(1)}, u32[]{:S(2)}, u32[]{:S(2)}) collective-permute-start(f32[4,64,128]{2,1,0:T(8,128)S(1)} %shard_map.115.share_own), channel_id=1, source_target_pairs={{0,4},{4,0},{8,12},{12,8},{16,20},{20,16},{24,28},{28,24},{1,5},{5... | collective-permute-start | bytes 393224 | tf_op jit(solution)/shard_map/ppermute | solution.py:511
  18.7 1.0 %copy-start.3 = (f32[3,8,8,128]{3,2,1,0:T(8,128)S(1)}, f32[3,8,8,128]{3,2,1,0:T(8,128)}, u32[]{:S(2)}) copy-start(f32[3,8,8,128]{3,2,1,0:T(8,128)} %kappa.5) | copy-start | bytes 294916
  19.6 1.5 %collective-permute-start.7 = (f32[4,96,128]{2,1,0:T(8,128)S(1)}, f32[4,96,128]{2,1,0:T(8,128)S(1)}, u32[]{:S(2)}, u32[]{:S(2)}) collective-permute-start(f32[4,96,128]{2,1,0:T(8,128)S(1)} %get-tuple-element.54), channel_id=1, source_target_pairs={{0,4},{4,0},{8,12},{12,8},{16,20},{20,16},{24,28},{28,24},{1,5},{5... | collective-permute-start | bytes 589832 | tf_op jit(solution)/shard_map/ppermute | solution.py:539
  21.1 4.2 %collective-permute-start.10 = (f32[96,128]{1,0:T(8,128)S(1)}, f32[96,128]{1,0:T(8,128)S(1)}, u32[]{:S(2)}, u32[]{:S(2)}) collective-permute-start(f32[96,128]{1,0:T(8,128)S(1)} %get-tuple-element.65), channel_id=1, source_target_pairs={{0,8},{4,12},{8,0},{12,4},{16,24},{20,28},{24,16},{28,20},{1,9},{5... | collective-permute-start | bytes 147464 | tf_op jit(solution)/shard_map/ppermute | solution.py:563
  22.9 5.0 %collective-permute-start.8 = (f32[96,128]{1,0:T(8,128)S(1)}, f32[96,128]{1,0:T(8,128)S(1)}, u32[]{:S(2)}, u32[]{:S(2)}) collective-permute-start(f32[96,128]{1,0:T(8,128)S(1)} %get-tuple-element.63), channel_id=1, source_target_pairs={{0,24},{4,28},{8,16},{12,20},{16,8},{20,12},{24,0},{28,4},{1,25},{... | collective-permute-start | bytes 147464 | tf_op jit(solution)/shard_map/ppermute | solution.py:563
  24.3 4.1 %collective-permute-start.9 = (f32[96,128]{1,0:T(8,128)S(1)}, f32[96,128]{1,0:T(8,128)S(1)}, u32[]{:S(2)}, u32[]{:S(2)}) collective-permute-start(f32[96,128]{1,0:T(8,128)S(1)} %get-tuple-element.64), channel_id=1, source_target_pairs={{0,16},{4,20},{8,24},{12,28},{16,0},{20,4},{24,8},{28,12},{1,17},{... | collective-permute-start | bytes 147464 | tf_op jit(solution)/shard_map/ppermute | solution.py:563
  28.5 4.5 %copy-start.4 = (f32[8,8,128]{2,1,0:T(8,128)S(1)}, f32[8,8,128]{2,1,0:T(8,128)}, u32[]{:S(2)}) copy-start(f32[8,8,128]{2,1,0:T(8,128)} %momentum.1) | copy-start | bytes 98308
  28.5 4.5 %collective-permute-start.11 = (f32[24,128]{1,0:T(8,128)S(1)}, f32[24,128]{1,0:T(8,128)S(1)}, u32[]{:S(2)}, u32[]{:S(2)}) collective-permute-start(f32[24,128]{1,0:T(8,128)S(1)} %get-tuple-element.68), channel_id=1, source_target_pairs={{0,1},{1,0},{2,3},{3,2},{4,5},{5,4},{6,7},{7,6},{8,9},{9,8},{10,11... | collective-permute-start | bytes 36872 | tf_op jit(solution)/shard_map/ppermute | solution.py:574
  31.3 1.7 %collective-permute-start.12 = (f32[24,128]{1,0:T(8,128)S(1)}, f32[24,128]{1,0:T(8,128)S(1)}, u32[]{:S(2)}, u32[]{:S(2)}) collective-permute-start(f32[24,128]{1,0:T(8,128)S(1)} %get-tuple-element.69), channel_id=1, source_target_pairs={{0,4},{1,2},{2,1},{3,7},{4,0},{5,6},{6,5},{7,3},{8,12},{9,10},{10,... | collective-permute-start | bytes 36872 | tf_op jit(solution)/shard_map/ppermute | solution.py:573

commit v4 on v3

--- a/solution.py
+++ b/solution.py
@@ -153,21 +153,19 @@
 
 
 def partial_body(
-    state, velocity, cells, residuals, kappa,
-    partial_u, image, partial_q, push, out_b, out_a, side_a, side_b, field_u, field_q, grid_now,
+    state, velocity, cells, residuals, kappa, source_cells, source_codes, wavelets,
+    partial_u, image, partial_q, push, tap_u, weight, out_b, out_a, third_b, third_a,
+    field_u, field_q, grid_now, cells_here, codes_here, wavelets_here, sems, *, scale,
 ):
+    small = [(source_cells, cells_here), (source_codes, codes_here), (wavelets, wavelets_here)]
+    copies = run_copies(small, sems)
     depth, size_x, size_y = velocity.shape
     strip = kappa.shape[2]
     even = lax.rem(lax.axis_index("slab"), 2) == 0
-    even_strip = lax.rem(lax.axis_index("shot"), 2) == 0
     for j in range(3):
-        tail = kappa[j, :, strip - 1, :]
-        head = kappa[j, :, 0, :]
-        side_a[j * depth : (j + 1) * depth, :] = jnp.where(even_strip, tail, head)
-        side_b[j * depth : (j + 1) * depth, :] = jnp.where(even_strip, head, tail)
         tail = kappa[j, depth - 1]
         head = kappa[j, 0]
-        at = 2 * RADIUS * size_x + j * strip
+        at = RADIUS * size_x + j * strip
         out_a[at : at + strip, :] = jnp.where(even, tail, head)
         out_b[at : at + strip, :] = jnp.where(even, head, tail)
     for which, field in ((0, field_u), (1, field_q)):
@@ -206,12 +204,29 @@
         drive = vv * (laplacian_row(field_q, z, depth, size_x, size_y, lane) + grid_now[0, at, :])
         partial_q[z] = (2.0 * state[1, 0, 1, z] - state[0, 0, 1, z]) + drive
         push[z] = vv * grid_now[1, at, :]
+        weight[z] = -0.2 / (v * scale)
+
+    def inject(z, x, spot):
+        @pl.when((z >= 0) & (z < depth))
+        def _():
+            at = (z, pl.ds(x, 1), slice(None))
+            v = velocity[at]
+            change = (v * v) * spot
+            partial_u[at] = partial_u[at] + change
+            image[at] = image[at] + change * state[1, 0, 1, z, pl.ds(x, 1), :]
+
+    for copy in copies:
+        copy.wait()
+    first_layer = lax.axis_index("slab") * depth
+    point_cells(cells_here, codes_here, wavelets_here, 0, first_layer, size_x, size_y, inject)
     for k in range(2 * RADIUS):
-        source = partial_u if k < RADIUS else partial_q
-        tail = source[depth - RADIUS + k % RADIUS]
-        head = source[k % RADIUS]
-        out_a[k * size_x : (k + 1) * size_x, :] = jnp.where(even, tail, head)
-        out_b[k * size_x : (k + 1) * size_x, :] = jnp.where(even, head, tail)
+        tap_u[k] = weighted([(r, state[1, 0, 0, own]) for r, own in halo_near(k, depth)])
+    for source, to_a, to_b in ((partial_u, out_a, out_b), (partial_q, third_a, third_b)):
+        for k in range(RADIUS):
+            tail = source[depth - RADIUS + k]
+            head = source[k]
+            to_a[k * size_x : (k + 1) * size_x, :] = jnp.where(even, tail, head)
+            to_b[k * size_x : (k + 1) * size_x, :] = jnp.where(even, head, tail)
 
 
 def share_body(first_a, first_b, share):
@@ -245,31 +260,26 @@
 
 
 def near_body(
-    state, velocity, partial_u, image0, partial_q, push, first_b, first_a, cells, codes, wavelets,
-    u_part, q_part, image, gain, tap_u, tap_q,
-    u_edge, q_edge, u_now, q_now, cells_here, codes_here, wavelets_here, sems, *, scale,
+    state, velocity, partial_u, image0, partial_q, weight, first_a, first_b, cells, codes, wavelets,
+    u_part, q_next, image, gain,
+    u_edge, q_edge, u_now, cells_here, codes_here, wavelets_here, sems,
 ):
     small = run_copies([(cells, cells_here), (codes, codes_here), (wavelets, wavelets_here)], sems)
     depth, size_x, size_y = velocity.shape
-    here = lax.axis_index("slab")
-    even = lax.rem(here, 2) == 0
+    even = lax.rem(lax.axis_index("slab"), 2) == 0
     border = at_border()
     middle = slice(PAD, PAD + size_x)
     clear_sides(u_now, size_x)
-    clear_sides(q_now, size_x)
     for k in range(2 * RADIUS):
         row = k % RADIUS
         pick = ahead if k < RADIUS else after
         u_edge[k] = pick(even, border, first_a[row], first_b[row])
         q_edge[k] = pick(even, border, first_a[RADIUS + row], first_b[RADIUS + row])
-        near = halo_near(k, depth)
-        tap_u[k] = weighted([(r, state[1, 0, 0, own]) for r, own in near])
-        tap_q[k] = weighted([(r, state[1, 0, 1, own]) for r, own in near])
     for z in range(depth):
         near = own_near(z, depth)
         if not near:
             u_now[z, middle, :] = partial_u[z]
-            q_now[z, middle, :] = partial_q[z]
+            q_next[z] = partial_q[z]
             image[z] = image0[z]
             continue
         v = velocity[z]
@@ -277,24 +287,7 @@
         change = vv * weighted([(r, u_edge[k]) for r, k in near])
         u_now[z, middle, :] = partial_u[z] + change
         image[z] = image0[z] + change * state[1, 0, 1, z]
-        q_now[z, middle, :] = partial_q[z] + vv * weighted([(r, q_edge[k]) for r, k in near])
-
-    def first_step(z, x, spot):
-        @pl.when((z >= 0) & (z < depth))
-        def _():
-            v = velocity[z, pl.ds(x, 1), :]
-            change = (v * v) * spot
-            at = (z, pl.ds(PAD + x, 1), slice(None))
-            u_now[at] = u_now[at] + change
-            at = (z, pl.ds(x, 1), slice(None))
-            image[at] = image[at] + change * state[1, 0, 1, z, pl.ds(x, 1), :]
-
-        before = (z >= -RADIUS) & (z < 0)
-
-        @pl.when(before | ((z >= depth) & (z < depth + RADIUS)))
-        def _():
-            at = (jnp.where(before, z + RADIUS, z + RADIUS - depth), pl.ds(x, 1), slice(None))
-            tap_u[at] = tap_u[at] + spot
+        q_next[z] = partial_q[z] + vv * weighted([(r, q_edge[k]) for r, k in near])
 
     def second_step(z, x, spot):
         @pl.when((z >= 0) & (z < depth))
@@ -303,32 +296,29 @@
             v = velocity[at]
             change = (v * v) * spot
             u_part[at] = u_part[at] + change
-            image[at] = image[at] + (-0.2 * (change * q_now[z, pl.ds(PAD + x, 1), :])) / (v * scale)
-
-    for copy in small:
-        copy.wait()
-    sources = (cells_here, codes_here, wavelets_here)
-    point_cells(*sources, 0, here * depth, size_x, size_y, first_step)
+            image[at] = image[at] + weight[at] * (change * q_next[at])
+
     lane = lax.broadcasted_iota(jnp.int32, (size_x, size_y), 1)
     for z in range(depth):
         v = velocity[z]
         vv = v * v
-        adjoint = q_now[z, middle, :]
+        adjoint = q_next[z]
         drive = vv * laplacian_row(u_now, z, depth, size_x, size_y, lane)
         u_part[z] = (2.0 * u_now[z, middle, :] - state[1, 0, 0, z]) + drive
-        image[z] = (-0.2 * (image[z] + drive * adjoint)) / (v * scale)
-        gain[z] = (-0.2 / scale) * (v * adjoint)
-        drive = vv * laplacian_row(q_now, z, depth, size_x, size_y, lane) + push[z]
-        q_part[z] = (2.0 * adjoint - state[1, 0, 1, z]) + drive
-    point_cells(*sources, 1, here * depth, size_x, size_y, second_step)
-
-
-def halo_field(halo, second_b, second_a, tap, share_own, share_got, which):
+        image[z] = weight[z] * (image[z] + drive * adjoint)
+        gain[z] = (weight[z] * vv) * adjoint
+    for copy in small:
+        copy.wait()
+    first_layer = lax.axis_index("slab") * depth
+    point_cells(cells_here, codes_here, wavelets_here, 1, first_layer, size_x, size_y, second_step)
+
+
+def halo_field(halo, second_b, second_a, tap, share_own, share_got):
     size_x = halo.shape[1]
     even = lax.rem(lax.axis_index("slab"), 2) == 0
     border = at_border()
     for k in range(2 * RADIUS):
-        row = which * RADIUS + k % RADIUS
+        row = k % RADIUS
         rows = slice(row * size_x, (row + 1) * size_x)
         pick = ahead if k < RADIUS else after
         v = halo_speed(k, share_own, share_got)
@@ -336,14 +326,14 @@
 
 
 def image_body(
-    velocity, u_part, image_own, gain, tap_u, share_own, share_got, second_b, second_a,
-    fields, keep, send, halo, image, u_out, out_sem,
+    velocity, kappa, u_part, image_own, gain, tap_u, share_own, share_got, second_b, second_a,
+    fields, keep, packed, halo, image, u_out, out_sem,
 ):
     depth, size_x, size_y = velocity.shape
     core = lax.rem(lax.axis_index("shot"), 2)
     middle = slice(PAD, PAD + size_x)
     clear_sides(image, size_x)
-    halo_field(halo, second_b, second_a, tap_u, share_own, share_got, 0)
+    halo_field(halo, second_b, second_a, tap_u, share_own, share_got)
     for z in range(depth):
         near = own_near(z, depth)
         if not near:
@@ -360,6 +350,7 @@
     chips = keep.shape[0]
     strip = size_x // (2 * chips)
     wide = strip + 4
+    rows = depth * wide
     for m in range(chips):
         to = jnp.bitwise_xor(chip, m)
         for z in range(depth):
@@ -367,23 +358,37 @@
             low = image[z, at : at + wide, :]
             high = image[z, at + strip : at + strip + wide, :]
             keep[to, z * wide : (z + 1) * wide, :] = jnp.where(core == 0, low, high)
-            send[to, z * wide : (z + 1) * wide, :] = jnp.where(core == 0, high, low)
+            packed[pl.ds(to * rows + z * wide, wide), :] = jnp.where(core == 0, high, low)
+    for j in range(3):
+        tail = kappa[j, :, strip - 1, :]
+        head = kappa[j, :, 0, :]
+        at = chips * rows + j * depth
+        packed[at : at + depth, :] = jnp.where(core == 0, tail, head)
+        packed[at + 3 * depth : at + 4 * depth, :] = jnp.where(core == 0, head, tail)
     copy_out.wait()
 
 
+def hands_on(k):
+    return k > 0 and k & (k + 1) == 0
+
+
 def pair_sum_body(keep, got, *outs):
+    rows = keep.shape[1]
     for k, out in enumerate(outs):
-        out[...] = keep[k] + got[k]
+        out[0:rows, :] = keep[k] + got[k * rows : (k + 1) * rows, :]
+        if hands_on(k):
+            side = (out.shape[0] - rows)
+            out[rows : rows + side, :] = got[len(outs) * rows + side : len(outs) * rows + 2 * side, :]
 
 
 def strip_sum_body(*refs, count, wide):
     parts, (total, edge_b, edge_a) = refs[:count], refs[count:]
-    added = parts[0][...]
+    rows = total.shape[0]
+    added = parts[0][0:rows, :]
     for part in parts[1:]:
-        added = added + part[...]
+        added = added + part[0:rows, :]
     total[...] = added
     even = lax.rem(lax.axis_index("slab"), 2) == 0
-    rows = total.shape[0]
     head = total[0 : 2 * wide, :]
     tail = total[rows - 2 * wide : rows, :]
     edge_a[...] = jnp.where(even, tail, head)
@@ -391,34 +396,52 @@
 
 
 def adjoint_body(
-    fields_in, velocity, q_part, tap_q, share_own, share_got, second_b, second_a, fields, halo, q_out, out_sem
+    fields_in, state, velocity, q_next, push, share_own, share_got, third_b, third_a, fields, field, tap, halo, q_out, out_sem
 ):
-    depth = velocity.shape[0]
-    halo_field(halo, second_b, second_a, tap_q, share_own, share_got, 1)
+    depth, size_x, size_y = velocity.shape
+    whole = depth + 2 * RADIUS
+    middle = slice(PAD, PAD + size_x)
+    clear_sides(field, size_x)
+    for k in range(2 * RADIUS):
+        tap[k] = weighted([(r, state[1, 0, 1, own]) for r, own in halo_near(k, depth)])
+    halo_field(halo, third_b, third_a, tap, share_own, share_got)
+    for z in range(whole):
+        inner = RADIUS <= z < RADIUS + depth
+        field[z, middle, :] = q_next[z - RADIUS] if inner else halo[z if z < RADIUS else z - depth]
+    lane = lax.broadcasted_iota(jnp.int32, (size_x, size_y), 1)
     for z in range(depth):
-        near = own_near(z, depth)
         v = velocity[z]
-        q_out[z] = q_part[z] + (v * v) * weighted([(r, halo[k]) for r, k in near]) if near else q_part[z]
+        drive = (v * v) * laplacian_row(field, z + RADIUS, whole, size_x, size_y, lane) + push[z]
+        q_out[z] = (2.0 * q_next[z] - state[1, 0, 1, z]) + drive
     copy = pltpu.make_async_copy(q_out, fields.at[0, 1], out_sem)
     copy.start()
     copy.wait()
 
 
-def coefficient_body(kappa, second_b, second_a, side_a, side_b, coef, *, size_x):
+def coefficient_body(kappa, second_b, second_a, got, *rest, size_x, distances):
+    arrived, coef = rest[:-1], rest[-1]
     _, depth, strip, _ = kappa.shape
     even = lax.rem(lax.axis_index("slab"), 2) == 0
     border = at_border()
     shot = lax.axis_index("shot")
     even_strip = lax.rem(shot, 2) == 0
     end_strip = (shot == 0) | (shot == lax.axis_size("shot") - 1)
+    chip = lax.div(shot, 2)
+    distance = jnp.bitwise_xor(chip, jnp.where(even_strip, chip - 1, chip + 1))
+    side = 3 * depth
+    ends = [part.shape[0] for part in arrived]
+    far = arrived[0][ends[0] - side : ends[0], :]
+    for k, end, part in zip(distances[1:], ends[1:], arrived[1:]):
+        far = jnp.where(distance == k, part[end - side : end, :], far)
+    facing = got[got.shape[0] - 2 * side : got.shape[0] - side, :]
     coef[...] = jnp.zeros(coef.shape, F32)
     for j in range(3):
-        at = slice(2 * RADIUS * size_x + j * strip, 2 * RADIUS * size_x + (j + 1) * strip)
+        at = slice(RADIUS * size_x + j * strip, RADIUS * size_x + (j + 1) * strip)
         coef[j, 0, 1 : strip + 1, :] = ahead(even, border, second_a[at, :], second_b[at, :])
         coef[j, depth + 1, 1 : strip + 1, :] = after(even, border, second_a[at, :], second_b[at, :])
         of = slice(j * depth, (j + 1) * depth)
-        left = ahead(even_strip, end_strip, side_a[of, :], side_b[of, :])
-        right = after(even_strip, end_strip, side_a[of, :], side_b[of, :])
+        left = ahead(even_strip, end_strip, facing[of, :], far[of, :])
+        right = after(even_strip, end_strip, facing[of, :], far[of, :])
         for z in range(depth):
             coef[j, z + 1, 1 : strip + 1, :] = kappa[j, z]
             coef[j, z + 1, 0:1, :] = left[z : z + 1, :]
@@ -489,49 +512,48 @@
     first_b = lax.ppermute(out_b, both, z_odd)
     first_a = lax.ppermute(out_a, "slab", z_even)
 
-    flat = shape(2 * RADIUS * size_x + 3 * strip, size_y)
-    side = shape(3 * depth, size_y)
+    flat = shape(RADIUS * size_x + 3 * strip, size_y)
+    flat_q = shape(RADIUS * size_x, size_y)
     edge = shape(RADIUS, size_x, size_y)
-    partial_u, image0, partial_q, push, out_b, out_a, side_a, side_b = call(
-        partial_body,
-        [shape(*cube)] * 4 + [flat, flat, side, side],
-        (wave_state, velocity, receiver_cells, residuals, diffusivity),
-        ["vmem"] * 5,
-        ["vmem"] * 8,
-        [pltpu.VMEM(padded, F32)] * 2 + [pltpu.VMEM((STEPS, depth * size_x, size_y), F32)],
+    ring = shape(2 * RADIUS, size_x, size_y)
+    ring_scratch = pltpu.VMEM(ring.shape, F32)
+    small = tuple(
+        pltpu.with_memory_space_constraint(x, pltpu.HBM) for x in (source_cells, source_codes, wavelets.T)
+    )
+    small_scratch = [pltpu.SMEM(x.shape, x.dtype) for x in small] + [dma((3,))]
+    partial_u, image0, partial_q, push, tap_u, weight, out_b, out_a, third_b, third_a = call(
+        functools.partial(partial_body, scale=math.sqrt(shots * STEPS)),
+        [shape(*cube)] * 4 + [ring, shape(*cube), flat, flat, flat_q, flat_q],
+        (wave_state, velocity, receiver_cells, residuals, diffusivity, *small),
+        ["vmem"] * 5 + ["hbm"] * 3,
+        ["vmem"] * 10,
+        [pltpu.VMEM(padded, F32)] * 2 + [pltpu.VMEM((STEPS, depth * size_x, size_y), F32)] + small_scratch,
         us=1.7,
     )
     second_b = lax.ppermute(out_b, both, z_odd)
     second_a = lax.ppermute(out_a, "slab", z_even)
-    side_a = lax.ppermute(side_a, "shot", even_pairs(shots))
-    side_b = lax.ppermute(side_b, "shot", odd_pairs(shots))
-
-    first_a, first_b, side_a, side_b = lax.optimization_barrier((first_a, first_b, side_a, side_b))
+    third_b = lax.ppermute(third_b, both, z_odd)
+    third_a = lax.ppermute(third_a, "slab", z_even)
+
     (share_own,) = call(share_body, [edge], (first_a, first_b), ["vmem"] * 2, ["vmem"])
     share_got = lax.ppermute(share_own, "shot", even_pairs(shots))
-    ring = shape(2 * RADIUS, size_x, size_y)
-    ring_scratch = pltpu.VMEM(ring.shape, F32)
-    small = (source_cells, source_codes, wavelets.T)
-    u_part, q_part, image_own, gain, tap_u, tap_q = call(
-        functools.partial(near_body, scale=math.sqrt(shots * STEPS)),
-        [shape(*cube)] * 4 + [ring, ring],
-        (wave_state, velocity, partial_u, image0, partial_q, push, first_b, first_a)
-        + tuple(pltpu.with_memory_space_constraint(x, pltpu.HBM) for x in small),
+    u_part, q_next, image_own, gain = call(
+        near_body,
+        [shape(*cube)] * 4,
+        (wave_state, velocity, partial_u, image0, partial_q, weight, first_a, first_b, *small),
         ["vmem"] * 8 + ["hbm"] * 3,
-        ["vmem"] * 6,
-        [ring_scratch] * 2
-        + [pltpu.VMEM(padded, F32)] * 2
-        + [pltpu.SMEM(x.shape, x.dtype) for x in small]
-        + [dma((3,))],
-        us=2.3,
+        ["vmem"] * 4,
+        [ring_scratch] * 2 + [pltpu.VMEM(padded, F32)] + small_scratch,
+        us=1.2,
     )
 
     part = shape(chips, depth * wide, size_y)
+    side = 3 * depth
     fields, keep, send = call(
         image_body,
-        [shape(1, 2, *cube), part, part],
-        (velocity, u_part, image_own, gain, tap_u, share_own, share_got, second_b, second_a),
-        ["vmem"] * 9,
+        [shape(1, 2, *cube), part, shape(chips * depth * wide + 2 * side, size_y)],
+        (velocity, diffusivity, u_part, image_own, gain, tap_u, share_own, share_got, second_b, second_a),
+        ["vmem"] * 10,
         ["any"] + ["vmem"] * 2,
         [ring_scratch, pltpu.VMEM(padded, F32), pltpu.VMEM(cube, F32), dma],
         us=1.0,
@@ -540,28 +562,26 @@
     (fields,) = call(
         adjoint_body,
         [shape(1, 2, *cube)],
-        (fields, velocity, q_part, tap_q, share_own, share_got, second_b, second_a),
-        ["any"] + ["vmem"] * 7,
+        (fields, wave_state, velocity, q_next, push, share_own, share_got, third_b, third_a),
+        ["any"] + ["vmem"] * 8,
         ["any"],
-        [ring_scratch, pltpu.VMEM(cube, F32), dma],
+        [
+            pltpu.VMEM((depth + 2 * RADIUS, size_x + 2 * PAD, size_y), F32),
+            ring_scratch,
+            ring_scratch,
+            pltpu.VMEM(cube, F32),
+            dma,
+        ],
         aliases={0: 0},
-        us=0.7,
-    )
-    tall = 8 * ((wide + 7) // 8)
-    (coef,) = call(
-        functools.partial(coefficient_body, size_x=size_x),
-        [shape(3, depth + 2, tall, size_y)],
-        (diffusivity, second_b, second_a, side_a, side_b),
-        ["vmem"] * 5,
-        ["vmem"],
-        us=0.3,
-    )
-    got, fields, coef = lax.optimization_barrier((got, fields, coef))
+        us=1.4,
+    )
     row_block = shape(depth * wide, size_y)
-    parts = call(pair_sum_body, [row_block] * chips, (keep, got), ["vmem"] * 2, ["vmem"] * chips)
+    sums = [shape(depth * wide + (side if hands_on(k) else 0), size_y) for k in range(chips)]
+    parts = call(pair_sum_body, sums, (keep, got), ["vmem"] * 2, ["vmem"] * chips)
     arrived = [
         lax.ppermute(parts[k], "shot", [(i, i ^ (2 * k)) for i in range(shots)]) for k in reversed(range(1, chips))
     ] + [parts[0]]
+    *arrived, fields = lax.optimization_barrier((*arrived, fields))
     two = shape(2 * wide, size_y)
     total, out_b, out_a = call(
         functools.partial(strip_sum_body, count=chips, wide=wide),
@@ -572,6 +592,16 @@
     )
     grad_b = lax.ppermute(out_b, both, z_odd)
     grad_a = lax.ppermute(out_a, "slab", z_even)
+    distances = [k for k in range(chips) if hands_on(k)]
+    tall = 8 * ((wide + 7) // 8)
+    (coef,) = call(
+        functools.partial(coefficient_body, size_x=size_x, distances=distances),
+        [shape(3, depth + 2, tall, size_y)],
+        (diffusivity, second_b, second_a, got, *(arrived[chips - 1 - k] for k in distances)),
+        ["vmem"] * (4 + len(distances)),
+        ["vmem"],
+        us=0.1,
+    )
     new_momentum, new_velocity = call(
         smooth_body,
         [shape(*momentum.shape)] * 2,

time: 34 us -> 32 us (0.941)
  waiting for transfers between devices: 9.43 us -> 6.31 us
  local copies, waits for them, and re-layouts: 0.92 us -> 1.57 us
  Pallas kernels: 7.58 us -> 8.07 us
    ppermute x2, waiting for transfers between devices: 2.98 us -> 0.34 us  [the longest x1 0.34 us: on_device(): third_a = lax.ppermute(third_a, 'slab', z_even)]
    ppermute x3, waiting for transfers between devices: 3.78 us -> 1.87 us  [on_device(): lax.ppermute(parts[k], 'shot', [(i, i ^ 2 * k) for i in range(shots)])]
    ppermute x1, waiting for transfers between devices: 0.01 us -> 1.22 us  [on_device(): first_a = lax.ppermute(out_a, 'slab', z_even)]
    ppermute x2, starting transfers between devices: 2.22 us -> 3.11 us  [the longest x1 2.95 us: on_device(): third_a = lax.ppermute(third_a, 'slab', z_even)]
    ppermute x1, starting transfers between devices: 2.78 us -> 1.93 us  [on_device(): grad_a = lax.ppermute(out_a, 'slab', z_even)]
    unnamed x14, local copies, waits for them, and re-layouts: 0.92 us -> 1.57 us
    ppermute x1, waiting for transfers between devices: 0.5 us -> 1.08 us  [on_device(): second_a = lax.ppermute(out_a, 'slab', z_even)]
    pallas_call x10, Pallas kernels: 7.58 us -> 8.07 us  [call(): pl.pallas_call(body, out_shape=list(out_shapes), in_specs=[SPECS[s] for s...]
  transfers between devices with their start and end apart: 13 -> 13, of which waited for: 8 -> 5; matrix products, arithmetic and copies ran while one was open for 0% -> 0% of each run, Pallas kernels for 13% -> 16%
where the time goes in v4:
time: 32 us; the launch traced here: 31.8 us
  starting transfers between devices  15 us (47%)
  Pallas kernels  8.07 us (25%)
  waiting for transfers between devices  6.31 us (20%)
  local copies, waits for them, and re-layouts  1.57 us (5%)
  between operations  0.77 us (2%)
    pallas_call x10, Pallas kernels, call(): pl.pallas_call(body, out_shape=list(out_shapes), in_specs=[SPECS[s] for s...  8.07 us
    ppermute x3, starting transfers between devices, on_device(): lax.ppermute(parts[k], 'shot', [(i, i ^ 2 * k) for i in range(shots)])  3.55 us
    ppermute x1, starting transfers between devices, on_device(): second_a = lax.ppermute(out_a, 'slab', z_even)  3.14 us
    ppermute x1, starting transfers between devices, on_device(): first_a = lax.ppermute(out_a, 'slab', z_even)  3.09 us
    ppermute x1, starting transfers between devices, on_device(): third_a = lax.ppermute(third_a, 'slab', z_even)  2.95 us
    ppermute x1, starting transfers between devices, on_device(): grad_a = lax.ppermute(out_a, 'slab', z_even)  1.93 us
    ppermute x3, waiting for transfers between devices, on_device(): lax.ppermute(parts[k], 'shot', [(i, i ^ 2 * k) for i in range(shots)])  1.87 us
    ppermute x1, waiting for transfers between devices, on_device(): grad_a = lax.ppermute(out_a, 'slab', z_even)  1.79 us
  transfers between devices with their start and end apart: 13, of which 5 were waited for; matrix products, arithmetic and copies ran while one was open for 0% of the time, Pallas kernels for 16%

profile of v4, /device:TPU:0, one launch (start us, length us, event | category | flops | bytes accessed | tf_op | source)
XLA Modules:
  0.0 31.8 jit_solution(18207890965884706693)
XLA Ops:
  0.6 1.3 %shard_map.113 = (f32[10,64,128]{2,1,0:T(8,128)S(1)}, f32[10,64,128]{2,1,0:T(8,128)S(1)}) custom-call(f32[2,1,2,8,64,128]{5,4,3,2,1,0:T(8,128)} %state.7, f32[8,64,128]{2,1,0:T(8,128)} %velocity.11), custom_call_target="tpu_custom_call" | custom-call | bytes 4797000 | tf_op jit(solution)/shard_map/pallas_call | solution.py:69
  2.0 3.1 %collective-permute-start = (f32[10,64,128]{2,1,0:T(8,128)S(1)}, f32[10,64,128]{2,1,0:T(8,128)S(1)}, u32[]{:S(2)}, u32[]{:S(2)}) collective-permute-start(f32[10,64,128]{2,1,0:T(8,128)S(1)} %get-tuple-element.40), channel_id=1, source_target_pairs={{0,1},{1,0},{2,3},{3,2},{4,5},{5,4},{6,7},{7,6},{8,9},{9,8},{10,11... | collective-permute-start | bytes 983048 | tf_op jit(solution)/shard_map/ppermute | solution.py:513
  5.1 0.7 %copy-done.6 = s32[1,256]{1,0:T(1,128)S(1)} copy-done((s32[1,256]{1,0:T(1,128)S(1)}, s32[1,256]{1,0:T(1,128)}, u32[]{:S(2)}) %copy-start.6) | copy-done | bytes 1048
  5.8 0.9 %copy-done.2 = f32[3,8,8,128]{3,2,1,0:T(8,128)S(1)} copy-done((f32[3,8,8,128]{3,2,1,0:T(8,128)S(1)}, f32[3,8,8,128]{3,2,1,0:T(8,128)}, u32[]{:S(2)}) %copy-start.2) | copy-done | bytes 98328
  6.7 2.2 %shard_map.112 = (f32[8,64,128]{2,1,0:T(8,128)S(1)}, f32[8,64,128]{2,1,0:T(8,128)S(1)}, f32[8,64,128]{2,1,0:T(8,128)S(1)}, f32[8,64,128]{2,1,0:T(8,128)S(1)}, f3...) custom-call(f32[2,1,2,8,64,128]{5,4,3,2,1,0:T(8,128)S(1)} %copy-done, ...), custom_call_target="tpu_custom_call" | custom-call | bytes 6273000 | tf_op jit(solution)/shard_map/pallas_call | solution.py:69
  8.9 0.1 collective-permute-start.3
  8.9 3.1 %collective-permute-start.4 = (f32[280,128]{1,0:T(8,128)S(1)}, f32[280,128]{1,0:T(8,128)S(1)}, u32[]{:S(2)}, u32[]{:S(2)}) collective-permute-start(f32[280,128]{1,0:T(8,128)S(1)} %get-tuple-element.47), channel_id=1, source_target_pairs={{0,1},{1,0},{2,3},{3,2},{4,5},{5,4},{6,7},{7,6},{8,9},{9,8},{10,11... | collective-permute-start | bytes 430088 | tf_op jit(solution)/shard_map/ppermute | solution.py:534
  12.1 1.2 %collective-permute-done.first_a = f32[10,64,128]{2,1,0:T(8,128)S(1)} collective-permute-done((f32[10,64,128]{2,1,0:T(8,128)S(1)}, f32[10,64,128]{2,1,0:T(8,128)S(1)}, u32[]{:S(2)}, u32[]{:S(2)}) %collective-permute-start) | collective-permute-done | bytes 327712 | tf_op jit(solution)/shard_map/ppermute | solution.py:513
  13.3 0.1 collective-permute-start.2
  13.4 1.4 %shard_map.114 = (f32[8,64,128]{2,1,0:T(8,128)S(1)}, f32[8,64,128]{2,1,0:T(8,128)S(1)}, f32[8,64,128]{2,1,0:T(8,128)S(1)}, f32[8,64,128]{2,1,0:T(8,128)S(1)}) custom-call(f32[2,1,2,8,64,128]{5,4,3,2,1,0:T(8,128)S(1)} %copy-done, f32[8,64,128]{2,1,0:T(8,128)S(1)} %copy-done.1, f32[8,64,128]{2,1,0:T(8,128)S(1)} %get-tuple-element.36.partial_u, ...), custom_call_target="tpu_custom_call" | custom-call | bytes 4428000 | tf_op jit(solution)/shard_map/pallas_call | solution.py:69
  14.8 1.1 %collective-permute-done.4.second_a = f32[280,128]{1,0:T(8,128)S(1)} collective-permute-done((f32[280,128]{1,0:T(8,128)S(1)}, f32[280,128]{1,0:T(8,128)S(1)}, u32[]{:S(2)}, u32[]{:S(2)}) %collective-permute-start.4) | collective-permute-done | bytes 143392 | tf_op jit(solution)/shard_map/ppermute | solution.py:534
  15.9 0.9 %shard_map.116 = (f32[1,2,8,64,128]{4,3,2,1,0:T(8,128)}, f32[4,96,128]{2,1,0:T(8,128)S(1)}, f32[432,128]{1,0:T(8,128)S(1)}) custom-call(f32[8,64,128]{2,1,0:T(8,128)S(1)} %copy-done.1, f32[3,8,8,128]{3,2,1,0:T(8,128)S(1)} %copy-done.3, f32[8,64,128]{2,1,0:T(8,128)S(1)} %get-tuple-element.42.u_part, f32[8,64,128]{2,1,0:T(8,128)S(1)} %get-tuple-element.43.image_own, ...), custom_call_target="tpu_custom_call" | custom-call | bytes 3690000 | tf_op jit(solution)/shard_map/pallas_call | solution.py:69
  16.8 0.1 collective-permute-start.5
  16.9 2.9 %collective-permute-start.10 = (f32[256,128]{1,0:T(8,128)S(1)}, f32[256,128]{1,0:T(8,128)S(1)}, u32[]{:S(2)}, u32[]{:S(2)}) collective-permute-start(f32[256,128]{1,0:T(8,128)S(1)} %get-tuple-element.58), channel_id=1, source_target_pairs={{0,1},{1,0},{2,3},{3,2},{4,5},{5,4},{6,7},{7,6},{8,9},{9,8},{10,11... | collective-permute-start | bytes 393224 | tf_op jit(solution)/shard_map/ppermute | solution.py:536
  19.8 0.2 collective-permute-start.9
  20.0 2.5 %collective-permute-start.6 = (f32[120,128]{1,0:T(8,128)S(1)}, f32[120,128]{1,0:T(8,128)S(1)}, u32[]{:S(2)}, u32[]{:S(2)}) collective-permute-start(f32[120,128]{1,0:T(8,128)S(1)} %get-tuple-element.50), channel_id=1, source_target_pairs={{0,24},{4,28},{8,16},{12,20},{16,8},{20,12},{24,0},{28,4},{1,25},{... | collective-permute-start | bytes 184328 | tf_op jit(solution)/shard_map/ppermute | solution.py:582
  22.5 0.5 %collective-permute-start.8 = (f32[120,128]{1,0:T(8,128)S(1)}, f32[120,128]{1,0:T(8,128)S(1)}, u32[]{:S(2)}, u32[]{:S(2)}) collective-permute-start(f32[120,128]{1,0:T(8,128)S(1)} %get-tuple-element.52), channel_id=1, source_target_pairs={{0,8},{4,12},{8,0},{12,4},{16,24},{20,28},{24,16},{28,20},{1,9},{5... | collective-permute-start | bytes 184328 | tf_op jit(solution)/shard_map/ppermute | solution.py:582
  23.1 0.5 %collective-permute-start.7 = (f32[96,128]{1,0:T(8,128)S(1)}, f32[96,128]{1,0:T(8,128)S(1)}, u32[]{:S(2)}, u32[]{:S(2)}) collective-permute-start(f32[96,128]{1,0:T(8,128)S(1)} %get-tuple-element.51), channel_id=1, source_target_pairs={{0,16},{4,20},{8,24},{12,28},{16,0},{20,4},{24,8},{28,12},{1,17},{... | collective-permute-start | bytes 147464 | tf_op jit(solution)/shard_map/ppermute | solution.py:582
  23.6 0.3 %collective-permute-done.10.third_a = f32[256,128]{1,0:T(8,128)S(1)} collective-permute-done((f32[256,128]{1,0:T(8,128)S(1)}, f32[256,128]{1,0:T(8,128)S(1)}, u32[]{:S(2)}, u32[]{:S(2)}) %collective-permute-start.10) | collective-permute-done | bytes 131104 | tf_op jit(solution)/shard_map/ppermute | solution.py:536
  23.9 1.4 %shard_map.118 = f32[1,2,8,64,128]{4,3,2,1,0:T(8,128)} custom-call(f32[1,2,8,64,128]{4,3,2,1,0:T(8,128)} %get-tuple-element.54.fields_in, f32[2,1,2,8,64,128]{5,4,3,2,1,0:T(8,128)S(1)} %copy-done, f32[8,64,128]{2,1,0:T(8,128)S(1)} %copy-done.1, f32[8,64,128]{2,1,0:T(8,128)S(1)} %get-tuple-element.55.q_next, ...), custom_call_target="tpu_custom_call", output_to_operand_aliasing={{}: (0, {})} | custom-call | bytes 5166000 | tf_op jit(solution)/shard_map/pallas_call | solution.py:69
  25.3 1.9 %collective-permute-done.7.refs_1_ = f32[96,128]{1,0:T(8,128)S(1)} collective-permute-done((f32[96,128]{1,0:T(8,128)S(1)}, f32[96,128]{1,0:T(8,128)S(1)}, u32[]{:S(2)}, u32[]{:S(2)}) %collective-permute-start.7) | collective-permute-done | bytes 49184 | tf_op jit(solution)/shard_map/ppermute | solution.py:582
  27.2 1.9 %collective-permute-start.11 = (f32[24,128]{1,0:T(8,128)S(1)}, f32[24,128]{1,0:T(8,128)S(1)}, u32[]{:S(2)}, u32[]{:S(2)}) collective-permute-start(f32[24,128]{1,0:T(8,128)S(1)} %get-tuple-element.65), channel_id=1, source_target_pairs={{0,1},{1,0},{2,3},{3,2},{4,5},{5,4},{6,7},{7,6},{8,9},{9,8},{10,11... | collective-permute-start | bytes 36872 | tf_op jit(solution)/shard_map/ppermute | solution.py:594
  29.1 1.8 %collective-permute-done.11.got_a = f32[24,128]{1,0:T(8,128)S(1)} collective-permute-done((f32[24,128]{1,0:T(8,128)S(1)}, f32[24,128]{1,0:T(8,128)S(1)}, u32[]{:S(2)}, u32[]{:S(2)}) %collective-permute-start.11) | collective-permute-done | bytes 12320 | tf_op jit(solution)/shard_map/ppermute | solution.py:594
  30.9 0.8 %shard_map.121 = (f32[8,8,128]{2,1,0:T(8,128)}, f32[8,8,128]{2,1,0:T(8,128)}) custom-call(f32[96,128]{1,0:T(8,128)S(1)} %get-tuple-element.64.total, f32[24,128]{1,0:T(8,128)S(1)} %collective-permute-done.11.got_a, f32[24,128]{1,0:T(8,128)S(1)} %collective-permute-done.12.got_b, f32[3,8,8,128]{3,2,1,0:T(8,128)S(1)} %copy-done.3, ...), custom_call_target="tpu_custom_call" | custom-call | bytes 2583000 | tf_op jit(solution)/shard_map/pallas_call | solution.py:69
  (26 shorter events, 0.1 us)
Async XLA Ops:
  0.6 4.5 %copy-start = (f32[2,1,2,8,64,128]{5,4,3,2,1,0:T(8,128)S(1)}, f32[2,1,2,8,64,128]{5,4,3,2,1,0:T(8,128)}, u32[]{:S(2)}) copy-start(f32[2,1,2,8,64,128]{5,4,3,2,1,0:T(8,128)} %state.7) | copy-start | bytes 3145732
  0.6 4.5 %copy-start.1 = (f32[8,64,128]{2,1,0:T(8,128)S(1)}, f32[8,64,128]{2,1,0:T(8,128)}, u32[]{:S(2)}) copy-start(f32[8,64,128]{2,1,0:T(8,128)} %velocity.11) | copy-start | bytes 786436
  2.0 3.1 %copy-start.5 = (f32[1,2,256]{2,1,0:T(2,128)S(1)}, f32[1,2,256]{2,1,0:T(2,128)}, u32[]{:S(2)}) copy-start(f32[1,2,256]{2,1,0:T(2,128)} %residuals.1) | copy-start | bytes 6148
  2.0 11.3 %collective-permute-start = (f32[10,64,128]{2,1,0:T(8,128)S(1)}, f32[10,64,128]{2,1,0:T(8,128)S(1)}, u32[]{:S(2)}, u32[]{:S(2)}) collective-permute-start(f32[10,64,128]{2,1,0:T(8,128)S(1)} %get-tuple-element.40), channel_id=1, source_target_pairs={{0,1},{1,0},{2,3},{3,2},{4,5},{5,4},{6,7},{7,6},{8,9},{9,8},{10,11... | collective-permute-start | bytes 983048 | tf_op jit(solution)/shard_map/ppermute | solution.py:513
  5.1 0.7 %copy-start.6 = (s32[1,256]{1,0:T(1,128)S(1)}, s32[1,256]{1,0:T(1,128)}, u32[]{:S(2)}) copy-start(s32[1,256]{1,0:T(1,128)} %cells.2) | copy-start | bytes 3076
  5.1 8.2 %collective-permute-start.1 = (f32[10,64,128]{2,1,0:T(8,128)S(1)}, f32[10,64,128]{2,1,0:T(8,128)S(1)}, u32[]{:S(2)}, u32[]{:S(2)}) collective-permute-start(f32[10,64,128]{2,1,0:T(8,128)S(1)} %get-tuple-element.41), channel_id=1, source_target_pairs={{0,4},{1,2},{2,1},{3,7},{4,0},{5,6},{6,5},{7,3},{8,12},{9,10},{10,... | collective-permute-start | bytes 983048 | tf_op jit(solution)/shard_map/ppermute | solution.py:512
  5.8 0.9 %copy-start.2 = (f32[3,8,8,128]{3,2,1,0:T(8,128)S(1)}, f32[3,8,8,128]{3,2,1,0:T(8,128)}, u32[]{:S(2)}) copy-start(f32[3,8,8,128]{3,2,1,0:T(8,128)} %kappa.7) | copy-start | bytes 294916
  8.9 5.9 %collective-permute-start.3 = (f32[280,128]{1,0:T(8,128)S(1)}, f32[280,128]{1,0:T(8,128)S(1)}, u32[]{:S(2)}, u32[]{:S(2)}) collective-permute-start(f32[280,128]{1,0:T(8,128)S(1)} %get-tuple-element.46), channel_id=1, source_target_pairs={{0,4},{1,2},{2,1},{3,7},{4,0},{5,6},{6,5},{7,3},{8,12},{9,10},{10,... | collective-permute-start | bytes 430088 | tf_op jit(solution)/shard_map/ppermute | solution.py:533
  8.9 6.9 %collective-permute-start.4 = (f32[280,128]{1,0:T(8,128)S(1)}, f32[280,128]{1,0:T(8,128)S(1)}, u32[]{:S(2)}, u32[]{:S(2)}) collective-permute-start(f32[280,128]{1,0:T(8,128)S(1)} %get-tuple-element.47), channel_id=1, source_target_pairs={{0,1},{1,0},{2,3},{3,2},{4,5},{5,4},{6,7},{7,6},{8,9},{9,8},{10,11... | collective-permute-start | bytes 430088 | tf_op jit(solution)/shard_map/ppermute | solution.py:534
  13.3 2.5 %collective-permute-start.2 = (f32[4,64,128]{2,1,0:T(8,128)S(1)}, f32[4,64,128]{2,1,0:T(8,128)S(1)}, u32[]{:S(2)}, u32[]{:S(2)}) collective-permute-start(f32[4,64,128]{2,1,0:T(8,128)S(1)} %shard_map.115.share_own), channel_id=1, source_target_pairs={{0,4},{4,0},{8,12},{12,8},{16,20},{20,16},{24,28},{28,24},{1,5},{5... | collective-permute-start | bytes 393224 | tf_op jit(solution)/shard_map/ppermute | solution.py:539
  13.4 2.5 %copy-start.3 = (f32[3,8,8,128]{3,2,1,0:T(8,128)S(1)}, f32[3,8,8,128]{3,2,1,0:T(8,128)}, u32[]{:S(2)}) copy-start(f32[3,8,8,128]{3,2,1,0:T(8,128)} %kappa.7) | copy-start | bytes 294916
  16.8 3.2 %collective-permute-start.5 = (f32[432,128]{1,0:T(8,128)S(1)}, f32[432,128]{1,0:T(8,128)S(1)}, u32[]{:S(2)}, u32[]{:S(2)}) collective-permute-start(f32[432,128]{1,0:T(8,128)S(1)} %get-tuple-element.49), channel_id=1, source_target_pairs={{0,4},{4,0},{8,12},{12,8},{16,20},{20,16},{24,28},{28,24},{1,5},{5... | collective-permute-start | bytes 663560 | tf_op jit(solution)/shard_map/ppermute | solution.py:561
  16.9 7.0 %collective-permute-start.10 = (f32[256,128]{1,0:T(8,128)S(1)}, f32[256,128]{1,0:T(8,128)S(1)}, u32[]{:S(2)}, u32[]{:S(2)}) collective-permute-start(f32[256,128]{1,0:T(8,128)S(1)} %get-tuple-element.58), channel_id=1, source_target_pairs={{0,1},{1,0},{2,3},{3,2},{4,5},{5,4},{6,7},{7,6},{8,9},{9,8},{10,11... | collective-permute-start | bytes 393224 | tf_op jit(solution)/shard_map/ppermute | solution.py:536
  19.8 4.1 %collective-permute-start.9 = (f32[256,128]{1,0:T(8,128)S(1)}, f32[256,128]{1,0:T(8,128)S(1)}, u32[]{:S(2)}, u32[]{:S(2)}) collective-permute-start(f32[256,128]{1,0:T(8,128)S(1)} %get-tuple-element.57), channel_id=1, source_target_pairs={{0,4},{1,2},{2,1},{3,7},{4,0},{5,6},{6,5},{7,3},{8,12},{9,10},{10,... | collective-permute-start | bytes 393224 | tf_op jit(solution)/shard_map/ppermute | solution.py:535
  20.0 7.1 %collective-permute-start.6 = (f32[120,128]{1,0:T(8,128)S(1)}, f32[120,128]{1,0:T(8,128)S(1)}, u32[]{:S(2)}, u32[]{:S(2)}) collective-permute-start(f32[120,128]{1,0:T(8,128)S(1)} %get-tuple-element.50), channel_id=1, source_target_pairs={{0,24},{4,28},{8,16},{12,20},{16,8},{20,12},{24,0},{28,4},{1,25},{... | collective-permute-start | bytes 184328 | tf_op jit(solution)/shard_map/ppermute | solution.py:582
  22.5 4.6 %collective-permute-start.8 = (f32[120,128]{1,0:T(8,128)S(1)}, f32[120,128]{1,0:T(8,128)S(1)}, u32[]{:S(2)}, u32[]{:S(2)}) collective-permute-start(f32[120,128]{1,0:T(8,128)S(1)} %get-tuple-element.52), channel_id=1, source_target_pairs={{0,8},{4,12},{8,0},{12,4},{16,24},{20,28},{24,16},{28,20},{1,9},{5... | collective-permute-start | bytes 184328 | tf_op jit(solution)/shard_map/ppermute | solution.py:582
  23.1 4.1 %collective-permute-start.7 = (f32[96,128]{1,0:T(8,128)S(1)}, f32[96,128]{1,0:T(8,128)S(1)}, u32[]{:S(2)}, u32[]{:S(2)}) collective-permute-start(f32[96,128]{1,0:T(8,128)S(1)} %get-tuple-element.51), channel_id=1, source_target_pairs={{0,16},{4,20},{8,24},{12,28},{16,0},{20,4},{24,8},{28,12},{1,17},{... | collective-permute-start | bytes 147464 | tf_op jit(solution)/shard_map/ppermute | solution.py:582
  27.2 3.8 %collective-permute-start.11 = (f32[24,128]{1,0:T(8,128)S(1)}, f32[24,128]{1,0:T(8,128)S(1)}, u32[]{:S(2)}, u32[]{:S(2)}) collective-permute-start(f32[24,128]{1,0:T(8,128)S(1)} %get-tuple-element.65), channel_id=1, source_target_pairs={{0,1},{1,0},{2,3},{3,2},{4,5},{5,4},{6,7},{7,6},{8,9},{9,8},{10,11... | collective-permute-start | bytes 36872 | tf_op jit(solution)/shard_map/ppermute | solution.py:594
  29.1 1.8 %copy-start.4 = (f32[8,8,128]{2,1,0:T(8,128)S(1)}, f32[8,8,128]{2,1,0:T(8,128)}, u32[]{:S(2)}) copy-start(f32[8,8,128]{2,1,0:T(8,128)} %momentum.1) | copy-start | bytes 98308
  29.1 1.8 %collective-permute-start.12 = (f32[24,128]{1,0:T(8,128)S(1)}, f32[24,128]{1,0:T(8,128)S(1)}, u32[]{:S(2)}, u32[]{:S(2)}) collective-permute-start(f32[24,128]{1,0:T(8,128)S(1)} %get-tuple-element.66), channel_id=1, source_target_pairs={{0,4},{1,2},{2,1},{3,7},{4,0},{5,6},{6,5},{7,3},{8,12},{9,10},{10,... | collective-permute-start | bytes 36872 | tf_op jit(solution)/shard_map/ppermute | solution.py:593

commit v5 on v4

--- a/solution.py
+++ b/solution.py
@@ -154,7 +154,7 @@
 
 def partial_body(
     state, velocity, cells, residuals, kappa, source_cells, source_codes, wavelets,
-    partial_u, image, partial_q, push, tap_u, weight, out_b, out_a, third_b, third_a,
+    partial_u, image, partial_q, push_u, push, tap_u, weight, out_b, out_a, third_b, third_a,
     field_u, field_q, grid_now, cells_here, codes_here, wavelets_here, sems, *, scale,
 ):
     small = [(source_cells, cells_here), (source_codes, codes_here), (wavelets, wavelets_here)]
@@ -166,8 +166,8 @@
         tail = kappa[j, depth - 1]
         head = kappa[j, 0]
         at = RADIUS * size_x + j * strip
-        out_a[at : at + strip, :] = jnp.where(even, tail, head)
-        out_b[at : at + strip, :] = jnp.where(even, head, tail)
+        third_a[at : at + strip, :] = jnp.where(even, tail, head)
+        third_b[at : at + strip, :] = jnp.where(even, head, tail)
     for which, field in ((0, field_u), (1, field_q)):
         clear_sides(field, size_x)
         for z in range(depth):
@@ -205,6 +205,7 @@
         partial_q[z] = (2.0 * state[1, 0, 1, z] - state[0, 0, 1, z]) + drive
         push[z] = vv * grid_now[1, at, :]
         weight[z] = -0.2 / (v * scale)
+        push_u[z] = jnp.zeros((size_x, size_y), F32)
 
     def inject(z, x, spot):
         @pl.when((z >= 0) & (z < depth))
@@ -215,10 +216,18 @@
             partial_u[at] = partial_u[at] + change
             image[at] = image[at] + change * state[1, 0, 1, z, pl.ds(x, 1), :]
 
+    def inject_next(z, x, spot):
+        @pl.when((z >= 0) & (z < depth))
+        def _():
+            at = (z, pl.ds(x, 1), slice(None))
+            v = velocity[at]
+            push_u[at] = push_u[at] + (v * v) * spot
+
     for copy in copies:
         copy.wait()
     first_layer = lax.axis_index("slab") * depth
     point_cells(cells_here, codes_here, wavelets_here, 0, first_layer, size_x, size_y, inject)
+    point_cells(cells_here, codes_here, wavelets_here, 1, first_layer, size_x, size_y, inject_next)
     for k in range(2 * RADIUS):
         tap_u[k] = weighted([(r, state[1, 0, 0, own]) for r, own in halo_near(k, depth)])
     for source, to_a, to_b in ((partial_u, out_a, out_b), (partial_q, third_a, third_b)):
@@ -260,11 +269,9 @@
 
 
 def near_body(
-    state, velocity, partial_u, image0, partial_q, weight, first_a, first_b, cells, codes, wavelets,
-    u_part, q_next, image, gain,
-    u_edge, q_edge, u_now, cells_here, codes_here, wavelets_here, sems,
+    state, velocity, partial_u, image0, partial_q, push, weight, first_a, first_b,
+    u_part, q_next, image, gain, u_edge, q_edge, u_now,
 ):
-    small = run_copies([(cells, cells_here), (codes, codes_here), (wavelets, wavelets_here)], sems)
     depth, size_x, size_y = velocity.shape
     even = lax.rem(lax.axis_index("slab"), 2) == 0
     border = at_border()
@@ -289,28 +296,15 @@
         image[z] = image0[z] + change * state[1, 0, 1, z]
         q_next[z] = partial_q[z] + vv * weighted([(r, q_edge[k]) for r, k in near])
 
-    def second_step(z, x, spot):
-        @pl.when((z >= 0) & (z < depth))
-        def _():
-            at = (z, pl.ds(x, 1), slice(None))
-            v = velocity[at]
-            change = (v * v) * spot
-            u_part[at] = u_part[at] + change
-            image[at] = image[at] + weight[at] * (change * q_next[at])
-
     lane = lax.broadcasted_iota(jnp.int32, (size_x, size_y), 1)
     for z in range(depth):
         v = velocity[z]
         vv = v * v
         adjoint = q_next[z]
-        drive = vv * laplacian_row(u_now, z, depth, size_x, size_y, lane)
+        drive = vv * laplacian_row(u_now, z, depth, size_x, size_y, lane) + push[z]
         u_part[z] = (2.0 * u_now[z, middle, :] - state[1, 0, 0, z]) + drive
         image[z] = weight[z] * (image[z] + drive * adjoint)
         gain[z] = (weight[z] * vv) * adjoint
-    for copy in small:
-        copy.wait()
-    first_layer = lax.axis_index("slab") * depth
-    point_cells(cells_here, codes_here, wavelets_here, 1, first_layer, size_x, size_y, second_step)
 
 
 def halo_field(halo, second_b, second_a, tap, share_own, share_got):
@@ -327,7 +321,7 @@
 
 def image_body(
     velocity, kappa, u_part, image_own, gain, tap_u, share_own, share_got, second_b, second_a,
-    fields, keep, packed, halo, image, u_out, out_sem,
+    u_out, keep, packed, halo, image,
 ):
     depth, size_x, size_y = velocity.shape
     core = lax.rem(lax.axis_index("shot"), 2)
@@ -344,8 +338,6 @@
         crossing = weighted([(r, halo[k]) for r, k in near])
         u_out[z] = u_part[z] + (v * v) * crossing
         image[z, middle, :] = image_own[z] + gain[z] * crossing
-    copy_out = pltpu.make_async_copy(u_out, fields.at[0, 0], out_sem)
-    copy_out.start()
     chip = lax.div(lax.axis_index("shot"), 2)
     chips = keep.shape[0]
     strip = size_x // (2 * chips)
@@ -365,7 +357,6 @@
         at = chips * rows + j * depth
         packed[at : at + depth, :] = jnp.where(core == 0, tail, head)
         packed[at + 3 * depth : at + 4 * depth, :] = jnp.where(core == 0, head, tail)
-    copy_out.wait()
 
 
 def hands_on(k):
@@ -396,8 +387,10 @@
 
 
 def adjoint_body(
-    fields_in, state, velocity, q_next, push, share_own, share_got, third_b, third_a, fields, field, tap, halo, q_out, out_sem
+    state, velocity, u_out, q_next, push, share_own, share_got, third_b, third_a, fields, field, tap, halo, q_out, sems
 ):
+    copy_u = pltpu.make_async_copy(u_out, fields.at[0, 0], sems.at[0])
+    copy_u.start()
     depth, size_x, size_y = velocity.shape
     whole = depth + 2 * RADIUS
     middle = slice(PAD, PAD + size_x)
@@ -413,12 +406,13 @@
         v = velocity[z]
         drive = (v * v) * laplacian_row(field, z + RADIUS, whole, size_x, size_y, lane) + push[z]
         q_out[z] = (2.0 * q_next[z] - state[1, 0, 1, z]) + drive
-    copy = pltpu.make_async_copy(q_out, fields.at[0, 1], out_sem)
-    copy.start()
-    copy.wait()
-
-
-def coefficient_body(kappa, second_b, second_a, got, *rest, size_x, distances):
+    copy_q = pltpu.make_async_copy(q_out, fields.at[0, 1], sems.at[1])
+    copy_q.start()
+    copy_u.wait()
+    copy_q.wait()
+
+
+def coefficient_body(kappa, third_b, third_a, got, *rest, size_x, distances):
     arrived, coef = rest[:-1], rest[-1]
     _, depth, strip, _ = kappa.shape
     even = lax.rem(lax.axis_index("slab"), 2) == 0
@@ -437,8 +431,8 @@
     coef[...] = jnp.zeros(coef.shape, F32)
     for j in range(3):
         at = slice(RADIUS * size_x + j * strip, RADIUS * size_x + (j + 1) * strip)
-        coef[j, 0, 1 : strip + 1, :] = ahead(even, border, second_a[at, :], second_b[at, :])
-        coef[j, depth + 1, 1 : strip + 1, :] = after(even, border, second_a[at, :], second_b[at, :])
+        coef[j, 0, 1 : strip + 1, :] = ahead(even, border, third_a[at, :], third_b[at, :])
+        coef[j, depth + 1, 1 : strip + 1, :] = after(even, border, third_a[at, :], third_b[at, :])
         of = slice(j * depth, (j + 1) * depth)
         left = ahead(even_strip, end_strip, facing[of, :], far[of, :])
         right = after(even_strip, end_strip, facing[of, :], far[of, :])
@@ -512,8 +506,8 @@
     first_b = lax.ppermute(out_b, both, z_odd)
     first_a = lax.ppermute(out_a, "slab", z_even)
 
-    flat = shape(RADIUS * size_x + 3 * strip, size_y)
-    flat_q = shape(RADIUS * size_x, size_y)
+    flat = shape(RADIUS * size_x, size_y)
+    flat_q = shape(RADIUS * size_x + 3 * strip, size_y)
     edge = shape(RADIUS, size_x, size_y)
     ring = shape(2 * RADIUS, size_x, size_y)
     ring_scratch = pltpu.VMEM(ring.shape, F32)
@@ -521,12 +515,12 @@
         pltpu.with_memory_space_constraint(x, pltpu.HBM) for x in (source_cells, source_codes, wavelets.T)
     )
     small_scratch = [pltpu.SMEM(x.shape, x.dtype) for x in small] + [dma((3,))]
-    partial_u, image0, partial_q, push, tap_u, weight, out_b, out_a, third_b, third_a = call(
+    partial_u, image0, partial_q, push_u, push, tap_u, weight, out_b, out_a, third_b, third_a = call(
         functools.partial(partial_body, scale=math.sqrt(shots * STEPS)),
-        [shape(*cube)] * 4 + [ring, shape(*cube), flat, flat, flat_q, flat_q],
+        [shape(*cube)] * 5 + [ring, shape(*cube), flat, flat, flat_q, flat_q],
         (wave_state, velocity, receiver_cells, residuals, diffusivity, *small),
         ["vmem"] * 5 + ["hbm"] * 3,
-        ["vmem"] * 10,
+        ["vmem"] * 11,
         [pltpu.VMEM(padded, F32)] * 2 + [pltpu.VMEM((STEPS, depth * size_x, size_y), F32)] + small_scratch,
         us=1.7,
     )
@@ -540,39 +534,38 @@
     u_part, q_next, image_own, gain = call(
         near_body,
         [shape(*cube)] * 4,
-        (wave_state, velocity, partial_u, image0, partial_q, weight, first_a, first_b, *small),
-        ["vmem"] * 8 + ["hbm"] * 3,
+        (wave_state, velocity, partial_u, image0, partial_q, push_u, weight, first_a, first_b),
+        ["vmem"] * 9,
         ["vmem"] * 4,
-        [ring_scratch] * 2 + [pltpu.VMEM(padded, F32)] + small_scratch,
-        us=1.2,
+        [ring_scratch] * 2 + [pltpu.VMEM(padded, F32)],
+        us=0.8,
     )
 
     part = shape(chips, depth * wide, size_y)
     side = 3 * depth
-    fields, keep, send = call(
+    u_out, keep, send = call(
         image_body,
-        [shape(1, 2, *cube), part, shape(chips * depth * wide + 2 * side, size_y)],
+        [shape(*cube), part, shape(chips * depth * wide + 2 * side, size_y)],
         (velocity, diffusivity, u_part, image_own, gain, tap_u, share_own, share_got, second_b, second_a),
         ["vmem"] * 10,
-        ["any"] + ["vmem"] * 2,
-        [ring_scratch, pltpu.VMEM(padded, F32), pltpu.VMEM(cube, F32), dma],
-        us=1.0,
+        ["vmem"] * 3,
+        [ring_scratch, pltpu.VMEM(padded, F32)],
+        us=0.3,
     )
     got = lax.ppermute(send, "shot", even_pairs(shots))
     (fields,) = call(
         adjoint_body,
         [shape(1, 2, *cube)],
-        (fields, wave_state, velocity, q_next, push, share_own, share_got, third_b, third_a),
-        ["any"] + ["vmem"] * 8,
+        (wave_state, velocity, u_out, q_next, push, share_own, share_got, third_b, third_a),
+        ["vmem"] * 9,
         ["any"],
         [
             pltpu.VMEM((depth + 2 * RADIUS, size_x + 2 * PAD, size_y), F32),
             ring_scratch,
             ring_scratch,
             pltpu.VMEM(cube, F32),
-            dma,
+            dma((2,)),
         ],
-        aliases={0: 0},
         us=1.4,
     )
     row_block = shape(depth * wide, size_y)
@@ -597,7 +590,7 @@
     (coef,) = call(
         functools.partial(coefficient_body, size_x=size_x, distances=distances),
         [shape(3, depth + 2, tall, size_y)],
-        (diffusivity, second_b, second_a, got, *(arrived[chips - 1 - k] for k in distances)),
+        (diffusivity, third_b, third_a, got, *(arrived[chips - 1 - k] for k in distances)),
         ["vmem"] * (4 + len(distances)),
         ["vmem"],
         us=0.1,

time: 32 us -> 31.1 us (0.972)
  Pallas kernels: 8.07 us -> 6.89 us
    pallas_call x10, Pallas kernels: 8.07 us -> 6.89 us  [call(): pl.pallas_call(body, out_shape=list(out_shapes), in_specs=[SPECS[s] for s...]
    ppermute x1, waiting for transfers between devices: 1.08 us -> 1.46 us  [on_device(): second_a = lax.ppermute(out_a, 'slab', z_even)]
  transfers between devices with their start and end apart: 13 -> 13, of which waited for: 5 -> 5; matrix products, arithmetic and copies ran while one was open for 0% -> 0% of each run, Pallas kernels for 16% -> 14%
where the time goes in v5:
time: 31.1 us; the launch traced here: 30.9 us
  starting transfers between devices  15 us (48%)
  Pallas kernels  6.89 us (22%)
  waiting for transfers between devices  6.6 us (21%)
  local copies, waits for them, and re-layouts  1.57 us (5%)
  between operations  0.77 us (2%)
    pallas_call x10, Pallas kernels, call(): pl.pallas_call(body, out_shape=list(out_shapes), in_specs=[SPECS[s] for s...  6.89 us
    ppermute x3, starting transfers between devices, on_device(): lax.ppermute(parts[k], 'shot', [(i, i ^ 2 * k) for i in range(shots)])  3.55 us
    ppermute x1, starting transfers between devices, on_device(): second_a = lax.ppermute(out_a, 'slab', z_even)  3.14 us
    ppermute x1, starting transfers between devices, on_device(): first_a = lax.ppermute(out_a, 'slab', z_even)  3.09 us
    ppermute x1, starting transfers between devices, on_device(): third_a = lax.ppermute(third_a, 'slab', z_even)  2.95 us
    ppermute x1, starting transfers between devices, on_device(): grad_a = lax.ppermute(out_a, 'slab', z_even)  1.9 us
    ppermute x1, waiting for transfers between devices, on_device(): grad_a = lax.ppermute(out_a, 'slab', z_even)  1.82 us
    unnamed x14, local copies, waits for them, and re-layouts  1.57 us
  transfers between devices with their start and end apart: 13, of which 5 were waited for; matrix products, arithmetic and copies ran while one was open for 0% of the time, Pallas kernels for 14%

profile of v5, /device:TPU:0, one launch (start us, length us, event | category | flops | bytes accessed | tf_op | source)
XLA Modules:
  0.0 30.9 jit_solution(1666294192834010148)
XLA Ops:
  0.6 1.3 %shard_map.113 = (f32[10,64,128]{2,1,0:T(8,128)S(1)}, f32[10,64,128]{2,1,0:T(8,128)S(1)}) custom-call(f32[2,1,2,8,64,128]{5,4,3,2,1,0:T(8,128)} %state.7, f32[8,64,128]{2,1,0:T(8,128)} %velocity.11), custom_call_target="tpu_custom_call" | custom-call | bytes 4797000 | tf_op jit(solution)/shard_map/pallas_call | solution.py:69
  2.0 3.1 %collective-permute-start = (f32[10,64,128]{2,1,0:T(8,128)S(1)}, f32[10,64,128]{2,1,0:T(8,128)S(1)}, u32[]{:S(2)}, u32[]{:S(2)}) collective-permute-start(f32[10,64,128]{2,1,0:T(8,128)S(1)} %get-tuple-element.42), channel_id=1, source_target_pairs={{0,1},{1,0},{2,3},{3,2},{4,5},{5,4},{6,7},{7,6},{8,9},{9,8},{10,11... | collective-permute-start | bytes 983048 | tf_op jit(solution)/shard_map/ppermute | solution.py:507
  5.1 0.7 %copy-done.6 = s32[1,256]{1,0:T(1,128)S(1)} copy-done((s32[1,256]{1,0:T(1,128)S(1)}, s32[1,256]{1,0:T(1,128)}, u32[]{:S(2)}) %copy-start.6) | copy-done | bytes 1048
  5.8 0.9 %copy-done.2 = f32[3,8,8,128]{3,2,1,0:T(8,128)S(1)} copy-done((f32[3,8,8,128]{3,2,1,0:T(8,128)S(1)}, f32[3,8,8,128]{3,2,1,0:T(8,128)}, u32[]{:S(2)}) %copy-start.2) | copy-done | bytes 98328
  6.7 2.2 %shard_map.112 = (f32[8,64,128]{2,1,0:T(8,128)S(1)}, f32[8,64,128]{2,1,0:T(8,128)S(1)}, f32[8,64,128]{2,1,0:T(8,128)S(1)}, f32[8,64,128]{2,1,0:T(8,128)S(1)}, f3...) custom-call(f32[2,1,2,8,64,128]{5,4,3,2,1,0:T(8,128)S(1)} %copy-done, ...), custom_call_target="tpu_custom_call" | custom-call | bytes 6273000 | tf_op jit(solution)/shard_map/pallas_call | solution.py:69
  8.9 0.1 collective-permute-start.3
  9.0 3.1 %collective-permute-start.4 = (f32[256,128]{1,0:T(8,128)S(1)}, f32[256,128]{1,0:T(8,128)S(1)}, u32[]{:S(2)}, u32[]{:S(2)}) collective-permute-start(f32[256,128]{1,0:T(8,128)S(1)} %get-tuple-element.49), channel_id=1, source_target_pairs={{0,1},{1,0},{2,3},{3,2},{4,5},{5,4},{6,7},{7,6},{8,9},{9,8},{10,11... | collective-permute-start | bytes 393224 | tf_op jit(solution)/shard_map/ppermute | solution.py:528
  12.1 1.2 %collective-permute-done.first_a = f32[10,64,128]{2,1,0:T(8,128)S(1)} collective-permute-done((f32[10,64,128]{2,1,0:T(8,128)S(1)}, f32[10,64,128]{2,1,0:T(8,128)S(1)}, u32[]{:S(2)}, u32[]{:S(2)}) %collective-permute-start) | collective-permute-done | bytes 327712 | tf_op jit(solution)/shard_map/ppermute | solution.py:507
  13.3 0.1 collective-permute-start.2
  13.4 0.8 %shard_map.114 = (f32[8,64,128]{2,1,0:T(8,128)S(1)}, f32[8,64,128]{2,1,0:T(8,128)S(1)}, f32[8,64,128]{2,1,0:T(8,128)S(1)}, f32[8,64,128]{2,1,0:T(8,128)S(1)}) custom-call(f32[2,1,2,8,64,128]{5,4,3,2,1,0:T(8,128)S(1)} %copy-done, f32[8,64,128]{2,1,0:T(8,128)S(1)} %copy-done.1, f32[8,64,128]{2,1,0:T(8,128)S(1)} %get-tuple-element.37.partial_u, ...), custom_call_target="tpu_custom_call" | custom-call | bytes 2952000 | tf_op jit(solution)/shard_map/pallas_call | solution.py:69
  14.1 1.5 %collective-permute-done.4.second_a = f32[256,128]{1,0:T(8,128)S(1)} collective-permute-done((f32[256,128]{1,0:T(8,128)S(1)}, f32[256,128]{1,0:T(8,128)S(1)}, u32[]{:S(2)}, u32[]{:S(2)}) %collective-permute-start.4) | collective-permute-done | bytes 131104 | tf_op jit(solution)/shard_map/ppermute | solution.py:528
  15.6 0.2 shard_map.116
  15.9 0.1 collective-permute-start.5
  15.9 3.0 %collective-permute-start.10 = (f32[280,128]{1,0:T(8,128)S(1)}, f32[280,128]{1,0:T(8,128)S(1)}, u32[]{:S(2)}, u32[]{:S(2)}) collective-permute-start(f32[280,128]{1,0:T(8,128)S(1)} %get-tuple-element.60), channel_id=1, source_target_pairs={{0,1},{1,0},{2,3},{3,2},{4,5},{5,4},{6,7},{7,6},{8,9},{9,8},{10,11... | collective-permute-start | bytes 430088 | tf_op jit(solution)/shard_map/ppermute | solution.py:530
  18.9 0.2 collective-permute-start.9
  19.1 2.5 %collective-permute-start.6 = (f32[120,128]{1,0:T(8,128)S(1)}, f32[120,128]{1,0:T(8,128)S(1)}, u32[]{:S(2)}, u32[]{:S(2)}) collective-permute-start(f32[120,128]{1,0:T(8,128)S(1)} %get-tuple-element.52), channel_id=1, source_target_pairs={{0,24},{4,28},{8,16},{12,20},{16,8},{20,12},{24,0},{28,4},{1,25},{... | collective-permute-start | bytes 184328 | tf_op jit(solution)/shard_map/ppermute | solution.py:575
  21.6 0.5 %collective-permute-start.8 = (f32[120,128]{1,0:T(8,128)S(1)}, f32[120,128]{1,0:T(8,128)S(1)}, u32[]{:S(2)}, u32[]{:S(2)}) collective-permute-start(f32[120,128]{1,0:T(8,128)S(1)} %get-tuple-element.54), channel_id=1, source_target_pairs={{0,8},{4,12},{8,0},{12,4},{16,24},{20,28},{24,16},{28,20},{1,9},{5... | collective-permute-start | bytes 184328 | tf_op jit(solution)/shard_map/ppermute | solution.py:575
  22.1 0.5 %collective-permute-start.7 = (f32[96,128]{1,0:T(8,128)S(1)}, f32[96,128]{1,0:T(8,128)S(1)}, u32[]{:S(2)}, u32[]{:S(2)}) collective-permute-start(f32[96,128]{1,0:T(8,128)S(1)} %get-tuple-element.53), channel_id=1, source_target_pairs={{0,16},{4,20},{8,24},{12,28},{16,0},{20,4},{24,8},{28,12},{1,17},{... | collective-permute-start | bytes 147464 | tf_op jit(solution)/shard_map/ppermute | solution.py:575
  22.6 0.6 %collective-permute-done.10.third_a = f32[280,128]{1,0:T(8,128)S(1)} collective-permute-done((f32[280,128]{1,0:T(8,128)S(1)}, f32[280,128]{1,0:T(8,128)S(1)}, u32[]{:S(2)}, u32[]{:S(2)}) %collective-permute-start.10) | collective-permute-done | bytes 143392 | tf_op jit(solution)/shard_map/ppermute | solution.py:530
  23.2 1.4 %shard_map.118 = f32[1,2,8,64,128]{4,3,2,1,0:T(8,128)} custom-call(f32[2,1,2,8,64,128]{5,4,3,2,1,0:T(8,128)S(1)} %copy-done, f32[8,64,128]{2,1,0:T(8,128)S(1)} %copy-done.1, f32[8,64,128]{2,1,0:T(8,128)S(1)} %get-tuple-element.56.u_out, f32[8,64,128]{2,1,0:T(8,128)S(1)} %get-tuple-element.57.q_next, f32[8,64,128]{2,1,0:T(8,128)S(1)} %get-tuple-element.58.push, ...), custom_call_target="tpu_custom_call" | custom-call | bytes 5166000 | tf_op jit(solution)/shard_map/pallas_call | solution.py:69
  24.7 1.6 %collective-permute-done.7.refs_1_ = f32[96,128]{1,0:T(8,128)S(1)} collective-permute-done((f32[96,128]{1,0:T(8,128)S(1)}, f32[96,128]{1,0:T(8,128)S(1)}, u32[]{:S(2)}, u32[]{:S(2)}) %collective-permute-start.7) | collective-permute-done | bytes 49184 | tf_op jit(solution)/shard_map/ppermute | solution.py:575
  26.3 1.9 %collective-permute-start.11 = (f32[24,128]{1,0:T(8,128)S(1)}, f32[24,128]{1,0:T(8,128)S(1)}, u32[]{:S(2)}, u32[]{:S(2)}) collective-permute-start(f32[24,128]{1,0:T(8,128)S(1)} %get-tuple-element.67), channel_id=1, source_target_pairs={{0,1},{1,0},{2,3},{3,2},{4,5},{5,4},{6,7},{7,6},{8,9},{9,8},{10,11... | collective-permute-start | bytes 36872 | tf_op jit(solution)/shard_map/ppermute | solution.py:587
  28.2 1.8 %collective-permute-done.11.got_a = f32[24,128]{1,0:T(8,128)S(1)} collective-permute-done((f32[24,128]{1,0:T(8,128)S(1)}, f32[24,128]{1,0:T(8,128)S(1)}, u32[]{:S(2)}, u32[]{:S(2)}) %collective-permute-start.11) | collective-permute-done | bytes 12320 | tf_op jit(solution)/shard_map/ppermute | solution.py:587
  30.0 0.8 %shard_map.121 = (f32[8,8,128]{2,1,0:T(8,128)}, f32[8,8,128]{2,1,0:T(8,128)}) custom-call(f32[96,128]{1,0:T(8,128)S(1)} %get-tuple-element.66.total, f32[24,128]{1,0:T(8,128)S(1)} %collective-permute-done.11.got_a, f32[24,128]{1,0:T(8,128)S(1)} %collective-permute-done.12.got_b, f32[3,8,8,128]{3,2,1,0:T(8,128)S(1)} %copy-done.3, ...), custom_call_target="tpu_custom_call" | custom-call | bytes 2583000 | tf_op jit(solution)/shard_map/pallas_call | solution.py:69
  (26 shorter events, 0.1 us)
Async XLA Ops:
  0.6 4.5 %copy-start = (f32[2,1,2,8,64,128]{5,4,3,2,1,0:T(8,128)S(1)}, f32[2,1,2,8,64,128]{5,4,3,2,1,0:T(8,128)}, u32[]{:S(2)}) copy-start(f32[2,1,2,8,64,128]{5,4,3,2,1,0:T(8,128)} %state.7) | copy-start | bytes 3145732
  0.6 4.5 %copy-start.1 = (f32[8,64,128]{2,1,0:T(8,128)S(1)}, f32[8,64,128]{2,1,0:T(8,128)}, u32[]{:S(2)}) copy-start(f32[8,64,128]{2,1,0:T(8,128)} %velocity.11) | copy-start | bytes 786436
  2.0 3.1 %copy-start.5 = (f32[1,2,256]{2,1,0:T(2,128)S(1)}, f32[1,2,256]{2,1,0:T(2,128)}, u32[]{:S(2)}) copy-start(f32[1,2,256]{2,1,0:T(2,128)} %residuals.1) | copy-start | bytes 6148
  2.0 11.3 %collective-permute-start = (f32[10,64,128]{2,1,0:T(8,128)S(1)}, f32[10,64,128]{2,1,0:T(8,128)S(1)}, u32[]{:S(2)}, u32[]{:S(2)}) collective-permute-start(f32[10,64,128]{2,1,0:T(8,128)S(1)} %get-tuple-element.42), channel_id=1, source_target_pairs={{0,1},{1,0},{2,3},{3,2},{4,5},{5,4},{6,7},{7,6},{8,9},{9,8},{10,11... | collective-permute-start | bytes 983048 | tf_op jit(solution)/shard_map/ppermute | solution.py:507
  5.1 0.7 %copy-start.6 = (s32[1,256]{1,0:T(1,128)S(1)}, s32[1,256]{1,0:T(1,128)}, u32[]{:S(2)}) copy-start(s32[1,256]{1,0:T(1,128)} %cells.1) | copy-start | bytes 3076
  5.1 8.2 %collective-permute-start.1 = (f32[10,64,128]{2,1,0:T(8,128)S(1)}, f32[10,64,128]{2,1,0:T(8,128)S(1)}, u32[]{:S(2)}, u32[]{:S(2)}) collective-permute-start(f32[10,64,128]{2,1,0:T(8,128)S(1)} %get-tuple-element.43), channel_id=1, source_target_pairs={{0,4},{1,2},{2,1},{3,7},{4,0},{5,6},{6,5},{7,3},{8,12},{9,10},{10,... | collective-permute-start | bytes 983048 | tf_op jit(solution)/shard_map/ppermute | solution.py:506
  5.8 0.9 %copy-start.2 = (f32[3,8,8,128]{3,2,1,0:T(8,128)S(1)}, f32[3,8,8,128]{3,2,1,0:T(8,128)}, u32[]{:S(2)}) copy-start(f32[3,8,8,128]{3,2,1,0:T(8,128)} %kappa.7) | copy-start | bytes 294916
  8.9 5.2 %collective-permute-start.3 = (f32[256,128]{1,0:T(8,128)S(1)}, f32[256,128]{1,0:T(8,128)S(1)}, u32[]{:S(2)}, u32[]{:S(2)}) collective-permute-start(f32[256,128]{1,0:T(8,128)S(1)} %get-tuple-element.48), channel_id=1, source_target_pairs={{0,4},{1,2},{2,1},{3,7},{4,0},{5,6},{6,5},{7,3},{8,12},{9,10},{10,... | collective-permute-start | bytes 393224 | tf_op jit(solution)/shard_map/ppermute | solution.py:527
  9.0 6.6 %collective-permute-start.4 = (f32[256,128]{1,0:T(8,128)S(1)}, f32[256,128]{1,0:T(8,128)S(1)}, u32[]{:S(2)}, u32[]{:S(2)}) collective-permute-start(f32[256,128]{1,0:T(8,128)S(1)} %get-tuple-element.49), channel_id=1, source_target_pairs={{0,1},{1,0},{2,3},{3,2},{4,5},{5,4},{6,7},{7,6},{8,9},{9,8},{10,11... | collective-permute-start | bytes 393224 | tf_op jit(solution)/shard_map/ppermute | solution.py:528
  13.3 2.3 %collective-permute-start.2 = (f32[4,64,128]{2,1,0:T(8,128)S(1)}, f32[4,64,128]{2,1,0:T(8,128)S(1)}, u32[]{:S(2)}, u32[]{:S(2)}) collective-permute-start(f32[4,64,128]{2,1,0:T(8,128)S(1)} %shard_map.115.share_own), channel_id=1, source_target_pairs={{0,4},{4,0},{8,12},{12,8},{16,20},{20,16},{24,28},{28,24},{1,5},{5... | collective-permute-start | bytes 393224 | tf_op jit(solution)/shard_map/ppermute | solution.py:533
  13.4 2.2 %copy-start.3 = (f32[3,8,8,128]{3,2,1,0:T(8,128)S(1)}, f32[3,8,8,128]{3,2,1,0:T(8,128)}, u32[]{:S(2)}) copy-start(f32[3,8,8,128]{3,2,1,0:T(8,128)} %kappa.7) | copy-start | bytes 294916
  15.9 3.2 %collective-permute-start.5 = (f32[432,128]{1,0:T(8,128)S(1)}, f32[432,128]{1,0:T(8,128)S(1)}, u32[]{:S(2)}, u32[]{:S(2)}) collective-permute-start(f32[432,128]{1,0:T(8,128)S(1)} %get-tuple-element.51), channel_id=1, source_target_pairs={{0,4},{4,0},{8,12},{12,8},{16,20},{20,16},{24,28},{28,24},{1,5},{5... | collective-permute-start | bytes 663560 | tf_op jit(solution)/shard_map/ppermute | solution.py:555
  15.9 7.3 %collective-permute-start.10 = (f32[280,128]{1,0:T(8,128)S(1)}, f32[280,128]{1,0:T(8,128)S(1)}, u32[]{:S(2)}, u32[]{:S(2)}) collective-permute-start(f32[280,128]{1,0:T(8,128)S(1)} %get-tuple-element.60), channel_id=1, source_target_pairs={{0,1},{1,0},{2,3},{3,2},{4,5},{5,4},{6,7},{7,6},{8,9},{9,8},{10,11... | collective-permute-start | bytes 430088 | tf_op jit(solution)/shard_map/ppermute | solution.py:530
  18.9 4.4 %collective-permute-start.9 = (f32[280,128]{1,0:T(8,128)S(1)}, f32[280,128]{1,0:T(8,128)S(1)}, u32[]{:S(2)}, u32[]{:S(2)}) collective-permute-start(f32[280,128]{1,0:T(8,128)S(1)} %get-tuple-element.59), channel_id=1, source_target_pairs={{0,4},{1,2},{2,1},{3,7},{4,0},{5,6},{6,5},{7,3},{8,12},{9,10},{10,... | collective-permute-start | bytes 430088 | tf_op jit(solution)/shard_map/ppermute | solution.py:529
  19.1 7.1 %collective-permute-start.6 = (f32[120,128]{1,0:T(8,128)S(1)}, f32[120,128]{1,0:T(8,128)S(1)}, u32[]{:S(2)}, u32[]{:S(2)}) collective-permute-start(f32[120,128]{1,0:T(8,128)S(1)} %get-tuple-element.52), channel_id=1, source_target_pairs={{0,24},{4,28},{8,16},{12,20},{16,8},{20,12},{24,0},{28,4},{1,25},{... | collective-permute-start | bytes 184328 | tf_op jit(solution)/shard_map/ppermute | solution.py:575
  21.6 4.6 %collective-permute-start.8 = (f32[120,128]{1,0:T(8,128)S(1)}, f32[120,128]{1,0:T(8,128)S(1)}, u32[]{:S(2)}, u32[]{:S(2)}) collective-permute-start(f32[120,128]{1,0:T(8,128)S(1)} %get-tuple-element.54), channel_id=1, source_target_pairs={{0,8},{4,12},{8,0},{12,4},{16,24},{20,28},{24,16},{28,20},{1,9},{5... | collective-permute-start | bytes 184328 | tf_op jit(solution)/shard_map/ppermute | solution.py:575
  22.1 4.1 %collective-permute-start.7 = (f32[96,128]{1,0:T(8,128)S(1)}, f32[96,128]{1,0:T(8,128)S(1)}, u32[]{:S(2)}, u32[]{:S(2)}) collective-permute-start(f32[96,128]{1,0:T(8,128)S(1)} %get-tuple-element.53), channel_id=1, source_target_pairs={{0,16},{4,20},{8,24},{12,28},{16,0},{20,4},{24,8},{28,12},{1,17},{... | collective-permute-start | bytes 147464 | tf_op jit(solution)/shard_map/ppermute | solution.py:575
  26.3 3.8 %collective-permute-start.11 = (f32[24,128]{1,0:T(8,128)S(1)}, f32[24,128]{1,0:T(8,128)S(1)}, u32[]{:S(2)}, u32[]{:S(2)}) collective-permute-start(f32[24,128]{1,0:T(8,128)S(1)} %get-tuple-element.67), channel_id=1, source_target_pairs={{0,1},{1,0},{2,3},{3,2},{4,5},{5,4},{6,7},{7,6},{8,9},{9,8},{10,11... | collective-permute-start | bytes 36872 | tf_op jit(solution)/shard_map/ppermute | solution.py:587
  28.2 1.9 %copy-start.4 = (f32[8,8,128]{2,1,0:T(8,128)S(1)}, f32[8,8,128]{2,1,0:T(8,128)}, u32[]{:S(2)}) copy-start(f32[8,8,128]{2,1,0:T(8,128)} %momentum.1) | copy-start | bytes 98308
  28.2 1.9 %collective-permute-start.12 = (f32[24,128]{1,0:T(8,128)S(1)}, f32[24,128]{1,0:T(8,128)S(1)}, u32[]{:S(2)}, u32[]{:S(2)}) collective-permute-start(f32[24,128]{1,0:T(8,128)S(1)} %get-tuple-element.68), channel_id=1, source_target_pairs={{0,4},{1,2},{2,1},{3,7},{4,0},{5,6},{6,5},{7,3},{8,12},{9,10},{10,... | collective-permute-start | bytes 36872 | tf_op jit(solution)/shard_map/ppermute | solution.py:586

commit v6 on v5

--- a/solution.py
+++ b/solution.py
@@ -154,7 +154,7 @@
 
 def partial_body(
     state, velocity, cells, residuals, kappa, source_cells, source_codes, wavelets,
-    partial_u, image, partial_q, push_u, push, tap_u, weight, out_b, out_a, third_b, third_a,
+    partial_u, image, partial_q, push_u, push, tap_u, weight, out_b, out_a, third_b, third_a, far,
     field_u, field_q, grid_now, cells_here, codes_here, wavelets_here, sems, *, scale,
 ):
     small = [(source_cells, cells_here), (source_codes, codes_here), (wavelets, wavelets_here)]
@@ -162,7 +162,9 @@
     depth, size_x, size_y = velocity.shape
     strip = kappa.shape[2]
     even = lax.rem(lax.axis_index("slab"), 2) == 0
+    core = lax.rem(lax.axis_index("shot"), 2)
     for j in range(3):
+        far[j * depth : (j + 1) * depth, :] = jnp.where(core == 0, kappa[j, :, 0, :], kappa[j, :, strip - 1, :])
         tail = kappa[j, depth - 1]
         head = kappa[j, 0]
         at = RADIUS * size_x + j * strip
@@ -352,32 +354,22 @@
             keep[to, z * wide : (z + 1) * wide, :] = jnp.where(core == 0, low, high)
             packed[pl.ds(to * rows + z * wide, wide), :] = jnp.where(core == 0, high, low)
     for j in range(3):
-        tail = kappa[j, :, strip - 1, :]
-        head = kappa[j, :, 0, :]
         at = chips * rows + j * depth
-        packed[at : at + depth, :] = jnp.where(core == 0, tail, head)
-        packed[at + 3 * depth : at + 4 * depth, :] = jnp.where(core == 0, head, tail)
-
-
-def hands_on(k):
-    return k > 0 and k & (k + 1) == 0
+        packed[at : at + depth, :] = jnp.where(core == 0, kappa[j, :, strip - 1, :], kappa[j, :, 0, :])
 
 
 def pair_sum_body(keep, got, *outs):
     rows = keep.shape[1]
     for k, out in enumerate(outs):
-        out[0:rows, :] = keep[k] + got[k * rows : (k + 1) * rows, :]
-        if hands_on(k):
-            side = (out.shape[0] - rows)
-            out[rows : rows + side, :] = got[len(outs) * rows + side : len(outs) * rows + 2 * side, :]
+        out[...] = keep[k] + got[k * rows : (k + 1) * rows, :]
 
 
 def strip_sum_body(*refs, count, wide):
     parts, (total, edge_b, edge_a) = refs[:count], refs[count:]
     rows = total.shape[0]
-    added = parts[0][0:rows, :]
+    added = parts[0][...]
     for part in parts[1:]:
-        added = added + part[0:rows, :]
+        added = added + part[...]
     total[...] = added
     even = lax.rem(lax.axis_index("slab"), 2) == 0
     head = total[0 : 2 * wide, :]
@@ -387,7 +379,7 @@
 
 
 def adjoint_body(
-    state, velocity, u_out, q_next, push, share_own, share_got, third_b, third_a, fields, field, tap, halo, q_out, sems
+    state, velocity, u_out, q_next, push, share_own, share_got, third_a, third_b, fields, field, tap, halo, q_out, sems
 ):
     copy_u = pltpu.make_async_copy(u_out, fields.at[0, 0], sems.at[0])
     copy_u.start()
@@ -412,22 +404,14 @@
     copy_q.wait()
 
 
-def coefficient_body(kappa, third_b, third_a, got, *rest, size_x, distances):
-    arrived, coef = rest[:-1], rest[-1]
+def coefficient_body(kappa, third_b, third_a, got, far, coef, *, size_x):
     _, depth, strip, _ = kappa.shape
     even = lax.rem(lax.axis_index("slab"), 2) == 0
     border = at_border()
     shot = lax.axis_index("shot")
     even_strip = lax.rem(shot, 2) == 0
     end_strip = (shot == 0) | (shot == lax.axis_size("shot") - 1)
-    chip = lax.div(shot, 2)
-    distance = jnp.bitwise_xor(chip, jnp.where(even_strip, chip - 1, chip + 1))
-    side = 3 * depth
-    ends = [part.shape[0] for part in arrived]
-    far = arrived[0][ends[0] - side : ends[0], :]
-    for k, end, part in zip(distances[1:], ends[1:], arrived[1:]):
-        far = jnp.where(distance == k, part[end - side : end, :], far)
-    facing = got[got.shape[0] - 2 * side : got.shape[0] - side, :]
+    facing = got[got.shape[0] - 3 * depth : got.shape[0], :]
     coef[...] = jnp.zeros(coef.shape, F32)
     for j in range(3):
         at = slice(RADIUS * size_x + j * strip, RADIUS * size_x + (j + 1) * strip)
@@ -515,12 +499,12 @@
         pltpu.with_memory_space_constraint(x, pltpu.HBM) for x in (source_cells, source_codes, wavelets.T)
     )
     small_scratch = [pltpu.SMEM(x.shape, x.dtype) for x in small] + [dma((3,))]
-    partial_u, image0, partial_q, push_u, push, tap_u, weight, out_b, out_a, third_b, third_a = call(
+    partial_u, image0, partial_q, push_u, push, tap_u, weight, out_b, out_a, third_b, third_a, far = call(
         functools.partial(partial_body, scale=math.sqrt(shots * STEPS)),
-        [shape(*cube)] * 5 + [ring, shape(*cube), flat, flat, flat_q, flat_q],
+        [shape(*cube)] * 5 + [ring, shape(*cube), flat, flat, flat_q, flat_q, shape(3 * depth, size_y)],
         (wave_state, velocity, receiver_cells, residuals, diffusivity, *small),
         ["vmem"] * 5 + ["hbm"] * 3,
-        ["vmem"] * 11,
+        ["vmem"] * 12,
         [pltpu.VMEM(padded, F32)] * 2 + [pltpu.VMEM((STEPS, depth * size_x, size_y), F32)] + small_scratch,
         us=1.7,
     )
@@ -529,6 +513,8 @@
     third_b = lax.ppermute(third_b, both, z_odd)
     third_a = lax.ppermute(third_a, "slab", z_even)
 
+    far = lax.ppermute(far, "shot", odd_pairs(shots))
+    first_a, first_b, far = lax.optimization_barrier((first_a, first_b, far))
     (share_own,) = call(share_body, [edge], (first_a, first_b), ["vmem"] * 2, ["vmem"])
     share_got = lax.ppermute(share_own, "shot", even_pairs(shots))
     u_part, q_next, image_own, gain = call(
@@ -545,7 +531,7 @@
     side = 3 * depth
     u_out, keep, send = call(
         image_body,
-        [shape(*cube), part, shape(chips * depth * wide + 2 * side, size_y)],
+        [shape(*cube), part, shape(chips * depth * wide + side, size_y)],
         (velocity, diffusivity, u_part, image_own, gain, tap_u, share_own, share_got, second_b, second_a),
         ["vmem"] * 10,
         ["vmem"] * 3,
@@ -556,7 +542,7 @@
     (fields,) = call(
         adjoint_body,
         [shape(1, 2, *cube)],
-        (wave_state, velocity, u_out, q_next, push, share_own, share_got, third_b, third_a),
+        (wave_state, velocity, u_out, q_next, push, share_own, share_got, third_a, third_b),
         ["vmem"] * 9,
         ["any"],
         [
@@ -569,8 +555,7 @@
         us=1.4,
     )
     row_block = shape(depth * wide, size_y)
-    sums = [shape(depth * wide + (side if hands_on(k) else 0), size_y) for k in range(chips)]
-    parts = call(pair_sum_body, sums, (keep, got), ["vmem"] * 2, ["vmem"] * chips)
+    parts = call(pair_sum_body, [row_block] * chips, (keep, got), ["vmem"] * 2, ["vmem"] * chips)
     arrived = [
         lax.ppermute(parts[k], "shot", [(i, i ^ (2 * k)) for i in range(shots)]) for k in reversed(range(1, chips))
     ] + [parts[0]]
@@ -585,13 +570,12 @@
     )
     grad_b = lax.ppermute(out_b, both, z_odd)
     grad_a = lax.ppermute(out_a, "slab", z_even)
-    distances = [k for k in range(chips) if hands_on(k)]
     tall = 8 * ((wide + 7) // 8)
     (coef,) = call(
-        functools.partial(coefficient_body, size_x=size_x, distances=distances),
+        functools.partial(coefficient_body, size_x=size_x),
         [shape(3, depth + 2, tall, size_y)],
-        (diffusivity, third_b, third_a, got, *(arrived[chips - 1 - k] for k in distances)),
-        ["vmem"] * (4 + len(distances)),
+        (diffusivity, third_b, third_a, got, far),
+        ["vmem"] * 5,
         ["vmem"],
         us=0.1,
     )

time: 31.1 us -> 30.9 us (level)
  waiting for transfers between devices: 6.6 us -> 5.69 us
  starting transfers between devices: 15 us -> 15.7 us
    ppermute x0 -> x1, starting transfers between devices: none -> 1.96 us  [on_device(): far = lax.ppermute(far, 'shot', odd_pairs(shots))]
    ppermute x1, waiting for transfers between devices: 1.15 us -> 0.01 us  [on_device(): first_a = lax.ppermute(out_a, 'slab', z_even)]
    ppermute x1, starting transfers between devices: 2.95 us -> 1.81 us  [on_device(): third_a = lax.ppermute(third_a, 'slab', z_even)]
    ppermute x1, waiting for transfers between devices: 1.46 us -> 2.48 us  [on_device(): second_a = lax.ppermute(out_a, 'slab', z_even)]
    ppermute x3, waiting for transfers between devices: 1.56 us -> 0.93 us  [on_device(): lax.ppermute(parts[k], 'shot', [(i, i ^ 2 * k) for i in range(shots)])]
  transfers between devices with their start and end apart: 13 -> 14, of which waited for: 5 -> 5; matrix products, arithmetic and copies ran while one was open for 0% -> 0% of each run, Pallas kernels for 14% -> 15%
where the time goes in v6:
time: 30.9 us; the launch traced here: 30.7 us
  starting transfers between devices  15.7 us (51%)
  Pallas kernels  6.95 us (22%)
  waiting for transfers between devices  5.69 us (18%)
  local copies, waits for them, and re-layouts  1.57 us (5%)
  between operations  0.78 us (3%)
    pallas_call x10, Pallas kernels, call(): pl.pallas_call(body, out_shape=list(out_shapes), in_specs=[SPECS[s] for s...  6.95 us
    ppermute x3, starting transfers between devices, on_device(): lax.ppermute(parts[k], 'shot', [(i, i ^ 2 * k) for i in range(shots)])  3.55 us
    ppermute x1, starting transfers between devices, on_device(): first_a = lax.ppermute(out_a, 'slab', z_even)  3.09 us
    ppermute x1, starting transfers between devices, on_device(): second_a = lax.ppermute(out_a, 'slab', z_even)  2.86 us
    ppermute x1, waiting for transfers between devices, on_device(): second_a = lax.ppermute(out_a, 'slab', z_even)  2.48 us
    ppermute x1, starting transfers between devices, on_device(): grad_a = lax.ppermute(out_a, 'slab', z_even)  2.11 us
    ppermute x1, starting transfers between devices, on_device(): far = lax.ppermute(far, 'shot', odd_pairs(shots))  1.96 us
    ppermute x1, starting transfers between devices, on_device(): third_a = lax.ppermute(third_a, 'slab', z_even)  1.81 us
  transfers between devices with their start and end apart: 14, of which 5 were waited for; matrix products, arithmetic and copies ran while one was open for 0% of the time, Pallas kernels for 15%

profile of v6, /device:TPU:0, one launch (start us, length us, event | category | flops | bytes accessed | tf_op | source)
XLA Modules:
  0.0 30.7 jit_solution(16932587230896746597)
XLA Ops:
  0.6 1.3 %shard_map.113 = (f32[10,64,128]{2,1,0:T(8,128)S(1)}, f32[10,64,128]{2,1,0:T(8,128)S(1)}) custom-call(f32[2,1,2,8,64,128]{5,4,3,2,1,0:T(8,128)} %state.7, f32[8,64,128]{2,1,0:T(8,128)} %velocity.11), custom_call_target="tpu_custom_call" | custom-call | bytes 4797000 | tf_op jit(solution)/shard_map/pallas_call | solution.py:69
  2.0 3.1 %collective-permute-start = (f32[10,64,128]{2,1,0:T(8,128)S(1)}, f32[10,64,128]{2,1,0:T(8,128)S(1)}, u32[]{:S(2)}, u32[]{:S(2)}) collective-permute-start(f32[10,64,128]{2,1,0:T(8,128)S(1)} %get-tuple-element.46), channel_id=1, source_target_pairs={{0,1},{1,0},{2,3},{3,2},{4,5},{5,4},{6,7},{7,6},{8,9},{9,8},{10,11... | collective-permute-start | bytes 983048 | tf_op jit(solution)/shard_map/ppermute | solution.py:491
  5.1 0.7 %copy-done.6 = s32[1,256]{1,0:T(1,128)S(1)} copy-done((s32[1,256]{1,0:T(1,128)S(1)}, s32[1,256]{1,0:T(1,128)}, u32[]{:S(2)}) %copy-start.6) | copy-done | bytes 1048
  5.8 0.9 %copy-done.2 = f32[3,8,8,128]{3,2,1,0:T(8,128)S(1)} copy-done((f32[3,8,8,128]{3,2,1,0:T(8,128)S(1)}, f32[3,8,8,128]{3,2,1,0:T(8,128)}, u32[]{:S(2)}) %copy-start.2) | copy-done | bytes 98328
  6.7 2.3 %shard_map.112 = (f32[8,64,128]{2,1,0:T(8,128)S(1)}, f32[8,64,128]{2,1,0:T(8,128)S(1)}, f32[8,64,128]{2,1,0:T(8,128)S(1)}, f32[8,64,128]{2,1,0:T(8,128)S(1)}, f3...) custom-call(f32[2,1,2,8,64,128]{5,4,3,2,1,0:T(8,128)S(1)} %copy-done, ...), custom_call_target="tpu_custom_call" | custom-call | bytes 6273000 | tf_op jit(solution)/shard_map/pallas_call | solution.py:69
  9.0 2.0 %collective-permute-start.2 = (f32[24,128]{1,0:T(8,128)S(1)}, f32[24,128]{1,0:T(8,128)S(1)}, u32[]{:S(2)}, u32[]{:S(2)}) collective-permute-start(f32[24,128]{1,0:T(8,128)S(1)} %get-tuple-element.48), channel_id=1, source_target_pairs={{4,8},{12,16},{20,24},{28,0},{8,4},{16,12},{24,20},{0,28},{5,9},{1... | collective-permute-start | bytes 36872 | tf_op jit(solution)/shard_map/ppermute | solution.py:516
  10.9 2.9 %collective-permute-start.5 = (f32[256,128]{1,0:T(8,128)S(1)}, f32[256,128]{1,0:T(8,128)S(1)}, u32[]{:S(2)}, u32[]{:S(2)}) collective-permute-start(f32[256,128]{1,0:T(8,128)S(1)} %get-tuple-element.56), channel_id=1, source_target_pairs={{0,1},{1,0},{2,3},{3,2},{4,5},{5,4},{6,7},{7,6},{8,9},{9,8},{10,11... | collective-permute-start | bytes 393224 | tf_op jit(solution)/shard_map/ppermute | solution.py:512
  13.8 0.1 collective-permute-start.3
  13.9 0.8 %shard_map.114 = (f32[8,64,128]{2,1,0:T(8,128)S(1)}, f32[8,64,128]{2,1,0:T(8,128)S(1)}, f32[8,64,128]{2,1,0:T(8,128)S(1)}, f32[8,64,128]{2,1,0:T(8,128)S(1)}) custom-call(f32[2,1,2,8,64,128]{5,4,3,2,1,0:T(8,128)S(1)} %copy-done, f32[8,64,128]{2,1,0:T(8,128)S(1)} %copy-done.1, f32[8,64,128]{2,1,0:T(8,128)S(1)} %get-tuple-element.41.partial_u, ...), custom_call_target="tpu_custom_call" | custom-call | bytes 2952000 | tf_op jit(solution)/shard_map/pallas_call | solution.py:69
  14.7 2.5 %collective-permute-done.5.second_a = f32[256,128]{1,0:T(8,128)S(1)} collective-permute-done((f32[256,128]{1,0:T(8,128)S(1)}, f32[256,128]{1,0:T(8,128)S(1)}, u32[]{:S(2)}, u32[]{:S(2)}) %collective-permute-start.5) | collective-permute-done | bytes 131104 | tf_op jit(solution)/shard_map/ppermute | solution.py:512
  17.2 0.2 shard_map.116
  17.4 0.1 collective-permute-start.6
  17.5 1.8 %collective-permute-start.10 = (f32[280,128]{1,0:T(8,128)S(1)}, f32[280,128]{1,0:T(8,128)S(1)}, u32[]{:S(2)}, u32[]{:S(2)}) collective-permute-start(f32[280,128]{1,0:T(8,128)S(1)} %get-tuple-element.66), channel_id=1, source_target_pairs={{0,1},{1,0},{2,3},{3,2},{4,5},{5,4},{6,7},{7,6},{8,9},{9,8},{10,11... | collective-permute-start | bytes 430088 | tf_op jit(solution)/shard_map/ppermute | solution.py:514
  19.3 0.2 collective-permute-start.11
  19.5 2.1 %collective-permute-start.7 = (f32[96,128]{1,0:T(8,128)S(1)}, f32[96,128]{1,0:T(8,128)S(1)}, u32[]{:S(2)}, u32[]{:S(2)}) collective-permute-start(f32[96,128]{1,0:T(8,128)S(1)} %get-tuple-element.59), channel_id=1, source_target_pairs={{0,24},{4,28},{8,16},{12,20},{16,8},{20,12},{24,0},{28,4},{1,25},{... | collective-permute-start | bytes 147464 | tf_op jit(solution)/shard_map/ppermute | solution.py:560
  21.6 0.4 %collective-permute-start.8 = (f32[96,128]{1,0:T(8,128)S(1)}, f32[96,128]{1,0:T(8,128)S(1)}, u32[]{:S(2)}, u32[]{:S(2)}) collective-permute-start(f32[96,128]{1,0:T(8,128)S(1)} %get-tuple-element.60), channel_id=1, source_target_pairs={{0,16},{4,20},{8,24},{12,28},{16,0},{20,4},{24,8},{28,12},{1,17},{... | collective-permute-start | bytes 147464 | tf_op jit(solution)/shard_map/ppermute | solution.py:560
  22.0 1.1 %collective-permute-start.9 = (f32[96,128]{1,0:T(8,128)S(1)}, f32[96,128]{1,0:T(8,128)S(1)}, u32[]{:S(2)}, u32[]{:S(2)}) collective-permute-start(f32[96,128]{1,0:T(8,128)S(1)} %get-tuple-element.61), channel_id=1, source_target_pairs={{0,8},{4,12},{8,0},{12,4},{16,24},{20,28},{24,16},{28,20},{1,9},{5... | collective-permute-start | bytes 147464 | tf_op jit(solution)/shard_map/ppermute | solution.py:560
  23.1 0.6 %collective-permute-done.10.third_a = f32[280,128]{1,0:T(8,128)S(1)} collective-permute-done((f32[280,128]{1,0:T(8,128)S(1)}, f32[280,128]{1,0:T(8,128)S(1)}, u32[]{:S(2)}, u32[]{:S(2)}) %collective-permute-start.10) | collective-permute-done | bytes 143392 | tf_op jit(solution)/shard_map/ppermute | solution.py:514
  23.7 1.4 %shard_map.118 = f32[1,2,8,64,128]{4,3,2,1,0:T(8,128)} custom-call(f32[2,1,2,8,64,128]{5,4,3,2,1,0:T(8,128)S(1)} %copy-done, f32[8,64,128]{2,1,0:T(8,128)S(1)} %copy-done.1, f32[8,64,128]{2,1,0:T(8,128)S(1)} %get-tuple-element.63.u_out, f32[8,64,128]{2,1,0:T(8,128)S(1)} %get-tuple-element.64.q_next, f32[8,64,128]{2,1,0:T(8,128)S(1)} %get-tuple-element.65.push, ...), custom_call_target="tpu_custom_call" | custom-call | bytes 5166000 | tf_op jit(solution)/shard_map/pallas_call | solution.py:69
  25.1 0.6 %collective-permute-done.8.refs_1_ = f32[96,128]{1,0:T(8,128)S(1)} collective-permute-done((f32[96,128]{1,0:T(8,128)S(1)}, f32[96,128]{1,0:T(8,128)S(1)}, u32[]{:S(2)}, u32[]{:S(2)}) %collective-permute-start.8) | collective-permute-done | bytes 49184 | tf_op jit(solution)/shard_map/ppermute | solution.py:560
  25.7 0.4 %collective-permute-done.9.refs_2_ = f32[96,128]{1,0:T(8,128)S(1)} collective-permute-done((f32[96,128]{1,0:T(8,128)S(1)}, f32[96,128]{1,0:T(8,128)S(1)}, u32[]{:S(2)}, u32[]{:S(2)}) %collective-permute-start.9) | collective-permute-done | bytes 49184 | tf_op jit(solution)/shard_map/ppermute | solution.py:560
  26.1 2.1 %collective-permute-start.12 = (f32[24,128]{1,0:T(8,128)S(1)}, f32[24,128]{1,0:T(8,128)S(1)}, u32[]{:S(2)}, u32[]{:S(2)}) collective-permute-start(f32[24,128]{1,0:T(8,128)S(1)} %get-tuple-element.74), channel_id=1, source_target_pairs={{0,1},{1,0},{2,3},{3,2},{4,5},{5,4},{6,7},{7,6},{8,9},{9,8},{10,11... | collective-permute-start | bytes 36872 | tf_op jit(solution)/shard_map/ppermute | solution.py:572
  28.2 1.6 %collective-permute-done.12.got_a = f32[24,128]{1,0:T(8,128)S(1)} collective-permute-done((f32[24,128]{1,0:T(8,128)S(1)}, f32[24,128]{1,0:T(8,128)S(1)}, u32[]{:S(2)}, u32[]{:S(2)}) %collective-permute-start.12) | collective-permute-done | bytes 12320 | tf_op jit(solution)/shard_map/ppermute | solution.py:572
  29.9 0.8 %shard_map.121 = (f32[8,8,128]{2,1,0:T(8,128)}, f32[8,8,128]{2,1,0:T(8,128)}) custom-call(f32[96,128]{1,0:T(8,128)S(1)} %get-tuple-element.73.total, f32[24,128]{1,0:T(8,128)S(1)} %collective-permute-done.12.got_a, f32[24,128]{1,0:T(8,128)S(1)} %collective-permute-done.13.got_b, f32[3,8,8,128]{3,2,1,0:T(8,128)S(1)} %copy-done.3, ...), custom_call_target="tpu_custom_call" | custom-call | bytes 2583000 | tf_op jit(solution)/shard_map/pallas_call | solution.py:69
  (28 shorter events, 0.1 us)
Async XLA Ops:
  0.6 4.5 %copy-start.1 = (f32[8,64,128]{2,1,0:T(8,128)S(1)}, f32[8,64,128]{2,1,0:T(8,128)}, u32[]{:S(2)}) copy-start(f32[8,64,128]{2,1,0:T(8,128)} %velocity.11) | copy-start | bytes 786436
  0.6 4.5 %copy-start = (f32[2,1,2,8,64,128]{5,4,3,2,1,0:T(8,128)S(1)}, f32[2,1,2,8,64,128]{5,4,3,2,1,0:T(8,128)}, u32[]{:S(2)}) copy-start(f32[2,1,2,8,64,128]{5,4,3,2,1,0:T(8,128)} %state.7) | copy-start | bytes 3145732
  2.0 3.1 %copy-start.5 = (f32[1,2,256]{2,1,0:T(2,128)S(1)}, f32[1,2,256]{2,1,0:T(2,128)}, u32[]{:S(2)}) copy-start(f32[1,2,256]{2,1,0:T(2,128)} %residuals.1) | copy-start | bytes 6148
  2.0 11.8 %collective-permute-start = (f32[10,64,128]{2,1,0:T(8,128)S(1)}, f32[10,64,128]{2,1,0:T(8,128)S(1)}, u32[]{:S(2)}, u32[]{:S(2)}) collective-permute-start(f32[10,64,128]{2,1,0:T(8,128)S(1)} %get-tuple-element.46), channel_id=1, source_target_pairs={{0,1},{1,0},{2,3},{3,2},{4,5},{5,4},{6,7},{7,6},{8,9},{9,8},{10,11... | collective-permute-start | bytes 983048 | tf_op jit(solution)/shard_map/ppermute | solution.py:491
  5.1 0.7 %copy-start.6 = (s32[1,256]{1,0:T(1,128)S(1)}, s32[1,256]{1,0:T(1,128)}, u32[]{:S(2)}) copy-start(s32[1,256]{1,0:T(1,128)} %cells.1) | copy-start | bytes 3076
  5.1 8.7 %collective-permute-start.1 = (f32[10,64,128]{2,1,0:T(8,128)S(1)}, f32[10,64,128]{2,1,0:T(8,128)S(1)}, u32[]{:S(2)}, u32[]{:S(2)}) collective-permute-start(f32[10,64,128]{2,1,0:T(8,128)S(1)} %get-tuple-element.47), channel_id=1, source_target_pairs={{0,4},{1,2},{2,1},{3,7},{4,0},{5,6},{6,5},{7,3},{8,12},{9,10},{10,... | collective-permute-start | bytes 983048 | tf_op jit(solution)/shard_map/ppermute | solution.py:490
  5.8 0.9 %copy-start.2 = (f32[3,8,8,128]{3,2,1,0:T(8,128)S(1)}, f32[3,8,8,128]{3,2,1,0:T(8,128)}, u32[]{:S(2)}) copy-start(f32[3,8,8,128]{3,2,1,0:T(8,128)} %kappa.7) | copy-start | bytes 294916
  9.0 4.8 %collective-permute-start.2 = (f32[24,128]{1,0:T(8,128)S(1)}, f32[24,128]{1,0:T(8,128)S(1)}, u32[]{:S(2)}, u32[]{:S(2)}) collective-permute-start(f32[24,128]{1,0:T(8,128)S(1)} %get-tuple-element.48), channel_id=1, source_target_pairs={{4,8},{12,16},{20,24},{28,0},{8,4},{16,12},{24,20},{0,28},{5,9},{1... | collective-permute-start | bytes 36872 | tf_op jit(solution)/shard_map/ppermute | solution.py:516
  10.9 3.7 %collective-permute-start.4 = (f32[256,128]{1,0:T(8,128)S(1)}, f32[256,128]{1,0:T(8,128)S(1)}, u32[]{:S(2)}, u32[]{:S(2)}) collective-permute-start(f32[256,128]{1,0:T(8,128)S(1)} %get-tuple-element.55), channel_id=1, source_target_pairs={{0,4},{1,2},{2,1},{3,7},{4,0},{5,6},{6,5},{7,3},{8,12},{9,10},{10,... | collective-permute-start | bytes 393224 | tf_op jit(solution)/shard_map/ppermute | solution.py:511
  10.9 6.2 %collective-permute-start.5 = (f32[256,128]{1,0:T(8,128)S(1)}, f32[256,128]{1,0:T(8,128)S(1)}, u32[]{:S(2)}, u32[]{:S(2)}) collective-permute-start(f32[256,128]{1,0:T(8,128)S(1)} %get-tuple-element.56), channel_id=1, source_target_pairs={{0,1},{1,0},{2,3},{3,2},{4,5},{5,4},{6,7},{7,6},{8,9},{9,8},{10,11... | collective-permute-start | bytes 393224 | tf_op jit(solution)/shard_map/ppermute | solution.py:512
  13.8 3.3 %collective-permute-start.3 = (f32[4,64,128]{2,1,0:T(8,128)S(1)}, f32[4,64,128]{2,1,0:T(8,128)S(1)}, u32[]{:S(2)}, u32[]{:S(2)}) collective-permute-start(f32[4,64,128]{2,1,0:T(8,128)S(1)} %shard_map.115.share_own), channel_id=1, source_target_pairs={{0,4},{4,0},{8,12},{12,8},{16,20},{20,16},{24,28},{28,24},{1,5},{5... | collective-permute-start | bytes 393224 | tf_op jit(solution)/shard_map/ppermute | solution.py:519
  13.9 3.3 %copy-start.3 = (f32[3,8,8,128]{3,2,1,0:T(8,128)S(1)}, f32[3,8,8,128]{3,2,1,0:T(8,128)}, u32[]{:S(2)}) copy-start(f32[3,8,8,128]{3,2,1,0:T(8,128)} %kappa.7) | copy-start | bytes 294916
  17.4 2.1 %collective-permute-start.6 = (f32[408,128]{1,0:T(8,128)S(1)}, f32[408,128]{1,0:T(8,128)S(1)}, u32[]{:S(2)}, u32[]{:S(2)}) collective-permute-start(f32[408,128]{1,0:T(8,128)S(1)} %get-tuple-element.58), channel_id=1, source_target_pairs={{0,4},{4,0},{8,12},{12,8},{16,20},{20,16},{24,28},{28,24},{1,5},{5... | collective-permute-start | bytes 626696 | tf_op jit(solution)/shard_map/ppermute | solution.py:541
  17.5 6.2 %collective-permute-start.10 = (f32[280,128]{1,0:T(8,128)S(1)}, f32[280,128]{1,0:T(8,128)S(1)}, u32[]{:S(2)}, u32[]{:S(2)}) collective-permute-start(f32[280,128]{1,0:T(8,128)S(1)} %get-tuple-element.66), channel_id=1, source_target_pairs={{0,1},{1,0},{2,3},{3,2},{4,5},{5,4},{6,7},{7,6},{8,9},{9,8},{10,11... | collective-permute-start | bytes 430088 | tf_op jit(solution)/shard_map/ppermute | solution.py:514
  19.3 4.4 %collective-permute-start.11 = (f32[280,128]{1,0:T(8,128)S(1)}, f32[280,128]{1,0:T(8,128)S(1)}, u32[]{:S(2)}, u32[]{:S(2)}) collective-permute-start(f32[280,128]{1,0:T(8,128)S(1)} %get-tuple-element.67), channel_id=1, source_target_pairs={{0,4},{1,2},{2,1},{3,7},{4,0},{5,6},{6,5},{7,3},{8,12},{9,10},{10,... | collective-permute-start | bytes 430088 | tf_op jit(solution)/shard_map/ppermute | solution.py:513
  19.5 5.6 %collective-permute-start.7 = (f32[96,128]{1,0:T(8,128)S(1)}, f32[96,128]{1,0:T(8,128)S(1)}, u32[]{:S(2)}, u32[]{:S(2)}) collective-permute-start(f32[96,128]{1,0:T(8,128)S(1)} %get-tuple-element.59), channel_id=1, source_target_pairs={{0,24},{4,28},{8,16},{12,20},{16,8},{20,12},{24,0},{28,4},{1,25},{... | collective-permute-start | bytes 147464 | tf_op jit(solution)/shard_map/ppermute | solution.py:560
  21.6 4.1 %collective-permute-start.8 = (f32[96,128]{1,0:T(8,128)S(1)}, f32[96,128]{1,0:T(8,128)S(1)}, u32[]{:S(2)}, u32[]{:S(2)}) collective-permute-start(f32[96,128]{1,0:T(8,128)S(1)} %get-tuple-element.60), channel_id=1, source_target_pairs={{0,16},{4,20},{8,24},{12,28},{16,0},{20,4},{24,8},{28,12},{1,17},{... | collective-permute-start | bytes 147464 | tf_op jit(solution)/shard_map/ppermute | solution.py:560
  22.0 4.1 %collective-permute-start.9 = (f32[96,128]{1,0:T(8,128)S(1)}, f32[96,128]{1,0:T(8,128)S(1)}, u32[]{:S(2)}, u32[]{:S(2)}) collective-permute-start(f32[96,128]{1,0:T(8,128)S(1)} %get-tuple-element.61), channel_id=1, source_target_pairs={{0,8},{4,12},{8,0},{12,4},{16,24},{20,28},{24,16},{28,20},{1,9},{5... | collective-permute-start | bytes 147464 | tf_op jit(solution)/shard_map/ppermute | solution.py:560
  26.1 3.8 %collective-permute-start.12 = (f32[24,128]{1,0:T(8,128)S(1)}, f32[24,128]{1,0:T(8,128)S(1)}, u32[]{:S(2)}, u32[]{:S(2)}) collective-permute-start(f32[24,128]{1,0:T(8,128)S(1)} %get-tuple-element.74), channel_id=1, source_target_pairs={{0,1},{1,0},{2,3},{3,2},{4,5},{5,4},{6,7},{7,6},{8,9},{9,8},{10,11... | collective-permute-start | bytes 36872 | tf_op jit(solution)/shard_map/ppermute | solution.py:572
  28.2 1.7 %copy-start.4 = (f32[8,8,128]{2,1,0:T(8,128)S(1)}, f32[8,8,128]{2,1,0:T(8,128)}, u32[]{:S(2)}) copy-start(f32[8,8,128]{2,1,0:T(8,128)} %momentum.1) | copy-start | bytes 98308
  28.2 1.7 %collective-permute-start.13 = (f32[24,128]{1,0:T(8,128)S(1)}, f32[24,128]{1,0:T(8,128)S(1)}, u32[]{:S(2)}, u32[]{:S(2)}) collective-permute-start(f32[24,128]{1,0:T(8,128)S(1)} %get-tuple-element.75), channel_id=1, source_target_pairs={{0,4},{1,2},{2,1},{3,7},{4,0},{5,6},{6,5},{7,3},{8,12},{9,10},{10,... | collective-permute-start | bytes 36872 | tf_op jit(solution)/shard_map/ppermute | solution.py:571

commit v7 on v6

--- a/solution.py
+++ b/solution.py
@@ -152,10 +152,51 @@
     return total
 
 
-def partial_body(
+def partial_u_body(
+    state, velocity, source_cells, source_codes, wavelets,
+    partial_u, image, tap_u, out_b, out_a,
+    field, cells_here, codes_here, wavelets_here, sems,
+):
+    small = [(source_cells, cells_here), (source_codes, codes_here), (wavelets, wavelets_here)]
+    copies = run_copies(small, sems)
+    depth, size_x, size_y = velocity.shape
+    even = lax.rem(lax.axis_index("slab"), 2) == 0
+    clear_sides(field, size_x)
+    for z in range(depth):
+        field[z, PAD : PAD + size_x, :] = state[1, 0, 0, z]
+    lane = lax.broadcasted_iota(jnp.int32, (size_x, size_y), 1)
+    for z in range(depth):
+        v = velocity[z]
+        drive = (v * v) * laplacian_row(field, z, depth, size_x, size_y, lane)
+        partial_u[z] = (2.0 * state[1, 0, 0, z] - state[0, 0, 0, z]) + drive
+        image[z] = drive * state[1, 0, 1, z]
+    for k in range(2 * RADIUS):
+        tap_u[k] = weighted([(r, state[1, 0, 0, own]) for r, own in halo_near(k, depth)])
+
+    def inject(z, x, spot):
+        @pl.when((z >= 0) & (z < depth))
+        def _():
+            at = (z, pl.ds(x, 1), slice(None))
+            v = velocity[at]
+            change = (v * v) * spot
+            partial_u[at] = partial_u[at] + change
+            image[at] = image[at] + change * state[1, 0, 1, z, pl.ds(x, 1), :]
+
+    for copy in copies:
+        copy.wait()
+    first_layer = lax.axis_index("slab") * depth
+    point_cells(cells_here, codes_here, wavelets_here, 0, first_layer, size_x, size_y, inject)
+    for k in range(RADIUS):
+        tail = partial_u[depth - RADIUS + k]
+        head = partial_u[k]
+        out_a[k * size_x : (k + 1) * size_x, :] = jnp.where(even, tail, head)
+        out_b[k * size_x : (k + 1) * size_x, :] = jnp.where(even, head, tail)
+
+
+def partial_q_body(
     state, velocity, cells, residuals, kappa, source_cells, source_codes, wavelets,
-    partial_u, image, partial_q, push_u, push, tap_u, weight, out_b, out_a, third_b, third_a, far,
-    field_u, field_q, grid_now, cells_here, codes_here, wavelets_here, sems, *, scale,
+    partial_q, push_u, push, weight, third_b, third_a, far,
+    field, grid_now, cells_here, codes_here, wavelets_here, sems, *, scale,
 ):
     small = [(source_cells, cells_here), (source_codes, codes_here), (wavelets, wavelets_here)]
     copies = run_copies(small, sems)
@@ -170,10 +211,9 @@
         at = RADIUS * size_x + j * strip
         third_a[at : at + strip, :] = jnp.where(even, tail, head)
         third_b[at : at + strip, :] = jnp.where(even, head, tail)
-    for which, field in ((0, field_u), (1, field_q)):
-        clear_sides(field, size_x)
-        for z in range(depth):
-            field[z, PAD : PAD + size_x, :] = state[1, 0, which, z]
+    clear_sides(field, size_x)
+    for z in range(depth):
+        field[z, PAD : PAD + size_x, :] = state[1, 0, 1, z]
 
     volume = depth * size_x * size_y
     count = cells.shape[1]
@@ -200,10 +240,7 @@
         at = slice(z * size_x, (z + 1) * size_x)
         v = velocity[z]
         vv = v * v
-        drive = vv * laplacian_row(field_u, z, depth, size_x, size_y, lane)
-        partial_u[z] = (2.0 * state[1, 0, 0, z] - state[0, 0, 0, z]) + drive
-        image[z] = drive * state[1, 0, 1, z]
-        drive = vv * (laplacian_row(field_q, z, depth, size_x, size_y, lane) + grid_now[0, at, :])
+        drive = vv * (laplacian_row(field, z, depth, size_x, size_y, lane) + grid_now[0, at, :])
         partial_q[z] = (2.0 * state[1, 0, 1, z] - state[0, 0, 1, z]) + drive
         push[z] = vv * grid_now[1, at, :]
         weight[z] = -0.2 / (v * scale)
@@ -214,30 +251,17 @@
         def _():
             at = (z, pl.ds(x, 1), slice(None))
             v = velocity[at]
-            change = (v * v) * spot
-            partial_u[at] = partial_u[at] + change
-            image[at] = image[at] + change * state[1, 0, 1, z, pl.ds(x, 1), :]
-
-    def inject_next(z, x, spot):
-        @pl.when((z >= 0) & (z < depth))
-        def _():
-            at = (z, pl.ds(x, 1), slice(None))
-            v = velocity[at]
             push_u[at] = push_u[at] + (v * v) * spot
 
     for copy in copies:
         copy.wait()
     first_layer = lax.axis_index("slab") * depth
-    point_cells(cells_here, codes_here, wavelets_here, 0, first_layer, size_x, size_y, inject)
-    point_cells(cells_here, codes_here, wavelets_here, 1, first_layer, size_x, size_y, inject_next)
-    for k in range(2 * RADIUS):
-        tap_u[k] = weighted([(r, state[1, 0, 0, own]) for r, own in halo_near(k, depth)])
-    for source, to_a, to_b in ((partial_u, out_a, out_b), (partial_q, third_a, third_b)):
-        for k in range(RADIUS):
-            tail = source[depth - RADIUS + k]
-            head = source[k]
-            to_a[k * size_x : (k + 1) * size_x, :] = jnp.where(even, tail, head)
-            to_b[k * size_x : (k + 1) * size_x, :] = jnp.where(even, head, tail)
+    point_cells(cells_here, codes_here, wavelets_here, 1, first_layer, size_x, size_y, inject)
+    for k in range(RADIUS):
+        tail = partial_q[depth - RADIUS + k]
+        head = partial_q[k]
+        third_a[k * size_x : (k + 1) * size_x, :] = jnp.where(even, tail, head)
+        third_b[k * size_x : (k + 1) * size_x, :] = jnp.where(even, head, tail)
 
 
 def share_body(first_a, first_b, share):
@@ -499,17 +523,27 @@
         pltpu.with_memory_space_constraint(x, pltpu.HBM) for x in (source_cells, source_codes, wavelets.T)
     )
     small_scratch = [pltpu.SMEM(x.shape, x.dtype) for x in small] + [dma((3,))]
-    partial_u, image0, partial_q, push_u, push, tap_u, weight, out_b, out_a, third_b, third_a, far = call(
-        functools.partial(partial_body, scale=math.sqrt(shots * STEPS)),
-        [shape(*cube)] * 5 + [ring, shape(*cube), flat, flat, flat_q, flat_q, shape(3 * depth, size_y)],
+    partial_u, image0, tap_u, out_b, out_a = call(
+        partial_u_body,
+        [shape(*cube)] * 2 + [ring, flat, flat],
+        (wave_state, velocity, *small),
+        ["vmem"] * 2 + ["hbm"] * 3,
+        ["vmem"] * 5,
+        [pltpu.VMEM(padded, F32)] + small_scratch,
+        us=1.0,
+    )
+    receiver_cells, out_b, out_a = lax.optimization_barrier((receiver_cells, out_b, out_a))
+    second_b = lax.ppermute(out_b, both, z_odd)
+    second_a = lax.ppermute(out_a, "slab", z_even)
+    partial_q, push_u, push, weight, third_b, third_a, far = call(
+        functools.partial(partial_q_body, scale=math.sqrt(shots * STEPS)),
+        [shape(*cube)] * 4 + [flat_q, flat_q, shape(3 * depth, size_y)],
         (wave_state, velocity, receiver_cells, residuals, diffusivity, *small),
         ["vmem"] * 5 + ["hbm"] * 3,
-        ["vmem"] * 12,
-        [pltpu.VMEM(padded, F32)] * 2 + [pltpu.VMEM((STEPS, depth * size_x, size_y), F32)] + small_scratch,
-        us=1.7,
-    )
-    second_b = lax.ppermute(out_b, both, z_odd)
-    second_a = lax.ppermute(out_a, "slab", z_even)
+        ["vmem"] * 7,
+        [pltpu.VMEM(padded, F32), pltpu.VMEM((STEPS, depth * size_x, size_y), F32)] + small_scratch,
+        us=1.3,
+    )
     third_b = lax.ppermute(third_b, both, z_odd)
     third_a = lax.ppermute(third_a, "slab", z_even)
 

time: 30.9 us -> 30.8 us (level)
  local copies, waits for them, and re-layouts: 1.57 us -> 0.69 us
  Pallas kernels: 6.95 us -> 7.74 us
    unnamed x14 -> x12, local copies, waits for them, and re-layouts: 1.57 us -> 0.69 us
    pallas_call x10 -> x11, Pallas kernels: 6.95 us -> 7.74 us  [call(): pl.pallas_call(body, out_shape=list(out_shapes), in_specs=[SPECS[s] for s...]
    ppermute x1, starting transfers between devices: 2.86 us -> 2.21 us  [on_device(): second_a = lax.ppermute(out_a, 'slab', z_even)]
    ppermute x1, starting transfers between devices: 1.96 us -> 2.61 us  [on_device(): far = lax.ppermute(far, 'shot', odd_pairs(shots))]
    ppermute x3, waiting for transfers between devices: 0.93 us -> 0.54 us  [on_device(): lax.ppermute(parts[k], 'shot', [(i, i ^ 2 * k) for i in range(shots)])]
    ppermute x1, waiting for transfers between devices: 2.48 us -> 2.83 us  [on_device(): second_a = lax.ppermute(out_a, 'slab', z_even)]
  transfers between devices with their start and end apart: 14 -> 14, of which waited for: 5 -> 5; matrix products, arithmetic and copies ran while one was open for 0% -> 0% of each run, Pallas kernels for 15% -> 17%
where the time goes in v7:
time: 30.8 us; the launch traced here: 30.5 us
  starting transfers between devices  15.6 us (51%)
  Pallas kernels  7.74 us (25%)
  waiting for transfers between devices  5.71 us (19%)
  between operations  0.79 us (3%)
  local copies, waits for them, and re-layouts  0.69 us (2%)
    pallas_call x11, Pallas kernels, call(): pl.pallas_call(body, out_shape=list(out_shapes), in_specs=[SPECS[s] for s...  7.74 us
    ppermute x3, starting transfers between devices, on_device(): lax.ppermute(parts[k], 'shot', [(i, i ^ 2 * k) for i in range(shots)])  3.55 us
    ppermute x1, starting transfers between devices, on_device(): first_a = lax.ppermute(out_a, 'slab', z_even)  3.09 us
    ppermute x1, waiting for transfers between devices, on_device(): second_a = lax.ppermute(out_a, 'slab', z_even)  2.83 us
    ppermute x1, starting transfers between devices, on_device(): far = lax.ppermute(far, 'shot', odd_pairs(shots))  2.61 us
    ppermute x1, starting transfers between devices, on_device(): second_a = lax.ppermute(out_a, 'slab', z_even)  2.21 us
    ppermute x1, starting transfers between devices, on_device(): grad_a = lax.ppermute(out_a, 'slab', z_even)  2.07 us
    ppermute x1, starting transfers between devices, on_device(): third_a = lax.ppermute(third_a, 'slab', z_even)  1.76 us
  transfers between devices with their start and end apart: 14, of which 5 were waited for; matrix products, arithmetic and copies ran while one was open for 0% of the time, Pallas kernels for 17%

profile of v7, /device:TPU:0, one launch (start us, length us, event | category | flops | bytes accessed | tf_op | source)
XLA Modules:
  0.0 30.5 jit_solution(16444942915955847767)
XLA Ops:
  0.6 1.3 %shard_map.114 = (f32[10,64,128]{2,1,0:T(8,128)S(1)}, f32[10,64,128]{2,1,0:T(8,128)S(1)}) custom-call(f32[2,1,2,8,64,128]{5,4,3,2,1,0:T(8,128)} %state.9, f32[8,64,128]{2,1,0:T(8,128)} %velocity.13), custom_call_target="tpu_custom_call" | custom-call | bytes 4797000 | tf_op jit(solution)/shard_map/pallas_call | solution.py:69
  2.0 3.1 %collective-permute-start = (f32[10,64,128]{2,1,0:T(8,128)S(1)}, f32[10,64,128]{2,1,0:T(8,128)S(1)}, u32[]{:S(2)}, u32[]{:S(2)}) collective-permute-start(f32[10,64,128]{2,1,0:T(8,128)S(1)} %get-tuple-element.52), channel_id=1, source_target_pairs={{0,1},{1,0},{2,3},{3,2},{4,5},{5,4},{6,7},{7,6},{8,9},{9,8},{10,11... | collective-permute-start | bytes 983048 | tf_op jit(solution)/shard_map/ppermute | solution.py:515
  5.1 1.3 %shard_map.112 = (f32[8,64,128]{2,1,0:T(8,128)S(1)}, f32[8,64,128]{2,1,0:T(8,128)S(1)}, f32[8,64,128]{2,1,0:T(8,128)S(1)}, f32[256,128]{1,0:T(8,128)S(1)}, f32[256,128]{1,0:T(8,128)S(1)}) custom-call(f32[2,1,2,8,64,128]{5,4,3,2,1,0:T(8,128)S(1)} %copy-done, f32[8,64,128]{2,1,0:T(8,128)S(1)} %copy-done.1, s32[1,4]{1,0:T(1,128)} %source_cells.3, ...), custom_call_target="tpu_custom_call" | custom-call | bytes 3690000 | tf_op jit(solution)/shard_map/pallas_call | solution.py:69
  6.5 0.7 %copy-done.4 = f32[1,2,256]{2,1,0:T(2,128)S(1)} copy-done((f32[1,2,256]{2,1,0:T(2,128)S(1)}, f32[1,2,256]{2,1,0:T(2,128)}, u32[]{:S(2)}) %copy-start.4) | copy-done | bytes 2072
  7.1 1.8 %shard_map.113 = (f32[8,64,128]{2,1,0:T(8,128)S(1)}, f32[8,64,128]{2,1,0:T(8,128)S(1)}, f32[8,64,128]{2,1,0:T(8,128)S(1)}, f32[8,64,128]{2,1,0:T(8,128)S(1)}, f3...) custom-call(f32[2,1,2,8,64,128]{5,4,3,2,1,0:T(8,128)S(1)} %copy-done, ...), custom_call_target="tpu_custom_call" | custom-call | bytes 4797000 | tf_op jit(solution)/shard_map/pallas_call | solution.py:69
  8.9 2.6 %collective-permute-start.2 = (f32[24,128]{1,0:T(8,128)S(1)}, f32[24,128]{1,0:T(8,128)S(1)}, u32[]{:S(2)}, u32[]{:S(2)}) collective-permute-start(f32[24,128]{1,0:T(8,128)S(1)} %get-tuple-element.54), channel_id=1, source_target_pairs={{4,8},{12,16},{20,24},{28,0},{8,4},{16,12},{24,20},{0,28},{5,9},{1... | collective-permute-start | bytes 36872 | tf_op jit(solution)/shard_map/ppermute | solution.py:550
  11.5 2.2 %collective-permute-start.5 = (f32[256,128]{1,0:T(8,128)S(1)}, f32[256,128]{1,0:T(8,128)S(1)}, u32[]{:S(2)}, u32[]{:S(2)}) collective-permute-start(f32[256,128]{1,0:T(8,128)S(1)} %get-tuple-element.62), channel_id=1, source_target_pairs={{0,1},{1,0},{2,3},{3,2},{4,5},{5,4},{6,7},{7,6},{8,9},{9,8},{10,11... | collective-permute-start | bytes 393224 | tf_op jit(solution)/shard_map/ppermute | solution.py:537
  13.8 0.1 collective-permute-start.3
  13.8 0.7 %shard_map.115 = (f32[8,64,128]{2,1,0:T(8,128)S(1)}, f32[8,64,128]{2,1,0:T(8,128)S(1)}, f32[8,64,128]{2,1,0:T(8,128)S(1)}, f32[8,64,128]{2,1,0:T(8,128)S(1)}) custom-call(f32[2,1,2,8,64,128]{5,4,3,2,1,0:T(8,128)S(1)} %copy-done, f32[8,64,128]{2,1,0:T(8,128)S(1)} %copy-done.1, f32[8,64,128]{2,1,0:T(8,128)S(1)} %get-tuple-element.44.partial_u, ...), custom_call_target="tpu_custom_call" | custom-call | bytes 2952000 | tf_op jit(solution)/shard_map/pallas_call | solution.py:69
  14.6 2.8 %collective-permute-done.5.second_a = f32[256,128]{1,0:T(8,128)S(1)} collective-permute-done((f32[256,128]{1,0:T(8,128)S(1)}, f32[256,128]{1,0:T(8,128)S(1)}, u32[]{:S(2)}, u32[]{:S(2)}) %collective-permute-start.5) | collective-permute-done | bytes 131104 | tf_op jit(solution)/shard_map/ppermute | solution.py:537
  17.4 0.2 shard_map.117
  17.7 0.1 collective-permute-start.6
  17.7 1.8 %collective-permute-start.10 = (f32[280,128]{1,0:T(8,128)S(1)}, f32[280,128]{1,0:T(8,128)S(1)}, u32[]{:S(2)}, u32[]{:S(2)}) collective-permute-start(f32[280,128]{1,0:T(8,128)S(1)} %get-tuple-element.72), channel_id=1, source_target_pairs={{0,1},{1,0},{2,3},{3,2},{4,5},{5,4},{6,7},{7,6},{8,9},{9,8},{10,11... | collective-permute-start | bytes 430088 | tf_op jit(solution)/shard_map/ppermute | solution.py:548
  19.5 0.2 collective-permute-start.11
  19.7 1.9 %collective-permute-start.7 = (f32[96,128]{1,0:T(8,128)S(1)}, f32[96,128]{1,0:T(8,128)S(1)}, u32[]{:S(2)}, u32[]{:S(2)}) collective-permute-start(f32[96,128]{1,0:T(8,128)S(1)} %get-tuple-element.65), channel_id=1, source_target_pairs={{0,24},{4,28},{8,16},{12,20},{16,8},{20,12},{24,0},{28,4},{1,25},{... | collective-permute-start | bytes 147464 | tf_op jit(solution)/shard_map/ppermute | solution.py:594
  21.6 0.3 collective-permute-start.8
  21.8 1.4 %collective-permute-start.9 = (f32[96,128]{1,0:T(8,128)S(1)}, f32[96,128]{1,0:T(8,128)S(1)}, u32[]{:S(2)}, u32[]{:S(2)}) collective-permute-start(f32[96,128]{1,0:T(8,128)S(1)} %get-tuple-element.67), channel_id=1, source_target_pairs={{0,8},{4,12},{8,0},{12,4},{16,24},{20,28},{24,16},{28,20},{1,9},{5... | collective-permute-start | bytes 147464 | tf_op jit(solution)/shard_map/ppermute | solution.py:594
  23.3 0.7 %collective-permute-done.10.third_a = f32[280,128]{1,0:T(8,128)S(1)} collective-permute-done((f32[280,128]{1,0:T(8,128)S(1)}, f32[280,128]{1,0:T(8,128)S(1)}, u32[]{:S(2)}, u32[]{:S(2)}) %collective-permute-start.10) | collective-permute-done | bytes 143392 | tf_op jit(solution)/shard_map/ppermute | solution.py:548
  23.9 1.4 %shard_map.119 = f32[1,2,8,64,128]{4,3,2,1,0:T(8,128)} custom-call(f32[2,1,2,8,64,128]{5,4,3,2,1,0:T(8,128)S(1)} %copy-done, f32[8,64,128]{2,1,0:T(8,128)S(1)} %copy-done.1, f32[8,64,128]{2,1,0:T(8,128)S(1)} %get-tuple-element.69.u_out, f32[8,64,128]{2,1,0:T(8,128)S(1)} %get-tuple-element.70.q_next, f32[8,64,128]{2,1,0:T(8,128)S(1)} %get-tuple-element.71.push, ...), custom_call_target="tpu_custom_call" | custom-call | bytes 5166000 | tf_op jit(solution)/shard_map/pallas_call | solution.py:69
  25.4 0.4 %collective-permute-done.8.refs_1_ = f32[96,128]{1,0:T(8,128)S(1)} collective-permute-done((f32[96,128]{1,0:T(8,128)S(1)}, f32[96,128]{1,0:T(8,128)S(1)}, u32[]{:S(2)}, u32[]{:S(2)}) %collective-permute-start.8) | collective-permute-done | bytes 49184 | tf_op jit(solution)/shard_map/ppermute | solution.py:594
  25.8 0.1 collective-permute-done.9.refs_2_
  25.9 2.1 %collective-permute-start.12 = (f32[24,128]{1,0:T(8,128)S(1)}, f32[24,128]{1,0:T(8,128)S(1)}, u32[]{:S(2)}, u32[]{:S(2)}) collective-permute-start(f32[24,128]{1,0:T(8,128)S(1)} %get-tuple-element.80), channel_id=1, source_target_pairs={{0,1},{1,0},{2,3},{3,2},{4,5},{5,4},{6,7},{7,6},{8,9},{9,8},{10,11... | collective-permute-start | bytes 36872 | tf_op jit(solution)/shard_map/ppermute | solution.py:606
  28.0 1.7 %collective-permute-done.12.got_a = f32[24,128]{1,0:T(8,128)S(1)} collective-permute-done((f32[24,128]{1,0:T(8,128)S(1)}, f32[24,128]{1,0:T(8,128)S(1)}, u32[]{:S(2)}, u32[]{:S(2)}) %collective-permute-start.12) | collective-permute-done | bytes 12320 | tf_op jit(solution)/shard_map/ppermute | solution.py:606
  29.7 0.8 %shard_map.122 = (f32[8,8,128]{2,1,0:T(8,128)}, f32[8,8,128]{2,1,0:T(8,128)}) custom-call(f32[96,128]{1,0:T(8,128)S(1)} %get-tuple-element.79.total, f32[24,128]{1,0:T(8,128)S(1)} %collective-permute-done.12.got_a, f32[24,128]{1,0:T(8,128)S(1)} %collective-permute-done.13.got_b, f32[3,8,8,128]{3,2,1,0:T(8,128)S(1)} %copy-done.2, ...), custom_call_target="tpu_custom_call" | custom-call | bytes 2583000 | tf_op jit(solution)/shard_map/pallas_call | solution.py:69
  (27 shorter events, 0.2 us)
Async XLA Ops:
  0.6 4.4 %copy-start.1 = (f32[8,64,128]{2,1,0:T(8,128)S(1)}, f32[8,64,128]{2,1,0:T(8,128)}, u32[]{:S(2)}) copy-start(f32[8,64,128]{2,1,0:T(8,128)} %velocity.13) | copy-start | bytes 786436
  0.6 4.4 %copy-start = (f32[2,1,2,8,64,128]{5,4,3,2,1,0:T(8,128)S(1)}, f32[2,1,2,8,64,128]{5,4,3,2,1,0:T(8,128)}, u32[]{:S(2)}) copy-start(f32[2,1,2,8,64,128]{5,4,3,2,1,0:T(8,128)} %state.9) | copy-start | bytes 3145732
  2.0 11.8 %collective-permute-start = (f32[10,64,128]{2,1,0:T(8,128)S(1)}, f32[10,64,128]{2,1,0:T(8,128)S(1)}, u32[]{:S(2)}, u32[]{:S(2)}) collective-permute-start(f32[10,64,128]{2,1,0:T(8,128)S(1)} %get-tuple-element.52), channel_id=1, source_target_pairs={{0,1},{1,0},{2,3},{3,2},{4,5},{5,4},{6,7},{7,6},{8,9},{9,8},{10,11... | collective-permute-start | bytes 983048 | tf_op jit(solution)/shard_map/ppermute | solution.py:515
  5.1 8.7 %collective-permute-start.1 = (f32[10,64,128]{2,1,0:T(8,128)S(1)}, f32[10,64,128]{2,1,0:T(8,128)S(1)}, u32[]{:S(2)}, u32[]{:S(2)}) collective-permute-start(f32[10,64,128]{2,1,0:T(8,128)S(1)} %get-tuple-element.53), channel_id=1, source_target_pairs={{0,4},{1,2},{2,1},{3,7},{4,0},{5,6},{6,5},{7,3},{8,12},{9,10},{10,... | collective-permute-start | bytes 983048 | tf_op jit(solution)/shard_map/ppermute | solution.py:514
  5.1 1.4 %copy-start.2 = (f32[3,8,8,128]{3,2,1,0:T(8,128)S(1)}, f32[3,8,8,128]{3,2,1,0:T(8,128)}, u32[]{:S(2)}) copy-start(f32[3,8,8,128]{3,2,1,0:T(8,128)} %kappa.7) | copy-start | bytes 294916
  6.4 0.7 %copy-start.4 = (f32[1,2,256]{2,1,0:T(2,128)S(1)}, f32[1,2,256]{2,1,0:T(2,128)}, u32[]{:S(2)}) copy-start(f32[1,2,256]{2,1,0:T(2,128)} %residuals.1) | copy-start | bytes 6148
  6.5 0.7 %copy-start.5 = (s32[1,256]{1,0:T(1,128)S(1)}, s32[1,256]{1,0:T(1,128)}, u32[]{:S(2)}) copy-start(s32[1,256]{1,0:T(1,128)} %cells) | copy-start | bytes 3076
  8.9 4.8 %collective-permute-start.2 = (f32[24,128]{1,0:T(8,128)S(1)}, f32[24,128]{1,0:T(8,128)S(1)}, u32[]{:S(2)}, u32[]{:S(2)}) collective-permute-start(f32[24,128]{1,0:T(8,128)S(1)} %get-tuple-element.54), channel_id=1, source_target_pairs={{4,8},{12,16},{20,24},{28,0},{8,4},{16,12},{24,20},{0,28},{5,9},{1... | collective-permute-start | bytes 36872 | tf_op jit(solution)/shard_map/ppermute | solution.py:550
  11.5 3.1 %collective-permute-start.4 = (f32[256,128]{1,0:T(8,128)S(1)}, f32[256,128]{1,0:T(8,128)S(1)}, u32[]{:S(2)}, u32[]{:S(2)}) collective-permute-start(f32[256,128]{1,0:T(8,128)S(1)} %get-tuple-element.61), channel_id=1, source_target_pairs={{0,4},{1,2},{2,1},{3,7},{4,0},{5,6},{6,5},{7,3},{8,12},{9,10},{10,... | collective-permute-start | bytes 393224 | tf_op jit(solution)/shard_map/ppermute | solution.py:536
  11.5 5.9 %collective-permute-start.5 = (f32[256,128]{1,0:T(8,128)S(1)}, f32[256,128]{1,0:T(8,128)S(1)}, u32[]{:S(2)}, u32[]{:S(2)}) collective-permute-start(f32[256,128]{1,0:T(8,128)S(1)} %get-tuple-element.62), channel_id=1, source_target_pairs={{0,1},{1,0},{2,3},{3,2},{4,5},{5,4},{6,7},{7,6},{8,9},{9,8},{10,11... | collective-permute-start | bytes 393224 | tf_op jit(solution)/shard_map/ppermute | solution.py:537
  13.8 3.7 %collective-permute-start.3 = (f32[4,64,128]{2,1,0:T(8,128)S(1)}, f32[4,64,128]{2,1,0:T(8,128)S(1)}, u32[]{:S(2)}, u32[]{:S(2)}) collective-permute-start(f32[4,64,128]{2,1,0:T(8,128)S(1)} %shard_map.116.share_own), channel_id=1, source_target_pairs={{0,4},{4,0},{8,12},{12,8},{16,20},{20,16},{24,28},{28,24},{1,5},{5... | collective-permute-start | bytes 393224 | tf_op jit(solution)/shard_map/ppermute | solution.py:553
  17.7 2.0 %collective-permute-start.6 = (f32[408,128]{1,0:T(8,128)S(1)}, f32[408,128]{1,0:T(8,128)S(1)}, u32[]{:S(2)}, u32[]{:S(2)}) collective-permute-start(f32[408,128]{1,0:T(8,128)S(1)} %get-tuple-element.64), channel_id=1, source_target_pairs={{0,4},{4,0},{8,12},{12,8},{16,20},{20,16},{24,28},{28,24},{1,5},{5... | collective-permute-start | bytes 626696 | tf_op jit(solution)/shard_map/ppermute | solution.py:575
  17.7 6.2 %collective-permute-start.10 = (f32[280,128]{1,0:T(8,128)S(1)}, f32[280,128]{1,0:T(8,128)S(1)}, u32[]{:S(2)}, u32[]{:S(2)}) collective-permute-start(f32[280,128]{1,0:T(8,128)S(1)} %get-tuple-element.72), channel_id=1, source_target_pairs={{0,1},{1,0},{2,3},{3,2},{4,5},{5,4},{6,7},{7,6},{8,9},{9,8},{10,11... | collective-permute-start | bytes 430088 | tf_op jit(solution)/shard_map/ppermute | solution.py:548
  19.5 4.4 %collective-permute-start.11 = (f32[280,128]{1,0:T(8,128)S(1)}, f32[280,128]{1,0:T(8,128)S(1)}, u32[]{:S(2)}, u32[]{:S(2)}) collective-permute-start(f32[280,128]{1,0:T(8,128)S(1)} %get-tuple-element.73), channel_id=1, source_target_pairs={{0,4},{1,2},{2,1},{3,7},{4,0},{5,6},{6,5},{7,3},{8,12},{9,10},{10,... | collective-permute-start | bytes 430088 | tf_op jit(solution)/shard_map/ppermute | solution.py:547
  19.7 5.7 %collective-permute-start.7 = (f32[96,128]{1,0:T(8,128)S(1)}, f32[96,128]{1,0:T(8,128)S(1)}, u32[]{:S(2)}, u32[]{:S(2)}) collective-permute-start(f32[96,128]{1,0:T(8,128)S(1)} %get-tuple-element.65), channel_id=1, source_target_pairs={{0,24},{4,28},{8,16},{12,20},{16,8},{20,12},{24,0},{28,4},{1,25},{... | collective-permute-start | bytes 147464 | tf_op jit(solution)/shard_map/ppermute | solution.py:594
  21.6 4.2 %collective-permute-start.8 = (f32[96,128]{1,0:T(8,128)S(1)}, f32[96,128]{1,0:T(8,128)S(1)}, u32[]{:S(2)}, u32[]{:S(2)}) collective-permute-start(f32[96,128]{1,0:T(8,128)S(1)} %get-tuple-element.66), channel_id=1, source_target_pairs={{0,16},{4,20},{8,24},{12,28},{16,0},{20,4},{24,8},{28,12},{1,17},{... | collective-permute-start | bytes 147464 | tf_op jit(solution)/shard_map/ppermute | solution.py:594
  21.8 4.1 %collective-permute-start.9 = (f32[96,128]{1,0:T(8,128)S(1)}, f32[96,128]{1,0:T(8,128)S(1)}, u32[]{:S(2)}, u32[]{:S(2)}) collective-permute-start(f32[96,128]{1,0:T(8,128)S(1)} %get-tuple-element.67), channel_id=1, source_target_pairs={{0,8},{4,12},{8,0},{12,4},{16,24},{20,28},{24,16},{28,20},{1,9},{5... | collective-permute-start | bytes 147464 | tf_op jit(solution)/shard_map/ppermute | solution.py:594
  25.9 3.8 %collective-permute-start.12 = (f32[24,128]{1,0:T(8,128)S(1)}, f32[24,128]{1,0:T(8,128)S(1)}, u32[]{:S(2)}, u32[]{:S(2)}) collective-permute-start(f32[24,128]{1,0:T(8,128)S(1)} %get-tuple-element.80), channel_id=1, source_target_pairs={{0,1},{1,0},{2,3},{3,2},{4,5},{5,4},{6,7},{7,6},{8,9},{9,8},{10,11... | collective-permute-start | bytes 36872 | tf_op jit(solution)/shard_map/ppermute | solution.py:606
  28.0 1.7 %copy-start.3 = (f32[8,8,128]{2,1,0:T(8,128)S(1)}, f32[8,8,128]{2,1,0:T(8,128)}, u32[]{:S(2)}) copy-start(f32[8,8,128]{2,1,0:T(8,128)} %momentum.1) | copy-start | bytes 98308
  28.0 1.7 %collective-permute-start.13 = (f32[24,128]{1,0:T(8,128)S(1)}, f32[24,128]{1,0:T(8,128)S(1)}, u32[]{:S(2)}, u32[]{:S(2)}) collective-permute-start(f32[24,128]{1,0:T(8,128)S(1)} %get-tuple-element.81), channel_id=1, source_target_pairs={{0,4},{1,2},{2,1},{3,7},{4,0},{5,6},{6,5},{7,3},{8,12},{9,10},{10,... | collective-permute-start | bytes 36872 | tf_op jit(solution)/shard_map/ppermute | solution.py:605

commit v8 on v7

--- a/solution.py
+++ b/solution.py
@@ -549,8 +549,6 @@
 
     far = lax.ppermute(far, "shot", odd_pairs(shots))
     first_a, first_b, far = lax.optimization_barrier((first_a, first_b, far))
-    (share_own,) = call(share_body, [edge], (first_a, first_b), ["vmem"] * 2, ["vmem"])
-    share_got = lax.ppermute(share_own, "shot", even_pairs(shots))
     u_part, q_next, image_own, gain = call(
         near_body,
         [shape(*cube)] * 4,
@@ -561,6 +559,9 @@
         us=0.8,
     )
 
+    gain, first_a, first_b = lax.optimization_barrier((gain, first_a, first_b))
+    (share_own,) = call(share_body, [edge], (first_a, first_b), ["vmem"] * 2, ["vmem"])
+    share_got = lax.ppermute(share_own, "shot", even_pairs(shots))
     part = shape(chips, depth * wide, size_y)
     side = 3 * depth
     u_out, keep, send = call(

time: 30.8 us -> 30.9 us (level)
  no operation moved by 1% of the time
where the time goes in v8:
time: 30.9 us; the launch traced here: 30.7 us
  starting transfers between devices  15.8 us (51%)
  Pallas kernels  7.74 us (25%)
  waiting for transfers between devices  5.69 us (18%)
  between operations  0.79 us (3%)
  local copies, waits for them, and re-layouts  0.69 us (2%)
    pallas_call x11, Pallas kernels, call(): pl.pallas_call(body, out_shape=list(out_shapes), in_specs=[SPECS[s] for s...  7.74 us
    ppermute x3, starting transfers between devices, on_device(): lax.ppermute(parts[k], 'shot', [(i, i ^ 2 * k) for i in range(shots)])  3.55 us
    ppermute x1, starting transfers between devices, on_device(): first_a = lax.ppermute(out_a, 'slab', z_even)  3.09 us
    ppermute x1, waiting for transfers between devices, on_device(): second_a = lax.ppermute(out_a, 'slab', z_even)  2.83 us
    ppermute x1, starting transfers between devices, on_device(): far = lax.ppermute(far, 'shot', odd_pairs(shots))  2.6 us
    ppermute x1, starting transfers between devices, on_device(): grad_a = lax.ppermute(out_a, 'slab', z_even)  2.22 us
    ppermute x1, starting transfers between devices, on_device(): second_a = lax.ppermute(out_a, 'slab', z_even)  2.21 us
    ppermute x1, starting transfers between devices, on_device(): third_a = lax.ppermute(third_a, 'slab', z_even)  1.76 us
  transfers between devices with their start and end apart: 14, of which 5 were waited for; matrix products, arithmetic and copies ran while one was open for 0% of the time, Pallas kernels for 17%

profile of v8, /device:TPU:0, one launch (start us, length us, event | category | flops | bytes accessed | tf_op | source)
XLA Modules:
  0.0 30.7 jit_solution(299011789970168768)
XLA Ops:
  0.6 1.3 %shard_map.114 = (f32[10,64,128]{2,1,0:T(8,128)S(1)}, f32[10,64,128]{2,1,0:T(8,128)S(1)}) custom-call(f32[2,1,2,8,64,128]{5,4,3,2,1,0:T(8,128)} %state.9, f32[8,64,128]{2,1,0:T(8,128)} %velocity.13), custom_call_target="tpu_custom_call" | custom-call | bytes 4797000 | tf_op jit(solution)/shard_map/pallas_call | solution.py:69
  2.0 3.1 %collective-permute-start = (f32[10,64,128]{2,1,0:T(8,128)S(1)}, f32[10,64,128]{2,1,0:T(8,128)S(1)}, u32[]{:S(2)}, u32[]{:S(2)}) collective-permute-start(f32[10,64,128]{2,1,0:T(8,128)S(1)} %get-tuple-element.55), channel_id=1, source_target_pairs={{0,1},{1,0},{2,3},{3,2},{4,5},{5,4},{6,7},{7,6},{8,9},{9,8},{10,11... | collective-permute-start | bytes 983048 | tf_op jit(solution)/shard_map/ppermute | solution.py:515
  5.1 1.3 %shard_map.112 = (f32[8,64,128]{2,1,0:T(8,128)S(1)}, f32[8,64,128]{2,1,0:T(8,128)S(1)}, f32[8,64,128]{2,1,0:T(8,128)S(1)}, f32[256,128]{1,0:T(8,128)S(1)}, f32[256,128]{1,0:T(8,128)S(1)}) custom-call(f32[2,1,2,8,64,128]{5,4,3,2,1,0:T(8,128)S(1)} %copy-done, f32[8,64,128]{2,1,0:T(8,128)S(1)} %copy-done.1, s32[1,4]{1,0:T(1,128)} %source_cells.3, ...), custom_call_target="tpu_custom_call" | custom-call | bytes 3690000 | tf_op jit(solution)/shard_map/pallas_call | solution.py:69
  6.5 0.7 %copy-done.4 = f32[1,2,256]{2,1,0:T(2,128)S(1)} copy-done((f32[1,2,256]{2,1,0:T(2,128)S(1)}, f32[1,2,256]{2,1,0:T(2,128)}, u32[]{:S(2)}) %copy-start.4) | copy-done | bytes 2072
  7.1 1.8 %shard_map.113 = (f32[8,64,128]{2,1,0:T(8,128)S(1)}, f32[8,64,128]{2,1,0:T(8,128)S(1)}, f32[8,64,128]{2,1,0:T(8,128)S(1)}, f32[8,64,128]{2,1,0:T(8,128)S(1)}, f3...) custom-call(f32[2,1,2,8,64,128]{5,4,3,2,1,0:T(8,128)S(1)} %copy-done, ...), custom_call_target="tpu_custom_call" | custom-call | bytes 4797000 | tf_op jit(solution)/shard_map/pallas_call | solution.py:69
  8.9 2.6 %collective-permute-start.2 = (f32[24,128]{1,0:T(8,128)S(1)}, f32[24,128]{1,0:T(8,128)S(1)}, u32[]{:S(2)}, u32[]{:S(2)}) collective-permute-start(f32[24,128]{1,0:T(8,128)S(1)} %get-tuple-element.57), channel_id=1, source_target_pairs={{4,8},{12,16},{20,24},{28,0},{8,4},{16,12},{24,20},{0,28},{5,9},{1... | collective-permute-start | bytes 36872 | tf_op jit(solution)/shard_map/ppermute | solution.py:550
  11.5 2.2 %collective-permute-start.5 = (f32[256,128]{1,0:T(8,128)S(1)}, f32[256,128]{1,0:T(8,128)S(1)}, u32[]{:S(2)}, u32[]{:S(2)}) collective-permute-start(f32[256,128]{1,0:T(8,128)S(1)} %get-tuple-element.68), channel_id=1, source_target_pairs={{0,1},{1,0},{2,3},{3,2},{4,5},{5,4},{6,7},{7,6},{8,9},{9,8},{10,11... | collective-permute-start | bytes 393224 | tf_op jit(solution)/shard_map/ppermute | solution.py:537
  13.7 0.7 %shard_map.115 = (f32[8,64,128]{2,1,0:T(8,128)S(1)}, f32[8,64,128]{2,1,0:T(8,128)S(1)}, f32[8,64,128]{2,1,0:T(8,128)S(1)}, f32[8,64,128]{2,1,0:T(8,128)S(1)}) custom-call(f32[2,1,2,8,64,128]{5,4,3,2,1,0:T(8,128)S(1)} %copy-done, f32[8,64,128]{2,1,0:T(8,128)S(1)} %copy-done.1, f32[8,64,128]{2,1,0:T(8,128)S(1)} %get-tuple-element.47.partial_u, ...), custom_call_target="tpu_custom_call" | custom-call | bytes 2952000 | tf_op jit(solution)/shard_map/pallas_call | solution.py:69
  14.5 0.1 collective-permute-start.3
  14.6 2.8 %collective-permute-done.5.second_a = f32[256,128]{1,0:T(8,128)S(1)} collective-permute-done((f32[256,128]{1,0:T(8,128)S(1)}, f32[256,128]{1,0:T(8,128)S(1)}, u32[]{:S(2)}, u32[]{:S(2)}) %collective-permute-start.5) | collective-permute-done | bytes 131104 | tf_op jit(solution)/shard_map/ppermute | solution.py:537
  17.4 0.2 shard_map.117
  17.7 0.1 collective-permute-start.6
  17.7 1.8 %collective-permute-start.10 = (f32[280,128]{1,0:T(8,128)S(1)}, f32[280,128]{1,0:T(8,128)S(1)}, u32[]{:S(2)}, u32[]{:S(2)}) collective-permute-start(f32[280,128]{1,0:T(8,128)S(1)} %get-tuple-element.78), channel_id=1, source_target_pairs={{0,1},{1,0},{2,3},{3,2},{4,5},{5,4},{6,7},{7,6},{8,9},{9,8},{10,11... | collective-permute-start | bytes 430088 | tf_op jit(solution)/shard_map/ppermute | solution.py:548
  19.5 0.2 collective-permute-start.11
  19.7 1.9 %collective-permute-start.7 = (f32[96,128]{1,0:T(8,128)S(1)}, f32[96,128]{1,0:T(8,128)S(1)}, u32[]{:S(2)}, u32[]{:S(2)}) collective-permute-start(f32[96,128]{1,0:T(8,128)S(1)} %get-tuple-element.71), channel_id=1, source_target_pairs={{0,24},{4,28},{8,16},{12,20},{16,8},{20,12},{24,0},{28,4},{1,25},{... | collective-permute-start | bytes 147464 | tf_op jit(solution)/shard_map/ppermute | solution.py:595
  21.6 0.2 collective-permute-start.8
  21.8 1.4 %collective-permute-start.9 = (f32[96,128]{1,0:T(8,128)S(1)}, f32[96,128]{1,0:T(8,128)S(1)}, u32[]{:S(2)}, u32[]{:S(2)}) collective-permute-start(f32[96,128]{1,0:T(8,128)S(1)} %get-tuple-element.73), channel_id=1, source_target_pairs={{0,8},{4,12},{8,0},{12,4},{16,24},{20,28},{24,16},{28,20},{1,9},{5... | collective-permute-start | bytes 147464 | tf_op jit(solution)/shard_map/ppermute | solution.py:595
  23.3 0.7 %collective-permute-done.10.third_a = f32[280,128]{1,0:T(8,128)S(1)} collective-permute-done((f32[280,128]{1,0:T(8,128)S(1)}, f32[280,128]{1,0:T(8,128)S(1)}, u32[]{:S(2)}, u32[]{:S(2)}) %collective-permute-start.10) | collective-permute-done | bytes 143392 | tf_op jit(solution)/shard_map/ppermute | solution.py:548
  23.9 1.4 %shard_map.119 = f32[1,2,8,64,128]{4,3,2,1,0:T(8,128)} custom-call(f32[2,1,2,8,64,128]{5,4,3,2,1,0:T(8,128)S(1)} %copy-done, f32[8,64,128]{2,1,0:T(8,128)S(1)} %copy-done.1, f32[8,64,128]{2,1,0:T(8,128)S(1)} %get-tuple-element.75.u_out, f32[8,64,128]{2,1,0:T(8,128)S(1)} %get-tuple-element.76.q_next, f32[8,64,128]{2,1,0:T(8,128)S(1)} %get-tuple-element.77.push, ...), custom_call_target="tpu_custom_call" | custom-call | bytes 5166000 | tf_op jit(solution)/shard_map/pallas_call | solution.py:69
  25.4 0.4 %collective-permute-done.8.refs_1_ = f32[96,128]{1,0:T(8,128)S(1)} collective-permute-done((f32[96,128]{1,0:T(8,128)S(1)}, f32[96,128]{1,0:T(8,128)S(1)}, u32[]{:S(2)}, u32[]{:S(2)}) %collective-permute-start.8) | collective-permute-done | bytes 49184 | tf_op jit(solution)/shard_map/ppermute | solution.py:595
  25.8 0.1 collective-permute-done.9.refs_2_
  25.9 2.2 %collective-permute-start.12 = (f32[24,128]{1,0:T(8,128)S(1)}, f32[24,128]{1,0:T(8,128)S(1)}, u32[]{:S(2)}, u32[]{:S(2)}) collective-permute-start(f32[24,128]{1,0:T(8,128)S(1)} %get-tuple-element.86), channel_id=1, source_target_pairs={{0,1},{1,0},{2,3},{3,2},{4,5},{5,4},{6,7},{7,6},{8,9},{9,8},{10,11... | collective-permute-start | bytes 36872 | tf_op jit(solution)/shard_map/ppermute | solution.py:607
  28.2 1.6 %collective-permute-done.12.got_a = f32[24,128]{1,0:T(8,128)S(1)} collective-permute-done((f32[24,128]{1,0:T(8,128)S(1)}, f32[24,128]{1,0:T(8,128)S(1)}, u32[]{:S(2)}, u32[]{:S(2)}) %collective-permute-start.12) | collective-permute-done | bytes 12320 | tf_op jit(solution)/shard_map/ppermute | solution.py:607
  29.8 0.8 %shard_map.122 = (f32[8,8,128]{2,1,0:T(8,128)}, f32[8,8,128]{2,1,0:T(8,128)}) custom-call(f32[96,128]{1,0:T(8,128)S(1)} %get-tuple-element.85.total, f32[24,128]{1,0:T(8,128)S(1)} %collective-permute-done.12.got_a, f32[24,128]{1,0:T(8,128)S(1)} %collective-permute-done.13.got_b, f32[3,8,8,128]{3,2,1,0:T(8,128)S(1)} %copy-done.2, ...), custom_call_target="tpu_custom_call" | custom-call | bytes 2583000 | tf_op jit(solution)/shard_map/pallas_call | solution.py:69
  (27 shorter events, 0.2 us)
Async XLA Ops:
  0.6 4.4 %copy-start.1 = (f32[8,64,128]{2,1,0:T(8,128)S(1)}, f32[8,64,128]{2,1,0:T(8,128)}, u32[]{:S(2)}) copy-start(f32[8,64,128]{2,1,0:T(8,128)} %velocity.13) | copy-start | bytes 786436
  0.6 4.4 %copy-start = (f32[2,1,2,8,64,128]{5,4,3,2,1,0:T(8,128)S(1)}, f32[2,1,2,8,64,128]{5,4,3,2,1,0:T(8,128)}, u32[]{:S(2)}) copy-start(f32[2,1,2,8,64,128]{5,4,3,2,1,0:T(8,128)} %state.9) | copy-start | bytes 3145732
  2.0 11.8 %collective-permute-start = (f32[10,64,128]{2,1,0:T(8,128)S(1)}, f32[10,64,128]{2,1,0:T(8,128)S(1)}, u32[]{:S(2)}, u32[]{:S(2)}) collective-permute-start(f32[10,64,128]{2,1,0:T(8,128)S(1)} %get-tuple-element.55), channel_id=1, source_target_pairs={{0,1},{1,0},{2,3},{3,2},{4,5},{5,4},{6,7},{7,6},{8,9},{9,8},{10,11... | collective-permute-start | bytes 983048 | tf_op jit(solution)/shard_map/ppermute | solution.py:515
  5.1 8.7 %collective-permute-start.1 = (f32[10,64,128]{2,1,0:T(8,128)S(1)}, f32[10,64,128]{2,1,0:T(8,128)S(1)}, u32[]{:S(2)}, u32[]{:S(2)}) collective-permute-start(f32[10,64,128]{2,1,0:T(8,128)S(1)} %get-tuple-element.56), channel_id=1, source_target_pairs={{0,4},{1,2},{2,1},{3,7},{4,0},{5,6},{6,5},{7,3},{8,12},{9,10},{10,... | collective-permute-start | bytes 983048 | tf_op jit(solution)/shard_map/ppermute | solution.py:514
  5.1 1.4 %copy-start.2 = (f32[3,8,8,128]{3,2,1,0:T(8,128)S(1)}, f32[3,8,8,128]{3,2,1,0:T(8,128)}, u32[]{:S(2)}) copy-start(f32[3,8,8,128]{3,2,1,0:T(8,128)} %kappa.7) | copy-start | bytes 294916
  6.4 0.7 %copy-start.4 = (f32[1,2,256]{2,1,0:T(2,128)S(1)}, f32[1,2,256]{2,1,0:T(2,128)}, u32[]{:S(2)}) copy-start(f32[1,2,256]{2,1,0:T(2,128)} %residuals.1) | copy-start | bytes 6148
  6.5 0.7 %copy-start.5 = (s32[1,256]{1,0:T(1,128)S(1)}, s32[1,256]{1,0:T(1,128)}, u32[]{:S(2)}) copy-start(s32[1,256]{1,0:T(1,128)} %cells) | copy-start | bytes 3076
  8.9 4.8 %collective-permute-start.2 = (f32[24,128]{1,0:T(8,128)S(1)}, f32[24,128]{1,0:T(8,128)S(1)}, u32[]{:S(2)}, u32[]{:S(2)}) collective-permute-start(f32[24,128]{1,0:T(8,128)S(1)} %get-tuple-element.57), channel_id=1, source_target_pairs={{4,8},{12,16},{20,24},{28,0},{8,4},{16,12},{24,20},{0,28},{5,9},{1... | collective-permute-start | bytes 36872 | tf_op jit(solution)/shard_map/ppermute | solution.py:550
  11.5 3.1 %collective-permute-start.4 = (f32[256,128]{1,0:T(8,128)S(1)}, f32[256,128]{1,0:T(8,128)S(1)}, u32[]{:S(2)}, u32[]{:S(2)}) collective-permute-start(f32[256,128]{1,0:T(8,128)S(1)} %get-tuple-element.67), channel_id=1, source_target_pairs={{0,4},{1,2},{2,1},{3,7},{4,0},{5,6},{6,5},{7,3},{8,12},{9,10},{10,... | collective-permute-start | bytes 393224 | tf_op jit(solution)/shard_map/ppermute | solution.py:536
  11.5 5.9 %collective-permute-start.5 = (f32[256,128]{1,0:T(8,128)S(1)}, f32[256,128]{1,0:T(8,128)S(1)}, u32[]{:S(2)}, u32[]{:S(2)}) collective-permute-start(f32[256,128]{1,0:T(8,128)S(1)} %get-tuple-element.68), channel_id=1, source_target_pairs={{0,1},{1,0},{2,3},{3,2},{4,5},{5,4},{6,7},{7,6},{8,9},{9,8},{10,11... | collective-permute-start | bytes 393224 | tf_op jit(solution)/shard_map/ppermute | solution.py:537
  14.5 2.9 %collective-permute-start.3 = (f32[4,64,128]{2,1,0:T(8,128)S(1)}, f32[4,64,128]{2,1,0:T(8,128)S(1)}, u32[]{:S(2)}, u32[]{:S(2)}) collective-permute-start(f32[4,64,128]{2,1,0:T(8,128)S(1)} %shard_map.116.share_own), channel_id=1, source_target_pairs={{0,4},{4,0},{8,12},{12,8},{16,20},{20,16},{24,28},{28,24},{1,5},{5... | collective-permute-start | bytes 393224 | tf_op jit(solution)/shard_map/ppermute | solution.py:564
  17.7 2.0 %collective-permute-start.6 = (f32[408,128]{1,0:T(8,128)S(1)}, f32[408,128]{1,0:T(8,128)S(1)}, u32[]{:S(2)}, u32[]{:S(2)}) collective-permute-start(f32[408,128]{1,0:T(8,128)S(1)} %get-tuple-element.70), channel_id=1, source_target_pairs={{0,4},{4,0},{8,12},{12,8},{16,20},{20,16},{24,28},{28,24},{1,5},{5... | collective-permute-start | bytes 626696 | tf_op jit(solution)/shard_map/ppermute | solution.py:576
  17.7 6.2 %collective-permute-start.10 = (f32[280,128]{1,0:T(8,128)S(1)}, f32[280,128]{1,0:T(8,128)S(1)}, u32[]{:S(2)}, u32[]{:S(2)}) collective-permute-start(f32[280,128]{1,0:T(8,128)S(1)} %get-tuple-element.78), channel_id=1, source_target_pairs={{0,1},{1,0},{2,3},{3,2},{4,5},{5,4},{6,7},{7,6},{8,9},{9,8},{10,11... | collective-permute-start | bytes 430088 | tf_op jit(solution)/shard_map/ppermute | solution.py:548
  19.5 4.4 %collective-permute-start.11 = (f32[280,128]{1,0:T(8,128)S(1)}, f32[280,128]{1,0:T(8,128)S(1)}, u32[]{:S(2)}, u32[]{:S(2)}) collective-permute-start(f32[280,128]{1,0:T(8,128)S(1)} %get-tuple-element.79), channel_id=1, source_target_pairs={{0,4},{1,2},{2,1},{3,7},{4,0},{5,6},{6,5},{7,3},{8,12},{9,10},{10,... | collective-permute-start | bytes 430088 | tf_op jit(solution)/shard_map/ppermute | solution.py:547
  19.7 5.7 %collective-permute-start.7 = (f32[96,128]{1,0:T(8,128)S(1)}, f32[96,128]{1,0:T(8,128)S(1)}, u32[]{:S(2)}, u32[]{:S(2)}) collective-permute-start(f32[96,128]{1,0:T(8,128)S(1)} %get-tuple-element.71), channel_id=1, source_target_pairs={{0,24},{4,28},{8,16},{12,20},{16,8},{20,12},{24,0},{28,4},{1,25},{... | collective-permute-start | bytes 147464 | tf_op jit(solution)/shard_map/ppermute | solution.py:595
  21.6 4.2 %collective-permute-start.8 = (f32[96,128]{1,0:T(8,128)S(1)}, f32[96,128]{1,0:T(8,128)S(1)}, u32[]{:S(2)}, u32[]{:S(2)}) collective-permute-start(f32[96,128]{1,0:T(8,128)S(1)} %get-tuple-element.72), channel_id=1, source_target_pairs={{0,16},{4,20},{8,24},{12,28},{16,0},{20,4},{24,8},{28,12},{1,17},{... | collective-permute-start | bytes 147464 | tf_op jit(solution)/shard_map/ppermute | solution.py:595
  21.8 4.1 %collective-permute-start.9 = (f32[96,128]{1,0:T(8,128)S(1)}, f32[96,128]{1,0:T(8,128)S(1)}, u32[]{:S(2)}, u32[]{:S(2)}) collective-permute-start(f32[96,128]{1,0:T(8,128)S(1)} %get-tuple-element.73), channel_id=1, source_target_pairs={{0,8},{4,12},{8,0},{12,4},{16,24},{20,28},{24,16},{28,20},{1,9},{5... | collective-permute-start | bytes 147464 | tf_op jit(solution)/shard_map/ppermute | solution.py:595
  25.9 3.9 %collective-permute-start.12 = (f32[24,128]{1,0:T(8,128)S(1)}, f32[24,128]{1,0:T(8,128)S(1)}, u32[]{:S(2)}, u32[]{:S(2)}) collective-permute-start(f32[24,128]{1,0:T(8,128)S(1)} %get-tuple-element.86), channel_id=1, source_target_pairs={{0,1},{1,0},{2,3},{3,2},{4,5},{5,4},{6,7},{7,6},{8,9},{9,8},{10,11... | collective-permute-start | bytes 36872 | tf_op jit(solution)/shard_map/ppermute | solution.py:607
  28.1 1.7 %copy-start.3 = (f32[8,8,128]{2,1,0:T(8,128)S(1)}, f32[8,8,128]{2,1,0:T(8,128)}, u32[]{:S(2)}) copy-start(f32[8,8,128]{2,1,0:T(8,128)} %momentum.1) | copy-start | bytes 98308
  28.1 1.7 %collective-permute-start.13 = (f32[24,128]{1,0:T(8,128)S(1)}, f32[24,128]{1,0:T(8,128)S(1)}, u32[]{:S(2)}, u32[]{:S(2)}) collective-permute-start(f32[24,128]{1,0:T(8,128)S(1)} %get-tuple-element.87), channel_id=1, source_target_pairs={{0,4},{1,2},{2,1},{3,7},{4,0},{5,6},{6,5},{7,3},{8,12},{9,10},{10,... | collective-permute-start | bytes 36872 | tf_op jit(solution)/shard_map/ppermute | solution.py:606
